TPU v7x, 128 devices: a whole 4x4x4 slice. The times are simulated.
128 devices in a mesh: fsdp: 16 (over z_hi, y, core), tp: 8 (over x, z_lo).
Axes of the slice: x: 4, y: 4, z: 4 (z_hi: 2, z_lo: 2; z = z_hi * 2 + z_lo), core: 2. Of those that a mesh axis runs over, the one named last changes fastest.
Arguments:
- inputs: bfloat16 [3, 16, 576, 1024], P(None, 'fsdp', 'tp'), may hold values from -6 to 6
- cotangent: bfloat16 [3, 16, 576, 1024], P(None, 'fsdp', 'tp'), may hold values from -6 to 6
- valid_slots: int32 [3, 16], P(None, 'fsdp'), may hold values 0 or 1
- ln1_gain: bfloat16 [1024], P(('fsdp', 'tp')), may hold values from 0.5 to 1.5
- ln1_bias: bfloat16 [1024], P(('fsdp', 'tp')), may hold values from -1 to 1
- qkv_weight: bfloat16 [3, 1024, 1024], P(None, 'fsdp', 'tp'), may hold values from -0.1875 to 0.1875
- qv_bias: bfloat16 [2, 16, 64], P(None, 'tp', 'fsdp'), may hold values from -0.59765625 to 0.59765625
- out_weight: bfloat16 [1024, 1024], P('tp', 'fsdp'), may hold values from -1 to 1
- out_bias: bfloat16 [1024], P(('fsdp', 'tp')), may hold values from -1 to 1
- ln2_gain: bfloat16 [1024], P(('fsdp', 'tp')), may hold values from 0.5 to 1.5
- ln2_bias: bfloat16 [1024], P(('fsdp', 'tp')), may hold values from -1 to 1
- fc1_weight: bfloat16 [1024, 4096], P('fsdp', 'tp'), may hold values from -0.1875 to 0.1875
- fc1_bias: bfloat16 [64, 64], P('tp', 'fsdp'), may hold values from -1 to 1
- fc2_weight: bfloat16 [4096, 1024], P('tp', 'fsdp'), may hold values from -0.09375 to 0.09375
- fc2_bias: bfloat16 [1024], P(('fsdp', 'tp')), may hold values from -1 to 1
Outputs:
- output_rows: bfloat16 [3, 16, 576, 1024], P(None, 'fsdp', 'tp')
- input_grad: bfloat16 [3, 16, 576, 1024], P(None, 'fsdp', 'tp')
- grad_ln1_gain: float32 [1024], P(('fsdp', 'tp'))
- grad_ln1_bias: float32 [1024], P(('fsdp', 'tp'))
- grad_qkv_weight: float32 [3, 1024, 1024], P(None, 'fsdp', 'tp')
- grad_qv_bias: float32 [2, 16, 64], P(None, 'tp', 'fsdp')
- grad_out_weight: float32 [1024, 1024], P('tp', 'fsdp')
- grad_out_bias: float32 [1024], P(('fsdp', 'tp'))
- grad_ln2_gain: float32 [1024], P(('fsdp', 'tp'))
- grad_ln2_bias: float32 [1024], P(('fsdp', 'tp'))
- grad_fc1_weight: float32 [1024, 4096], P('fsdp', 'tp')
- grad_fc1_bias: float32 [64, 64], P('tp', 'fsdp')
- grad_fc2_weight: float32 [4096, 1024], P('tp', 'fsdp')
- grad_fc2_bias: float32 [1024], P(('fsdp', 'tp'))
Inputs may be any that keep to these rules, and one draw needn't show every extreme that they name: `valid_slots`: 1 marks a slot that holds an image, 0 an empty slot.
All inputs are finite; a program needn't handle non-finite values. No bound on the sum of `valid_slots` on one device may be relied on, other than what follows from the above.
Results may differ from a plain program's by a relative error of at most 0.025.
Values may be sent and summed in bfloat16 or wider, within the bound.
A program may use at most 128 MiB of HBM per device.

v0:
```python
import math

import jax
import jax.numpy as jnp
from jax import lax
from jax.sharding import PartitionSpec as P

HD = 64


epsilon = 1e-05


def norm_stats(values):
    average = jnp.mean(values, -1, keepdims=True)
    centered = values - average
    inverse = lax.rsqrt(jnp.mean(centered * centered, -1, keepdims=True) + epsilon)
    return (centered * inverse, inverse)


def norm_back(upstream, normed, inverse, gain_vector):
    scaled = upstream * gain_vector
    return inverse * (
        scaled
        - jnp.mean(scaled, -1, keepdims=True)
        - normed * jnp.mean(scaled * normed, -1, keepdims=True)
    )


def head_scores(queries, key_rows, score_scale):
    return (
        jnp.einsum("bshd,bthd->bhst", queries, key_rows, preferred_element_type=jnp.float32)
        * score_scale
    )


def unpack_weights(gathered):
    qkv_full, pair_bias, out_full, fc1_full, hidden_bias, fc2_full = gathered
    return (
        qkv_full,
        pair_bias.reshape(2, -1).astype(jnp.float32),
        out_full,
        fc1_full,
        hidden_bias.reshape(-1).astype(jnp.float32),
        fc2_full,
    )


def per_device(
    inputs,
    cotangent,
    valid_slots,
    ln1_gain,
    ln1_bias,
    qkv_weight,
    qv_bias,
    out_weight,
    out_bias,
    ln2_gain,
    ln2_bias,
    fc1_weight,
    fc1_bias,
    fc2_weight,
    fc2_bias,
):
    micro_count, slot_count, local_seq, model_width = inputs.shape
    score_scale = 1.0 / math.sqrt(HD)
    vectors = (
        lax.all_gather(ln1_gain, ("fsdp", "tp"), axis=0, tiled=True),
        lax.all_gather(ln1_bias, ("fsdp", "tp"), axis=0, tiled=True),
        lax.all_gather(out_bias, ("fsdp", "tp"), axis=0, tiled=True),
        lax.all_gather(ln2_gain, ("fsdp", "tp"), axis=0, tiled=True),
        lax.all_gather(ln2_bias, ("fsdp", "tp"), axis=0, tiled=True),
        lax.all_gather(fc2_bias, ("fsdp", "tp"), axis=0, tiled=True),
    )
    gain_one, bias_one, bias_out, gain_two, bias_two, bias_last = [
        entry.astype(jnp.float32) for entry in vectors
    ]
    vector_sums = [jnp.zeros((model_width,), jnp.float32) for index_unused in range(6)]
    shard_sums = tuple(
        (
            jnp.zeros(shard.shape, jnp.float32)
            for shard in (qkv_weight, qv_bias, out_weight, fc1_weight, fc1_bias, fc2_weight)
        )
    )
    results = []
    input_grads = []
    for micro_step in range(micro_count):
        qkv_full, pair_bias, out_full, fc1_full, hidden_bias, fc2_full = unpack_weights(
            (
                lax.all_gather(qkv_weight, "fsdp", axis=1, tiled=True),
                lax.all_gather(qv_bias, "fsdp", axis=2, tiled=True),
                lax.all_gather(out_weight, "fsdp", axis=1, tiled=True),
                lax.all_gather(fc1_weight, "fsdp", axis=0, tiled=True),
                lax.all_gather(fc1_bias, "fsdp", axis=1, tiled=True),
                lax.all_gather(fc2_weight, "fsdp", axis=1, tiled=True),
            )
        )
        block_rows = inputs[micro_step].astype(jnp.float32)
        normed_one, inverse_one = norm_stats(block_rows)
        low_one = (normed_one * gain_one + bias_one).astype(jnp.bfloat16)
        flat_one = lax.all_gather(low_one, "tp", axis=1, tiled=True).reshape(-1, model_width)
        token_count = flat_one.shape[0]
        seq_len = token_count // slot_count
        projected = jnp.einsum(
            "nd,kdc->knc", flat_one, qkv_full, preferred_element_type=jnp.float32
        )
        local_width = projected.shape[2]
        local_heads = local_width // HD
        head_shape = (slot_count, seq_len, local_heads, HD)
        queries = (projected[0] + pair_bias[0]).astype(jnp.bfloat16).reshape(head_shape)
        key_rows = projected[1].astype(jnp.bfloat16).reshape(head_shape)
        value_rows = (projected[2] + pair_bias[1]).astype(jnp.bfloat16).reshape(head_shape)
        scores = head_scores(queries, key_rows, score_scale)
        largest = jnp.max(scores, -1, keepdims=True)
        log_total = largest + jnp.log(jnp.sum(jnp.exp(scores - largest), -1, keepdims=True))
        weights_low = jnp.exp(scores - log_total).astype(jnp.bfloat16)
        attended = jnp.einsum(
            "bhst,bthd->bshd", weights_low, value_rows, preferred_element_type=jnp.float32
        )
        attended = attended.astype(jnp.bfloat16).reshape(token_count, local_width)
        branch_part = jnp.dot(attended, out_full, preferred_element_type=jnp.float32)
        branch = lax.psum_scatter(
            branch_part.reshape(slot_count, seq_len, model_width),
            "tp",
            scatter_dimension=1,
            tiled=True,
        )
        middle = block_rows + branch + bias_out
        normed_two, inverse_two = norm_stats(middle)
        low_two = (normed_two * gain_two + bias_two).astype(jnp.bfloat16)
        flat_two = lax.all_gather(low_two, "tp", axis=1, tiled=True).reshape(-1, model_width)
        up_proj = jnp.dot(flat_two, fc1_full, preferred_element_type=jnp.float32) + hidden_bias
        sigmoid_up = jax.nn.sigmoid(1.702 * up_proj)
        activated = (up_proj * sigmoid_up).astype(jnp.bfloat16)
        mlp_part = jnp.dot(activated, fc2_full, preferred_element_type=jnp.float32)
        mlp_out = lax.psum_scatter(
            mlp_part.reshape(slot_count, seq_len, model_width).astype(jnp.bfloat16),
            "tp",
            scatter_dimension=1,
            tiled=True,
        ).astype(jnp.float32)
        results.append((middle + mlp_out + bias_last).astype(jnp.bfloat16))
        qkv_full, pair_bias, out_full, fc1_full, hidden_bias, fc2_full = unpack_weights(
            (
                lax.all_gather(qkv_weight, "fsdp", axis=1, tiled=True),
                lax.all_gather(qv_bias, "fsdp", axis=2, tiled=True),
                lax.all_gather(out_weight, "fsdp", axis=1, tiled=True),
                lax.all_gather(fc1_weight, "fsdp", axis=0, tiled=True),
                lax.all_gather(fc1_bias, "fsdp", axis=1, tiled=True),
                lax.all_gather(fc2_weight, "fsdp", axis=1, tiled=True),
            )
        )
        slot_weight = valid_slots[micro_step].astype(jnp.float32)[:, None, None]
        upstream = cotangent[micro_step].astype(jnp.float32) * slot_weight
        vector_sums[5] = vector_sums[5] + jnp.sum(upstream, (0, 1))
        upstream_low = upstream.astype(jnp.bfloat16)
        seq_upstream = lax.all_gather(upstream_low, "tp", axis=1, tiled=True).reshape(
            -1, model_width
        )
        grad_fc2 = jnp.einsum(
            "nf,nd->fd", activated, seq_upstream, preferred_element_type=jnp.float32
        )
        d_act = jnp.einsum("nd,fd->nf", seq_upstream, fc2_full, preferred_element_type=jnp.float32)
        d_up = (d_act * (sigmoid_up + 1.702 * up_proj * sigmoid_up * (1.0 - sigmoid_up))).astype(
            jnp.bfloat16
        )
        grad_fc1 = jnp.einsum("nd,nf->df", flat_two, d_up, preferred_element_type=jnp.float32)
        grad_hidden = jnp.sum(d_up.astype(jnp.float32), 0).reshape(-1, 64)
        part_two = jnp.einsum("nf,df->nd", d_up, fc1_full, preferred_element_type=jnp.float32)
        d_norm_two = lax.psum_scatter(
            part_two.reshape(slot_count, seq_len, model_width).astype(jnp.bfloat16),
            "tp",
            scatter_dimension=1,
            tiled=True,
        ).astype(jnp.float32)
        vector_sums[3] = vector_sums[3] + jnp.sum(d_norm_two * normed_two, (0, 1))
        vector_sums[4] = vector_sums[4] + jnp.sum(d_norm_two, (0, 1))
        d_middle = upstream + norm_back(d_norm_two, normed_two, inverse_two, gain_two)
        vector_sums[2] = vector_sums[2] + jnp.sum(d_middle, (0, 1))
        middle_low = d_middle.astype(jnp.bfloat16)
        seq_middle = lax.all_gather(middle_low, "tp", axis=1, tiled=True).reshape(-1, model_width)
        grad_outw = jnp.einsum(
            "nc,nd->cd", attended, seq_middle, preferred_element_type=jnp.float32
        )
        d_attended = jnp.einsum(
            "nd,cd->nc", seq_middle, out_full, preferred_element_type=jnp.float32
        )
        d_attended = d_attended.astype(jnp.bfloat16).reshape(head_shape)
        scores = head_scores(queries, key_rows, score_scale)
        probs_full = jnp.exp(scores - log_total)
        d_probs = jnp.einsum(
            "bshd,bthd->bhst", d_attended, value_rows, preferred_element_type=jnp.float32
        )
        d_scores = (
            probs_full * (d_probs - jnp.sum(probs_full * d_probs, -1, keepdims=True))
        ).astype(jnp.bfloat16)
        d_queries = (
            (
                jnp.einsum(
                    "bhst,bthd->bshd", d_scores, key_rows, preferred_element_type=jnp.float32
                )
                * score_scale
            )
            .astype(jnp.bfloat16)
            .reshape(token_count, local_width)
        )
        d_keys = (
            (
                jnp.einsum("bhst,bshd->bthd", d_scores, queries, preferred_element_type=jnp.float32)
                * score_scale
            )
            .astype(jnp.bfloat16)
            .reshape(token_count, local_width)
        )
        d_values = jnp.einsum(
            "bhst,bshd->bthd", weights_low, d_attended, preferred_element_type=jnp.float32
        )
        d_values = d_values.astype(jnp.bfloat16).reshape(token_count, local_width)
        d_project = jnp.stack([d_queries, d_keys, d_values])
        grad_qkv = jnp.einsum(
            "nd,knc->kdc", flat_one, d_project, preferred_element_type=jnp.float32
        )
        grad_pair = jnp.stack(
            [jnp.sum(d_queries.astype(jnp.float32), 0), jnp.sum(d_values.astype(jnp.float32), 0)]
        ).reshape(2, local_heads, HD)
        part_one = jnp.einsum(
            "knc,kdc->nd", d_project, qkv_full, preferred_element_type=jnp.float32
        )
        d_norm_one = lax.psum_scatter(
            part_one.reshape(slot_count, seq_len, model_width).astype(jnp.bfloat16),
            "tp",
            scatter_dimension=1,
            tiled=True,
        ).astype(jnp.float32)
        vector_sums[0] = vector_sums[0] + jnp.sum(d_norm_one * normed_one, (0, 1))
        vector_sums[1] = vector_sums[1] + jnp.sum(d_norm_one, (0, 1))
        grad_rows = d_middle + norm_back(d_norm_one, normed_one, inverse_one, gain_one)
        input_grads.append(grad_rows.astype(jnp.bfloat16))
        reduced = (
            lax.psum_scatter(
                grad_qkv.astype(jnp.bfloat16), "fsdp", scatter_dimension=1, tiled=True
            ).astype(jnp.float32),
            lax.psum_scatter(
                grad_pair.astype(jnp.bfloat16), "fsdp", scatter_dimension=2, tiled=True
            ).astype(jnp.float32),
            lax.psum_scatter(
                grad_outw.astype(jnp.bfloat16), "fsdp", scatter_dimension=1, tiled=True
            ).astype(jnp.float32),
            lax.psum_scatter(
                grad_fc1.astype(jnp.bfloat16), "fsdp", scatter_dimension=0, tiled=True
            ).astype(jnp.float32),
            lax.psum_scatter(
                grad_hidden.astype(jnp.bfloat16), "fsdp", scatter_dimension=1, tiled=True
            ).astype(jnp.float32),
            lax.psum_scatter(
                grad_fc2.astype(jnp.bfloat16), "fsdp", scatter_dimension=1, tiled=True
            ).astype(jnp.float32),
        )
        shard_sums = tuple((total + addend for total, addend in zip(shard_sums, reduced)))
    grad_vectors = (
        lax.psum_scatter(vector_sums[0], ("fsdp", "tp"), scatter_dimension=0, tiled=True),
        lax.psum_scatter(vector_sums[1], ("fsdp", "tp"), scatter_dimension=0, tiled=True),
        lax.psum_scatter(vector_sums[2], ("fsdp", "tp"), scatter_dimension=0, tiled=True),
        lax.psum_scatter(vector_sums[3], ("fsdp", "tp"), scatter_dimension=0, tiled=True),
        lax.psum_scatter(vector_sums[4], ("fsdp", "tp"), scatter_dimension=0, tiled=True),
        lax.psum_scatter(vector_sums[5], ("fsdp", "tp"), scatter_dimension=0, tiled=True),
    )
    return (
        jnp.stack(results),
        jnp.stack(input_grads),
        grad_vectors[0],
        grad_vectors[1],
        shard_sums[0],
        shard_sums[1],
        shard_sums[2],
        grad_vectors[2],
        grad_vectors[3],
        grad_vectors[4],
        shard_sums[3],
        shard_sums[4],
        shard_sums[5],
        grad_vectors[5],
    )


def solution(mesh):
    in_specs = (
        P(None, "fsdp", "tp", None),
        P(None, "fsdp", "tp", None),
        P(None, "fsdp"),
        P(("fsdp", "tp")),
        P(("fsdp", "tp")),
        P(None, "fsdp", "tp"),
        P(None, "tp", "fsdp"),
        P("tp", "fsdp"),
        P(("fsdp", "tp")),
        P(("fsdp", "tp")),
        P(("fsdp", "tp")),
        P("fsdp", "tp"),
        P("tp", "fsdp"),
        P("tp", "fsdp"),
        P(("fsdp", "tp")),
    )
    out_specs = (
        P(None, "fsdp", "tp", None),
        P(None, "fsdp", "tp", None),
        P(("fsdp", "tp")),
        P(("fsdp", "tp")),
        P(None, "fsdp", "tp"),
        P(None, "tp", "fsdp"),
        P("tp", "fsdp"),
        P(("fsdp", "tp")),
        P(("fsdp", "tp")),
        P(("fsdp", "tp")),
        P("fsdp", "tp"),
        P("tp", "fsdp"),
        P("tp", "fsdp"),
        P(("fsdp", "tp")),
    )
    return jax.shard_map(
        per_device, mesh=mesh, in_specs=in_specs, out_specs=out_specs, check_vma=False
    )
```

profile of v0, /device:TPU:0, one launch (start us, length us, event | category | flops | bytes accessed | tf_op | source)
XLA Modules:
  0.0 1857.9 jit_solution(1245730406476492708)
XLA Ops:
  16.0 68.5 %all-reduce.22 = (bf16[1024]{0:T(1024)(128)(2,1)S(1)}, bf16[1024]{0:T(1024)(128)(2,1)S(1)}, bf16[1024]{0:T(1024)(128)(2,1)}, bf16[1024]{0:T(1024)(128)(2,1)}, bf...) all-reduce(bf16[1024]{0:T(1024)(128)(2,1)S(1)} %dynamic-update-slice, ...), channel_id=1, replica_groups=mesh['fsdp'=16,'tp'=8] {'fsdp','tp'}, use_global_device_ids=true, to_apply=%add.1 | all-reduce | flops 6144 | bytes 24576
  87.3 21.4 %all_gather.100 = bf16[2,2,64]{1,0,2:T(2,128)(2,1)S(1)} all-gather(bf16[2,2,4]{1,0,2:T(2,128)(2,1)S(1)} %copy.106), channel_id=1, replica_groups=mesh['fsdp'=16,'tp'=8] {'fsdp'}, dimensions={2}, use_global_device_ids=true | all-gather | bytes 544 | tf_op jit(solution)/shard_map/all_gather | solution.py:92
  110.1 21.6 %all_gather.101 = bf16[128,1024]{0,1:T(8,128)(2,1)} all-gather(bf16[128,64]{0,1:T(8,128)(2,1)S(1)} %copy-done.81), channel_id=1, replica_groups=mesh['fsdp'=16,'tp'=8] {'fsdp'}, dimensions={1}, use_global_device_ids=true | all-gather | bytes 278528 | tf_op jit(solution)/shard_map/all_gather | solution.py:93
  131.6 23.0 %all_gather.99 = bf16[3,1024,128]{2,1,0:T(8,128)(2,1)S(1)} all-gather(bf16[3,64,128]{2,1,0:T(8,128)(2,1)S(1)} %copy-done.68), channel_id=1, replica_groups=mesh['fsdp'=16,'tp'=8] {'fsdp'}, dimensions={1}, use_global_device_ids=true | all-gather | bytes 835584 | tf_op jit(solution)/shard_map/all_gather | solution.py:91
  177.7 28.4 %all-gather.28.cloned.1.call-done = bf16[1,576,1024]{2,1,0:T(8,128)(2,1)} async-done(((bf16[1,72,1024]{2,1,0:T(8,128)(2,1)}), bf16[1,576,1024]{2,1,0:T(8,128)(2,1)}) %all-gather.28.cloned.1.call-update) | async-done | bytes 1179664 | tf_op jit(solution)/shard_map/all_gather | solution.py:102
  216.8 51.0 %reduce-scatter.28.cloned.1.call-done = f32[1,72,1024]{2,1,0:T(8,128)} async-done(((f32[1,576,1024]{2,1,0:T(8,128)}), f32[1,72,1024]{2,1,0:T(8,128)}) %reduce-scatter.28.cloned.1.call-update) | async-done | bytes 294928 | tf_op jit(solution)/shard_map/reduce_scatter | solution.py:123
  267.8 59.2 %reduce-scatter.32.cloned.1.call-done = f32[1,72,1024]{2,1,0:T(8,128)} async-done(((f32[1,576,1024]{2,1,0:T(8,128)}), f32[1,72,1024]{2,1,0:T(8,128)}) %reduce-scatter.32.cloned.1.call-update) | async-done | bytes 294928 | tf_op jit(solution)/shard_map/reduce_scatter | solution.py:123
  326.9 59.5 %reduce-scatter.36.cloned.1.call-done = f32[1,72,1024]{2,1,0:T(8,128)} async-done(((f32[1,576,1024]{2,1,0:T(8,128)}), f32[1,72,1024]{2,1,0:T(8,128)}) %reduce-scatter.36.cloned.1.call-update) | async-done | bytes 294928 | tf_op jit(solution)/shard_map/reduce_scatter | solution.py:123
  392.8 2.5 fusion.142
  398.0 24.2 %all-gather = bf16[16,4,8]{2,1,0:T(4,128)(2,1)S(1)} all-gather(bf16[1,4,8]{2,1,0:T(4,128)(2,1)S(1)} %bitcast.491), channel_id=1, replica_groups=mesh['fsdp'=16,'tp'=8] {'fsdp'}, dimensions={0}, use_global_device_ids=true | all-gather | bytes 1088 | tf_op jit(solution)/shard_map/all_gather | solution.py:95
  422.4 8.6 all-gather.30.cloned.1.call-done
  431.0 3.4 convolution_add_fusion
  434.3 44.2 %all-gather.22.cloned.1.call-done = bf16[512,1024]{0,1:T(8,128)(2,1)} async-done(((bf16[512,64]{0,1:T(8,128)(2,1)}), bf16[512,1024]{0,1:T(8,128)(2,1)}) %all-gather.22.cloned.1.call-update) | async-done | bytes 1048592 | tf_op jit(solution)/shard_map/all_gather | solution.py:96
  478.5 40.2 %all-gather.40.cloned.1.call-done = bf16[1,576,1024]{2,1,0:T(8,128)(2,1)} async-done(((bf16[1,72,1024]{2,1,0:T(8,128)(2,1)}), bf16[1,576,1024]{2,1,0:T(8,128)(2,1)}) %all-gather.40.cloned.1.call-update) | async-done | bytes 1179664 | tf_op jit(solution)/shard_map/all_gather | solution.py:158
  518.7 3.6 fusion.192
  525.2 35.3 %all-gather.26.cloned.1.call-done = bf16[1,576,1024]{2,1,0:T(8,128)(2,1)} async-done(((bf16[1,72,1024]{2,1,0:T(8,128)(2,1)}), bf16[1,576,1024]{2,1,0:T(8,128)(2,1)}) %all-gather.26.cloned.1.call-update) | async-done | bytes 1179664 | tf_op jit(solution)/shard_map/all_gather | solution.py:132
  565.8 36.3 %all-gather.36.cloned.1.call-done = bf16[1,576,1024]{2,1,0:T(8,128)(2,1)} async-done(((bf16[1,72,1024]{2,1,0:T(8,128)(2,1)}), bf16[1,576,1024]{2,1,0:T(8,128)(2,1)}) %all-gather.36.cloned.1.call-update) | async-done | bytes 1179664 | tf_op jit(solution)/shard_map/all_gather | solution.py:158
  602.1 3.6 fusion.191
  608.6 3.4 fusion.5
  612.1 31.5 %all-gather.18.cloned.1.call-done = bf16[1,576,1024]{2,1,0:T(8,128)(2,1)} async-done(((bf16[1,72,1024]{2,1,0:T(8,128)(2,1)}), bf16[1,576,1024]{2,1,0:T(8,128)(2,1)}) %all-gather.18.cloned.1.call-update) | async-done | bytes 1179664 | tf_op jit(solution)/shard_map/all_gather | solution.py:132
  649.2 35.9 %all-gather.32.cloned.1.call-done = bf16[1,576,1024]{2,1,0:T(8,128)(2,1)} async-done(((bf16[1,72,1024]{2,1,0:T(8,128)(2,1)}), bf16[1,576,1024]{2,1,0:T(8,128)(2,1)}) %all-gather.32.cloned.1.call-update) | async-done | bytes 1179664 | tf_op jit(solution)/shard_map/all_gather | solution.py:158
  685.1 3.7 fusion.193
  692.0 35.9 %reduce-scatter.48.cloned.1.call-done = bf16[1,72,1024]{2,1,0:T(8,128)(2,1)} async-done(((bf16[1,576,1024]{2,1,0:T(8,128)(2,1)}), bf16[1,72,1024]{2,1,0:T(8,128)(2,1)}) %reduce-scatter.48.cloned.1.call-update) | async-done | bytes 147472 | tf_op jit(solution)/shard_map/reduce_scatter | solution.py:171
  727.9 41.6 %reduce-scatter.34.cloned.1.call-done = bf16[1,72,1024]{2,1,0:T(8,128)(2,1)} async-done(((bf16[1,576,1024]{2,1,0:T(8,128)(2,1)}), bf16[1,72,1024]{2,1,0:T(8,128)(2,1)}) %reduce-scatter.34.cloned.1.call-update) | async-done | bytes 147472 | tf_op jit(solution)/shard_map/reduce_scatter | solution.py:137
  769.5 41.8 %reduce-scatter.44.cloned.1.call-done = bf16[1,72,1024]{2,1,0:T(8,128)(2,1)} async-done(((bf16[1,576,1024]{2,1,0:T(8,128)(2,1)}), bf16[1,72,1024]{2,1,0:T(8,128)(2,1)}) %reduce-scatter.44.cloned.1.call-update) | async-done | bytes 147472 | tf_op jit(solution)/shard_map/reduce_scatter | solution.py:171
  811.3 2.8 fusion.137
  816.2 37.1 %reduce-scatter.38.cloned.1.call-done = bf16[1,72,1024]{2,1,0:T(8,128)(2,1)} async-done(((bf16[1,576,1024]{2,1,0:T(8,128)(2,1)}), bf16[1,72,1024]{2,1,0:T(8,128)(2,1)}) %reduce-scatter.38.cloned.1.call-update) | async-done | bytes 147472 | tf_op jit(solution)/shard_map/reduce_scatter | solution.py:137
  853.2 41.7 %reduce-scatter.30.cloned.1.call-done = bf16[1,72,1024]{2,1,0:T(8,128)(2,1)} async-done(((bf16[1,576,1024]{2,1,0:T(8,128)(2,1)}), bf16[1,72,1024]{2,1,0:T(8,128)(2,1)}) %reduce-scatter.30.cloned.1.call-update) | async-done | bytes 147472 | tf_op jit(solution)/shard_map/reduce_scatter | solution.py:137
  894.9 41.7 %reduce-scatter.40.cloned.1.call-done = bf16[1,72,1024]{2,1,0:T(8,128)(2,1)} async-done(((bf16[1,576,1024]{2,1,0:T(8,128)(2,1)}), bf16[1,72,1024]{2,1,0:T(8,128)(2,1)}) %reduce-scatter.40.cloned.1.call-update) | async-done | bytes 147472 | tf_op jit(solution)/shard_map/reduce_scatter | solution.py:171
  936.7 3.0 fusion.178
  947.0 3.4 convolution_convert_fusion.9
  950.5 3.5 convolution_convert_fusion.10
  954.1 3.4 convolution_convert_fusion.11
  957.6 3.8 convolution_convert_fusion.6
  961.4 3.7 convolution_convert_fusion.7
  965.3 3.7 convolution_convert_fusion.8
  969.1 12.8 all-gather.34.cloned.1.call-done
  981.9 2.5 fusion.51
  985.5 2.7 convolution_convert_fusion.17
  988.2 3.7 bitcast_reduce_fusion.4
  992.2 30.7 %all-gather.38.cloned.1.call-done = bf16[1,576,1024]{2,1,0:T(8,128)(2,1)} async-done(((bf16[1,72,1024]{2,1,0:T(8,128)(2,1)}), bf16[1,576,1024]{2,1,0:T(8,128)(2,1)}) %all-gather.38.cloned.1.call-update) | async-done | bytes 1179664 | tf_op jit(solution)/shard_map/all_gather | solution.py:182
  1022.9 2.7 convolution_convert_fusion.16
  1025.6 5.0 multiply_reduce_fusion.2
  1030.6 3.5 multiply_convert_fusion.2
  1040.1 26.3 %all-gather.42.cloned.1.call-done = bf16[1,576,1024]{2,1,0:T(8,128)(2,1)} async-done(((bf16[1,72,1024]{2,1,0:T(8,128)(2,1)}), bf16[1,576,1024]{2,1,0:T(8,128)(2,1)}) %all-gather.42.cloned.1.call-update) | async-done | bytes 1179664 | tf_op jit(solution)/shard_map/all_gather | solution.py:182
  1066.4 2.6 convolution_convert_fusion.15
  1071.9 3.2 fusion.9
  1078.7 3.7 bitcast_reduce_fusion.2
  1084.1 2.9 multiply_reduce_fusion.1
  1093.4 3.2 fusion.10
  1105.3 2.5 bitcast_reduce_fusion
  1118.4 41.0 %reduce-scatter.58.cloned.1.call-done = bf16[64,512]{1,0:T(8,128)(2,1)} async-done(((bf16[1024,512]{1,0:T(8,128)(2,1)}), bf16[64,512]{1,0:T(8,128)(2,1)}) %reduce-scatter.58.cloned.1.call-update) | async-done | bytes 65552 | tf_op jit(solution)/shard_map/reduce_scatter | solution.py:250
  1160.9 68.5 %reduce-scatter.68.cloned.1.call-done = bf16[512,64]{0,1:T(8,128)(2,1)} async-done(((bf16[512,1024]{0,1:T(8,128)(2,1)}), bf16[512,64]{0,1:T(8,128)(2,1)}) %reduce-scatter.68.cloned.1.call-update) | async-done | bytes 65552 | tf_op jit(solution)/shard_map/reduce_scatter | solution.py:256
  1229.4 69.5 %reduce-scatter.66.cloned.1.call-done = bf16[512,64]{0,1:T(8,128)(2,1)} async-done(((bf16[512,1024]{0,1:T(8,128)(2,1)}), bf16[512,64]{0,1:T(8,128)(2,1)}) %reduce-scatter.66.cloned.1.call-update) | async-done | bytes 65552 | tf_op jit(solution)/shard_map/reduce_scatter | solution.py:256
  1298.9 70.1 %reduce-scatter.64.cloned.1.call-done = bf16[512,64]{0,1:T(8,128)(2,1)} async-done(((bf16[512,1024]{0,1:T(8,128)(2,1)}), bf16[512,64]{0,1:T(8,128)(2,1)}) %reduce-scatter.64.cloned.1.call-update) | async-done | bytes 65552 | tf_op jit(solution)/shard_map/reduce_scatter | solution.py:256
  1379.2 34.5 %all-reduce.23 = (bf16[2,2,64]{2,1,0:T(2,128)(2,1)S(1)}, bf16[2,2,64]{2,1,0:T(2,128)(2,1)S(1)}, bf16[2,2,64]{2,1,0:T(2,128)(2,1)S(1)}, bf16[8,64]{1,0:T(8,128)(2...) all-reduce(bf16[2,2,64]{2,1,0:T(2,128)(2,1)S(1)} %pad_maximum_fusio, ...), channel_id=19, replica_groups=mesh['fsdp'=16,'tp'=8] {'fsdp'}, use_global_device_ids=true, to_apply=%region_58.0.clone | all-reduce | flops 2304 | bytes 9216
  1415.1 21.5 %reduce-scatter.52.cloned.1.call-done = bf16[128,64]{0,1:T(8,128)(2,1)} async-done(((bf16[128,1024]{0,1:T(8,128)(2,1)}), bf16[128,64]{0,1:T(8,128)(2,1)}) %reduce-scatter.52.cloned.1.call-update) | async-done | bytes 16400 | tf_op jit(solution)/shard_map/reduce_scatter | solution.py:247
  1436.6 68.2 %reduce-scatter.54.cloned.1.call-done = bf16[128,64]{0,1:T(8,128)(2,1)} async-done(((bf16[128,1024]{0,1:T(8,128)(2,1)}), bf16[128,64]{0,1:T(8,128)(2,1)}) %reduce-scatter.54.cloned.1.call-update) | async-done | bytes 16400 | tf_op jit(solution)/shard_map/reduce_scatter | solution.py:247
  1504.8 67.7 %reduce-scatter.56.cloned.1.call-done = bf16[128,64]{0,1:T(8,128)(2,1)} async-done(((bf16[128,1024]{0,1:T(8,128)(2,1)}), bf16[128,64]{0,1:T(8,128)(2,1)}) %reduce-scatter.56.cloned.1.call-update) | async-done | bytes 16400 | tf_op jit(solution)/shard_map/reduce_scatter | solution.py:247
  1573.8 40.3 %reduce-scatter.42.cloned.1.call-done = bf16[1,72,1024]{2,1,0:T(8,128)(2,1)} async-done(((bf16[1,576,1024]{2,1,0:T(8,128)(2,1)}), bf16[1,72,1024]{2,1,0:T(8,128)(2,1)}) %reduce-scatter.42.cloned.1.call-update) | async-done | bytes 147472 | tf_op jit(solution)/shard_map/reduce_scatter | solution.py:230
  1614.1 42.0 %reduce-scatter.46.cloned.1.call-done = bf16[1,72,1024]{2,1,0:T(8,128)(2,1)} async-done(((bf16[1,576,1024]{2,1,0:T(8,128)(2,1)}), bf16[1,72,1024]{2,1,0:T(8,128)(2,1)}) %reduce-scatter.46.cloned.1.call-update) | async-done | bytes 147472 | tf_op jit(solution)/shard_map/reduce_scatter | solution.py:230
  1656.1 41.8 %reduce-scatter.50.cloned.1.call-done = bf16[1,72,1024]{2,1,0:T(8,128)(2,1)} async-done(((bf16[1,576,1024]{2,1,0:T(8,128)(2,1)}), bf16[1,72,1024]{2,1,0:T(8,128)(2,1)}) %reduce-scatter.50.cloned.1.call-update) | async-done | bytes 147472 | tf_op jit(solution)/shard_map/reduce_scatter | solution.py:230
  1699.7 65.8 %all-reduce.21 = (f32[1024]{0:T(1024)S(1)}, f32[1024]{0:T(1024)S(1)}, f32[1024]{0:T(1024)S(1)}, f32[1024]{0:T(1024)S(1)}, f32[1024]{0:T(1024)S(1)}, /*index=5*/f32[1024]{0:T(1024)S(1)}) all-reduce(f32[1024]{0:T(1024)S(1)} %add_add_fusion.5, f32[1024]{0:T(1024)S(1)} %add_add_fusion.4, ...), channel_id=14, replica_groups=mesh['fsdp'=16,'tp'=8] {'fsdp','tp'}, use_global_device_ids=true, to_apply=%region_48.0.clone | all-reduce | flops 6144 | bytes 49152
  1769.1 78.4 %all-reduce.27.cloned.1.call-done = (bf16[3,1024,128]{2,0,1:T(4,128)(2,1)}, bf16[3,1024,128]{2,0,1:T(4,128)(2,1)}, bf16[3,1024,128]{2,0,1:T(4,128)(2,1)}) async-done(((bf16[3,1024,128]{2,0,1:T(4,128)(2,1)}, bf16[3,1024,128]{2,0,1:T(4,128)(2,1)}, bf16[3,1024,128]{2,0,1:T(4,128)(2,1)}), (bf16[3,1024,128]{2,0,1:T(4,128)(2,1)}, bf16[3,1024,128]{2,0,1:T(4,128)(2,1)}, ...) | async-done | bytes 2359312
  (499 shorter events, 143.9 us)
Async XLA Ops:
  8.0 146.5 %all-gather.16.cloned.1.call-start = ((), (), s32[]{:S(2)}) async-start(), calls=%async_computation.21 | async-start | bytes 1327104 | tf_op jit(solution)/shard_map/all_gather | solution.py:102
  85.5 80.0 %all-gather.24.cloned.1.call-start = ((), (), s32[]{:S(2)}) async-start(), calls=%async_computation.27 | async-start | bytes 1327104 | tf_op jit(solution)/shard_map/all_gather | solution.py:102
  86.3 119.8 %all-gather.28.cloned.1.call-start = ((), (), s32[]{:S(2)}) async-start(), calls=%async_computation.31 | async-start | bytes 1327104 | tf_op jit(solution)/shard_map/all_gather | solution.py:102
  87.0 180.7 %reduce-scatter.28.cloned.1.call-start = ((), (), s32[]{:S(2)}) async-start(), calls=%async_computation.22 | async-start | bytes 2654208 | tf_op jit(solution)/shard_map/reduce_scatter | solution.py:123
  165.5 161.5 %reduce-scatter.32.cloned.1.call-start = ((), (), s32[]{:S(2)}) async-start(), calls=%async_computation.28 | async-start | bytes 2654208 | tf_op jit(solution)/shard_map/reduce_scatter | solution.py:123
  177.2 209.2 %reduce-scatter.36.cloned.1.call-start = ((), (), s32[]{:S(2)}) async-start(), calls=%async_computation.32 | async-start | bytes 2654208 | tf_op jit(solution)/shard_map/reduce_scatter | solution.py:123
  216.0 206.4 %all-gather.20.cloned.1.call-start = ((), (), s32[]{:S(2)}) async-start(), calls=%async_computation.24 | async-start | bytes 1114112 | tf_op jit(solution)/shard_map/all_gather | solution.py:94
  216.6 214.3 %all-gather.30.cloned.1.call-start = ((), (), s32[]{:S(2)}) async-start(), calls=%async_computation.33 | async-start | bytes 1327104 | tf_op jit(solution)/shard_map/all_gather | solution.py:132
  389.6 88.9 %all-gather.22.cloned.1.call-start = ((), (), s32[]{:S(2)}) async-start(), calls=%async_computation.25 | async-start | bytes 1114112 | tf_op jit(solution)/shard_map/all_gather | solution.py:96
  390.2 128.5 %all-gather.40.cloned.1.call-start = ((), (), s32[]{:S(2)}) async-start(), calls=%async_computation.43 | async-start | bytes 1327104 | tf_op jit(solution)/shard_map/all_gather | solution.py:158
  395.3 165.1 %all-gather.26.cloned.1.call-start = ((), (), s32[]{:S(2)}) async-start(), calls=%async_computation.29 | async-start | bytes 1327104 | tf_op jit(solution)/shard_map/all_gather | solution.py:132
  396.1 206.0 %all-gather.36.cloned.1.call-start = ((), (), s32[]{:S(2)}) async-start(), calls=%async_computation.39 | async-start | bytes 1327104 | tf_op jit(solution)/shard_map/all_gather | solution.py:158
  396.8 246.8 %all-gather.18.cloned.1.call-start = ((), (), s32[]{:S(2)}) async-start(), calls=%async_computation.23 | async-start | bytes 1327104 | tf_op jit(solution)/shard_map/all_gather | solution.py:132
  397.4 287.7 %all-gather.32.cloned.1.call-start = ((), (), s32[]{:S(2)}) async-start(), calls=%async_computation.35 | async-start | bytes 1327104 | tf_op jit(solution)/shard_map/all_gather | solution.py:158
  398.0 329.9 %reduce-scatter.48.cloned.1.call-start = ((), (), s32[]{:S(2)}) async-start(), calls=%async_computation.44 | async-start | bytes 1327104 | tf_op jit(solution)/shard_map/reduce_scatter | solution.py:171
  525.1 244.4 %reduce-scatter.34.cloned.1.call-start = ((), (), s32[]{:S(2)}) async-start(), calls=%async_computation.30 | async-start | bytes 1327104 | tf_op jit(solution)/shard_map/reduce_scatter | solution.py:137
  565.8 245.6 %reduce-scatter.44.cloned.1.call-start = ((), (), s32[]{:S(2)}) async-start(), calls=%async_computation.40 | async-start | bytes 1327104 | tf_op jit(solution)/shard_map/reduce_scatter | solution.py:171
  608.5 244.7 %reduce-scatter.38.cloned.1.call-start = ((), (), s32[]{:S(2)}) async-start(), calls=%async_computation.34 | async-start | bytes 1327104 | tf_op jit(solution)/shard_map/reduce_scatter | solution.py:137
  612.0 282.9 %reduce-scatter.30.cloned.1.call-start = ((), (), s32[]{:S(2)}) async-start(), calls=%async_computation.26 | async-start | bytes 1327104 | tf_op jit(solution)/shard_map/reduce_scatter | solution.py:137
  649.0 287.7 %reduce-scatter.40.cloned.1.call-start = ((), (), s32[]{:S(2)}) async-start(), calls=%async_computation.36 | async-start | bytes 1327104 | tf_op jit(solution)/shard_map/reduce_scatter | solution.py:171
  691.4 290.5 %all-gather.34.cloned.1.call-start = ((), (), s32[]{:S(2)}) async-start(), calls=%async_computation.37 | async-start | bytes 1327104 | tf_op jit(solution)/shard_map/all_gather | solution.py:182
  943.6 79.3 %all-gather.38.cloned.1.call-start = ((), (), s32[]{:S(2)}) async-start(), calls=%async_computation.41 | async-start | bytes 1327104 | tf_op jit(solution)/shard_map/all_gather | solution.py:182
  945.3 121.1 %all-gather.42.cloned.1.call-start = ((), (), s32[]{:S(2)}) async-start(), calls=%async_computation.45 | async-start | bytes 1327104 | tf_op jit(solution)/shard_map/all_gather | solution.py:182
  947.0 171.4 %reduce-scatter.62.cloned.1.call-start = ((), (), s32[]{:S(2)}) async-start(), calls=%async_computation.52 | async-start | bytes 1114112 | tf_op jit(solution)/shard_map/reduce_scatter | solution.py:250
  950.5 167.9 %reduce-scatter.60.cloned.1.call-start = ((), (), s32[]{:S(2)}) async-start(), calls=%async_computation.51 | async-start | bytes 1114112 | tf_op jit(solution)/shard_map/reduce_scatter | solution.py:250
  954.0 205.3 %reduce-scatter.58.cloned.1.call-start = ((), (), s32[]{:S(2)}) async-start(), calls=%async_computation.50 | async-start | bytes 1114112 | tf_op jit(solution)/shard_map/reduce_scatter | solution.py:250
  957.5 271.9 %reduce-scatter.68.cloned.1.call-start = ((), (), s32[]{:S(2)}) async-start(), calls=%async_computation.55 | async-start | bytes 1114112 | tf_op jit(solution)/shard_map/reduce_scatter | solution.py:256
  961.4 337.5 %reduce-scatter.66.cloned.1.call-start = ((), (), s32[]{:S(2)}) async-start(), calls=%async_computation.54 | async-start | bytes 1114112 | tf_op jit(solution)/shard_map/reduce_scatter | solution.py:256
  965.2 403.8 %reduce-scatter.64.cloned.1.call-start = ((), (), s32[]{:S(2)}) async-start(), calls=%async_computation.53 | async-start | bytes 1114112 | tf_op jit(solution)/shard_map/reduce_scatter | solution.py:256
  969.0 467.6 %reduce-scatter.52.cloned.1.call-start = ((), (), s32[]{:S(2)}) async-start(), calls=%async_computation.47 | async-start | bytes 278528 | tf_op jit(solution)/shard_map/reduce_scatter | solution.py:247
  991.9 512.8 %reduce-scatter.54.cloned.1.call-start = ((), (), s32[]{:S(2)}) async-start(), calls=%async_computation.48 | async-start | bytes 278528 | tf_op jit(solution)/shard_map/reduce_scatter | solution.py:247
  1030.5 541.9 %reduce-scatter.56.cloned.1.call-start = ((), (), s32[]{:S(2)}) async-start(), calls=%async_computation.49 | async-start | bytes 278528 | tf_op jit(solution)/shard_map/reduce_scatter | solution.py:247
  1069.0 545.1 %reduce-scatter.42.cloned.1.call-start = ((), (), s32[]{:S(2)}) async-start(), calls=%async_computation.38 | async-start | bytes 1327104 | tf_op jit(solution)/shard_map/reduce_scatter | solution.py:230
  1075.2 581.0 %reduce-scatter.46.cloned.1.call-start = ((), (), s32[]{:S(2)}) async-start(), calls=%async_computation.42 | async-start | bytes 1327104 | tf_op jit(solution)/shard_map/reduce_scatter | solution.py:230
  1096.7 601.3 %reduce-scatter.50.cloned.1.call-start = ((), (), s32[]{:S(2)}) async-start(), calls=%async_computation.46 | async-start | bytes 1327104 | tf_op jit(solution)/shard_map/reduce_scatter | solution.py:230
  1118.1 252.4 %copy-start.44 = (bf16[1,1,72,1024]{3,2,1,0:T(8,128)(2,1)S(1)}, bf16[1,1,72,1024]{3,2,1,0:T(8,128)(2,1)}, u32[]{:S(2)}) copy-start(bf16[1,1,72,1024]{3,2,1,0:T(8,128)(2,1)} %get-tuple-element.147) | copy-start | bytes 442372
  1118.1 252.4 %copy-start.45 = (bf16[1,1,72,1024]{3,2,1,0:T(8,128)(2,1)S(1)}, bf16[1,1,72,1024]{3,2,1,0:T(8,128)(2,1)}, u32[]{:S(2)}) copy-start(bf16[1,1,72,1024]{3,2,1,0:T(8,128)(2,1)} %get-tuple-element.148) | copy-start | bytes 442372
  1118.1 252.4 %copy-start.46 = (bf16[1,1,72,1024]{3,2,1,0:T(8,128)(2,1)S(1)}, bf16[1,1,72,1024]{3,2,1,0:T(8,128)(2,1)}, u32[]{:S(2)}) copy-start(bf16[1,1,72,1024]{3,2,1,0:T(8,128)(2,1)} %get-tuple-element.151) | copy-start | bytes 442372
  1118.1 253.3 %copy-start.74 = (f32[1024]{0:T(1024)S(1)}, f32[1024]{0:T(1024)}, u32[]{:S(2)}) copy-start(f32[1024]{0:T(1024)} %get-tuple-element.66) | copy-start | bytes 12292
  1118.2 253.3 %copy-start.75 = (f32[1024]{0:T(1024)S(1)}, f32[1024]{0:T(1024)}, u32[]{:S(2)}) copy-start(f32[1024]{0:T(1024)} %get-tuple-element.162) | copy-start | bytes 12292
  1118.2 253.2 %copy-start.78 = (f32[1024]{0:T(1024)S(1)}, f32[1024]{0:T(1024)}, u32[]{:S(2)}) copy-start(f32[1024]{0:T(1024)} %get-tuple-element.155) | copy-start | bytes 12292
  1118.2 253.2 %copy-start.72 = (f32[1024]{0:T(1024)S(1)}, f32[1024]{0:T(1024)}, u32[]{:S(2)}) copy-start(f32[1024]{0:T(1024)} %get-tuple-element.89) | copy-start | bytes 12292
  1118.2 253.2 %copy-start.73 = (f32[1024]{0:T(1024)S(1)}, f32[1024]{0:T(1024)}, u32[]{:S(2)}) copy-start(f32[1024]{0:T(1024)} %get-tuple-element.159) | copy-start | bytes 12292
  1118.2 253.2 %copy-start.77 = (f32[1024]{0:T(1024)S(1)}, f32[1024]{0:T(1024)}, u32[]{:S(2)}) copy-start(f32[1024]{0:T(1024)} %get-tuple-element.152) | copy-start | bytes 12292
  1118.2 253.3 %copy-start.76 = (f32[1024]{0:T(1024)S(1)}, f32[1024]{0:T(1024)}, u32[]{:S(2)}) copy-start(f32[1024]{0:T(1024)} %get-tuple-element.118) | copy-start | bytes 12292
  1118.2 253.3 %copy-start.79 = (f32[1024]{0:T(1024)S(1)}, f32[1024]{0:T(1024)}, u32[]{:S(2)}) copy-start(f32[1024]{0:T(1024)} %get-tuple-element.116) | copy-start | bytes 12292
  1118.2 253.3 %copy-start.80 = (f32[1024]{0:T(1024)S(1)}, f32[1024]{0:T(1024)}, u32[]{:S(2)}) copy-start(f32[1024]{0:T(1024)} %get-tuple-element.137) | copy-start | bytes 12292
  1118.2 253.3 %copy-start.34 = (bf16[1,576,1024]{2,1,0:T(8,128)(2,1)S(1)}, bf16[1,576,1024]{2,1,0:T(8,128)(2,1)}, u32[]{:S(2)}) copy-start(bf16[1,576,1024]{2,1,0:T(8,128)(2,1)} %all-gather.16.cloned.1.call-done) | copy-start | bytes 3538948
  1118.2 253.3 %copy-start.49 = (bf16[1,576,128]{2,1,0:T(8,128)(2,1)S(1)}, bf16[1,576,128]{2,1,0:T(8,128)(2,1)}, u32[]{:S(2)}) copy-start(bf16[1,576,128]{2,1,0:T(8,128)(2,1)} %copy.127) | copy-start | bytes 442372
  1118.2 253.3 %copy-start.50 = (bf16[1,576,128]{2,1,0:T(8,128)(2,1)S(1)}, bf16[1,576,128]{2,1,0:T(8,128)(2,1)}, u32[]{:S(2)}) copy-start(bf16[1,576,128]{2,1,0:T(8,128)(2,1)} %copy.125) | copy-start | bytes 442372
  1118.3 253.3 %copy-start.51 = (bf16[1,576,128]{2,1,0:T(8,128)(2,1)S(1)}, bf16[1,576,128]{2,1,0:T(8,128)(2,1)}, u32[]{:S(2)}) copy-start(bf16[1,576,128]{2,1,0:T(8,128)(2,1)} %copy.126) | copy-start | bytes 442372
  1118.3 729.2 %all-reduce.27.cloned.1.call-start = ((), (), s32[]{:S(2)}) async-start(), calls=%async_computation.56 | async-start | bytes 6291456
  1378.6 319.4 %copy-start.63 = (f32[1024]{0:T(1024)S(1)}, f32[1024]{0:T(1024)}, u32[]{:S(2)}) copy-start(f32[1024]{0:T(1024)} %copy-done.62) | copy-start | bytes 12292
  1378.6 319.4 %copy-start.84 = (f32[72]{0:T(128)S(1)}, f32[72]{0:T(128)}, u32[]{:S(2)}) copy-start(f32[72]{0:T(128)} %copy-done.83) | copy-start | bytes 868
  1378.6 319.4 %copy-start.86 = (f32[72]{0:T(128)S(1)}, f32[72]{0:T(128)}, u32[]{:S(2)}) copy-start(f32[72]{0:T(128)} %copy-done.85) | copy-start | bytes 868
  1378.6 319.4 %copy-start.88 = (f32[72]{0:T(128)S(1)}, f32[72]{0:T(128)}, u32[]{:S(2)}) copy-start(f32[72]{0:T(128)} %copy-done.87) | copy-start | bytes 868
  1378.6 319.4 %copy-start.94 = (f32[72]{0:T(128)S(1)}, f32[72]{0:T(128)}, u32[]{:S(2)}) copy-start(f32[72]{0:T(128)} %copy-done.93) | copy-start | bytes 868
  1378.6 319.4 %copy-start.96 = (f32[72]{0:T(128)S(1)}, f32[72]{0:T(128)}, u32[]{:S(2)}) copy-start(f32[72]{0:T(128)} %copy-done.95) | copy-start | bytes 868
  1378.6 319.4 %copy-start.98 = (f32[72]{0:T(128)S(1)}, f32[72]{0:T(128)}, u32[]{:S(2)}) copy-start(f32[72]{0:T(128)} %copy-done.97) | copy-start | bytes 868
  1378.6 321.1 %copy-start.82 = (f32[1024]{0:T(1024)S(1)}, f32[1024]{0:T(1024)}, u32[]{:S(2)}) copy-start(f32[1024]{0:T(1024)} %add_add_fusion) | copy-start | bytes 12292
  1379.2 469.8 %copy-start.19 = (f32[1,72,1024]{2,1,0:T(8,128)S(1)}, f32[1,72,1024]{2,1,0:T(8,128)}, u32[]{:S(2)}) copy-start(f32[1,72,1024]{2,1,0:T(8,128)} %get-tuple-element.119) | copy-start | bytes 884740
  1573.8 275.4 %copy-start.21 = (f32[1,72,1024]{2,1,0:T(8,128)S(1)}, f32[1,72,1024]{2,1,0:T(8,128)}, u32[]{:S(2)}) copy-start(f32[1,72,1024]{2,1,0:T(8,128)} %copy-done.20) | copy-start | bytes 884740
  1573.8 275.4 %copy-start.22 = (f32[1,72,1024]{2,1,0:T(8,128)S(1)}, f32[1,72,1024]{2,1,0:T(8,128)}, u32[]{:S(2)}) copy-start(f32[1,72,1024]{2,1,0:T(8,128)} %get-tuple-element.138) | copy-start | bytes 884740
  1614.1 235.2 %copy-start.47 = (bf16[1,72,1024]{2,1,0:T(8,128)(2,1)S(1)}, bf16[1,72,1024]{2,1,0:T(8,128)(2,1)}, u32[]{:S(2)}) copy-start(bf16[1,72,1024]{2,1,0:T(8,128)(2,1)} %reduce-scatter.42.cloned.1.call-done) | copy-start | bytes 442372
  (102 other events, 1637.7 us)
Sparse Core Ops, SparseCore 0:
  85.7 35.8 all-gather.15
  123.2 42.2 all-gather.23
  167.1 38.9 all-gather.27
  208.3 59.3 reduce-scatter.27
  270.0 56.8 reduce-scatter.31
  329.2 57.1 reduce-scatter.35
  943.7 38.2 all-gather.33
  983.7 39.1 all-gather.37
  1024.5 41.8 all-gather.41
Sparse Core Ops, SparseCore 1:
  219.0 53.8 all-gather.19
  389.7 41.2 all-gather.29
  433.3 45.2 all-gather.21
  480.2 38.5 all-gather.39
  520.4 40.0 all-gather.25
  562.1 39.9 all-gather.35
  603.6 39.9 all-gather.17
  645.1 39.9 all-gather.31
  687.4 40.5 reduce-scatter.47
  730.3 39.2 reduce-scatter.33
  771.8 39.5 reduce-scatter.43
  813.8 39.4 reduce-scatter.37
  855.5 39.4 reduce-scatter.29
  897.3 39.3 reduce-scatter.39
  951.6 65.8 reduce-scatter.61
  1021.8 68.0 reduce-scatter.59
  1093.6 65.7 reduce-scatter.57
  1163.7 65.7 reduce-scatter.67
  1233.1 65.7 reduce-scatter.65
  1303.2 65.7 reduce-scatter.63
  1372.6 64.0 reduce-scatter.51
  1440.7 64.0 reduce-scatter.53
  1508.4 64.0 reduce-scatter.55
  1575.0 39.0 reduce-scatter.41
  1616.5 39.6 reduce-scatter.45
  1658.7 39.2 reduce-scatter.49
  1700.9 146.5 all-reduce.26
where the time goes:
time: 1870 us; the launch traced here: 1860 us
  waiting for transfers between devices  1350 us (72%)
  blocking collectives  259 us (14%)
  matrix products  127 us (7%)
  local copies, waits for them, and re-layouts  54 us (3%)
  other arithmetic  40.3 us (2%)
  between operations  21 us (1%)
    reduce_scatter x3, waiting for transfers between devices, per_device(): lax.psum_scatter(grad_fc2.astype(jnp.bfloat16), 'fsdp', scatter_dimension...  208 us
    reduce_scatter x3, waiting for transfers between devices, per_device(): lax.psum_scatter(branch_part.reshape(slot_count, seq_len, model_width), '...  170 us
    unnamed x3, blocking collectives  169 us
    reduce_scatter x3, waiting for transfers between devices, per_device(): lax.psum_scatter(grad_outw.astype(jnp.bfloat16), 'fsdp', scatter_dimensio...  157 us
    reduce_scatter x3, waiting for transfers between devices, per_device(): lax.psum_scatter(part_one.reshape(slot_count, seq_len, model_width).astyp...  124 us
    reduce_scatter x3, waiting for transfers between devices, per_device(): lax.psum_scatter(mlp_part.reshape(slot_count, seq_len, model_width).astyp...  120 us
    reduce_scatter x3, waiting for transfers between devices, per_device(): lax.psum_scatter(part_two.reshape(slot_count, seq_len, model_width).astyp...  119 us
    all_gather x3, waiting for transfers between devices, per_device(): lax.all_gather(upstream_low, 'tp', axis=1, tiled=True)  112 us
  transfers between devices with their start and end apart: 36, of which 31 were waited for; matrix products, arithmetic and copies ran while one was open for 10% of the time, Pallas kernels for 0%

commit v1 on v0

v1 whole, which is shorter than its diff:
```python
import functools
import math

import jax
import jax.numpy as jnp
from jax import lax
from jax.experimental import pallas as pl
from jax.experimental.pallas import tpu as pltpu
from jax.sharding import PartitionSpec as P

MESH = pl.DeviceIdType.MESH
HD = 64
EPSILON = 1e-05
BF16 = jnp.bfloat16
F32 = jnp.float32
VMEM_LIMIT = 56 * 2**20
ORDERS = (("x", "y", "z"), ("y", "z", "x"), ("z", "x", "y"), ("x", "y", "z"))


def place():
    f, t = lax.axis_index("fsdp"), lax.axis_index("tp")
    return {
        "x": t // 2,
        "y": lax.rem(f // 2, 4),
        "z": (f // 8) * 2 + lax.rem(t, 2),
        "c": lax.rem(f, 2),
    }


def device_at(spot):
    return (
        (spot["z"] // 2) * 8 + spot["y"] * 2 + spot["c"],
        spot["x"] * 2 + lax.rem(spot["z"], 2),
    )


def shifted(spot, axis, by):
    return {**spot, axis: lax.rem(spot[axis] + by + 4, 4)}


def sibling(spot):
    return {**spot, "c": 1 - spot["c"]}


def greet(devices):
    barrier = pltpu.get_barrier_semaphore()
    for device in devices:
        pl.semaphore_signal(barrier, inc=1, device_id=device, device_id_type=MESH)
    pl.semaphore_wait(barrier, len(devices))


def greet_torus(spot):
    greet(
        [device_at(shifted(spot, axis, by)) for axis in "xyz" for by in (1, -1)]
        + [device_at(sibling(spot))]
    )


def view(ref, spot, full, core=None, rows=slice(None)):
    whole = slice(None)
    index = [
        whole if "x" in full else spot["x"],
        whole if "z" in full else lax.rem(spot["z"], 2),
        whole if "z" in full else spot["z"] // 2,
        whole if "y" in full else spot["y"],
    ]
    if core is not None:
        index.append(core)
    return ref.at[tuple(index) + (rows,)]


def gather_kernel(*refs):
    parts = len(ORDERS)
    ins, outs = refs[:parts], refs[parts : 2 * parts]
    local_sem, send_sem, recv_sem, sib_send, sib_recv = refs[2 * parts :]
    me = place()
    core = me["c"]
    greet_torus(me)
    other = device_at(sibling(me))
    sends = []

    def remote(src, dst, send, recv, device):
        copy = pltpu.make_async_remote_copy(
            src, dst, send, recv, device_id=device, device_id_type=MESH
        )
        copy.start()
        sends.append(copy)
        return copy

    shares = []

    def share(part, slot, piece):
        shares.append(
            remote(piece, piece, sib_send.at[part, slot], sib_recv.at[part, slot], other)
        )

    own = []
    for part in range(parts):
        copy = pltpu.make_async_copy(
            ins[part], view(outs[part], me, "", core), local_sem.at[part]
        )
        copy.start()
        own.append(copy)
    for part in range(parts):
        own[part].wait()
    for phase in range(3):
        near = {}
        for part in range(parts):
            order, out = ORDERS[part], outs[part]
            axis, full = order[phase], "".join(order[:phase])
            bundle = view(out, me, full, core)
            for way, by in enumerate((1, -1)):
                near[part, way] = remote(
                    bundle,
                    bundle,
                    send_sem.at[part, phase, way],
                    recv_sem.at[part, phase, way],
                    device_at(shifted(me, axis, by)),
                )
            if phase == 0:
                share(part, 0, bundle)
        far = {}
        for part in range(parts):
            order, out = ORDERS[part], outs[part]
            axis, full = order[phase], "".join(order[:phase])
            half = out.shape[-2] // 2
            for way, by in enumerate((1, -1)):
                near[part, way].wait_recv()
                piece = view(
                    out, shifted(me, axis, -by), full, core, pl.ds(way * half, half)
                )
                far[part, way] = remote(
                    piece,
                    piece,
                    send_sem.at[part, phase, 2 + way],
                    recv_sem.at[part, phase, 2 + way],
                    device_at(shifted(me, axis, by)),
                )
                share(part, 1 + 3 * phase + way, view(out, shifted(me, axis, -by), full, core))
        for part in range(parts):
            order, out = ORDERS[part], outs[part]
            axis, full = order[phase], "".join(order[:phase])
            for way in range(2):
                far[part, way].wait_recv()
            share(part, 3 + 3 * phase, view(out, shifted(me, axis, 2), full, core))
    for copy in sends:
        copy.wait_send()
    for copy in shares:
        copy.wait_recv()


def gather_weights(blocks):
    parts = len(blocks)
    return pl.pallas_call(
        gather_kernel,
        out_shape=[
            jax.ShapeDtypeStruct((4, 2, 2, 4, 2) + block.shape, block.dtype) for block in blocks
        ],
        in_specs=[pl.BlockSpec(memory_space=pl.ANY)] * parts,
        out_specs=[pl.BlockSpec(memory_space=pl.ANY)] * parts,
        scratch_shapes=[
            pltpu.SemaphoreType.DMA((parts,)),
            pltpu.SemaphoreType.DMA((parts, 3, 4)),
            pltpu.SemaphoreType.DMA((parts, 3, 4)),
            pltpu.SemaphoreType.DMA((parts, 10)),
            pltpu.SemaphoreType.DMA((parts, 10)),
        ],
        compiler_params=pltpu.CompilerParams(
            collective_id=0, has_side_effects=True, vmem_limit_bytes=VMEM_LIMIT
        ),
        name="gather_weights",
    )(*blocks)


def decode(number, spot, full):
    sizes = {"x": (4,), "z": (2, 2), "y": (4,)}
    at = {}
    for axis in "yzx":
        if axis in full:
            parts = []
            for size in reversed(sizes[axis]):
                parts.append(lax.rem(number, size))
                number = number // size
            at[axis] = tuple(reversed(parts))
    fixed = {"x": (spot["x"],), "z": (lax.rem(spot["z"], 2), spot["z"] // 2), "y": (spot["y"],)}
    index, inner = (), ()
    for axis in "xzy":
        index += at.get(axis, fixed[axis])
        inner += at.get(axis, ())
    return index, inner


def bundle_shape(full):
    sizes = {"x": (4,), "z": (2, 2), "y": (4,)}
    shape = ()
    for axis in "xzy":
        shape += sizes[axis] if axis in full else ()
    return shape


def scatter_kernel(*refs):
    parts = len(ORDERS)
    grads, outs = refs[:parts], refs[parts : 2 * parts]
    rest = refs[2 * parts :]
    accs, sibs = rest[:parts], rest[parts : 2 * parts]
    rest = rest[2 * parts :]
    nears = [rest[part * 3 : part * 3 + 3] for part in range(parts)]
    rest = rest[3 * parts :]
    fars = [rest[part * 3 : part * 3 + 3] for part in range(parts)]
    local_sem, sib_send, sib_recv, send_sem, recv_sem = rest[3 * parts :]
    me = place()
    core = me["c"]
    greet_torus(me)
    other = device_at(sibling(me))
    sends = []

    def remote(src, dst, send, recv, device):
        copy = pltpu.make_async_remote_copy(
            src, dst, send, recv, device_id=device, device_id_type=MESH
        )
        copy.start()
        sends.append(copy)
        return copy

    def add(part, spot, full, sources):
        acc = accs[part]
        count = math.prod(bundle_shape(full))

        def one(number, carry):
            index, inner = decode(number, spot, full)
            for first, rows, terms in sources:
                here = index + (pl.ds(first, rows),)
                total = acc[here].astype(F32)
                for ref, lead, base in terms:
                    place_in = index if lead is None else (lead,) + inner
                    total += ref[place_in + (pl.ds(base, rows),)].astype(F32)
                acc[here] = total.astype(acc.dtype)
            return carry

        lax.fori_loop(0, count, one, 0)

    distances = (2, 1, -1, 0)
    arrive = {}
    for slot, by in enumerate(distances):
        for part in range(parts):
            axis, full = ORDERS[part][2], "".join(ORDERS[part][:2])
            spot = shifted(me, axis, by)
            local = pltpu.make_async_copy(
                view(grads[part], spot, full, core),
                view(accs[part], spot, full),
                local_sem.at[part, slot],
            )
            local.start()
            share = remote(
                view(grads[part], spot, full, 1 - core),
                view(sibs[part], spot, full),
                sib_send.at[part, slot],
                sib_recv.at[part, slot],
                other,
            )
            arrive[part, slot] = (local, share)
    for phase in (2, 1, 0):
        copies = {}
        for slot, by in enumerate(distances):
            for part in range(parts):
                acc, near, far = accs[part], nears[part][phase], fars[part][phase]
                axis, full = ORDERS[part][phase], "".join(ORDERS[part][:phase])
                rows = acc.shape[-2]
                half = rows // 2
                spot = shifted(me, axis, by)
                first, second = [], []
                if phase == 2:
                    local, share = arrive[part, slot]
                    local.wait()
                    share.wait_recv()
                    first.append((sibs[part], None, 0))
                    second.append((sibs[part], None, half))
                if by == 1:
                    copies[part, 0].wait_recv()
                    first.append((far, 0, 0))
                if by == -1:
                    copies[part, 1].wait_recv()
                    second.append((far, 1, 0))
                if by == 0:
                    for way in range(2):
                        copies[part, 2 + way].wait_recv()
                        first.append((near, way, 0))
                        second.append((near, way, half))
                if phase == 0 and by == 0:
                    index, _ = decode(0, me, "")
                    outs[part][...] = (
                        acc[index].astype(F32) + near[0].astype(F32) + near[1].astype(F32)
                    )
                    continue
                sources = [
                    entry for entry in ((0, half, first), (half, half, second)) if entry[2]
                ]
                if sources:
                    add(part, spot, full, sources)
                if by == 2:
                    for way, step in enumerate((1, -1)):
                        copies[part, way] = remote(
                            view(acc, spot, full, None, pl.ds(way * half, half)),
                            far.at[way],
                            send_sem.at[part, phase, way],
                            recv_sem.at[part, phase, way],
                            device_at(shifted(me, axis, step)),
                        )
                if by in (1, -1):
                    way = 0 if by == 1 else 1
                    copies[part, 2 + way] = remote(
                        view(acc, spot, full),
                        near.at[way],
                        send_sem.at[part, phase, 2 + way],
                        recv_sem.at[part, phase, 2 + way],
                        device_at(shifted(me, axis, by)),
                    )
    for copy in sends:
        copy.wait_send()


def scatter_gradients(grads):
    parts = len(grads)
    blocks = [grad.shape[5:] for grad in grads]
    kinds = [grad.dtype for grad in grads]
    scratch = [pltpu.VMEM((4, 2, 2, 4) + b, k) for _ in range(2) for b, k in zip(blocks, kinds)]
    for pieces in (1, 2):
        for part in range(parts):
            rows, columns = blocks[part]
            for phase in range(3):
                lead = (2,) + bundle_shape(ORDERS[part][:phase])
                scratch.append(pltpu.VMEM(lead + (rows // pieces, columns), kinds[part]))
    return pl.pallas_call(
        scatter_kernel,
        out_shape=[jax.ShapeDtypeStruct(block, F32) for block in blocks],
        in_specs=[pl.BlockSpec(memory_space=pl.ANY)] * parts,
        out_specs=[pl.BlockSpec(memory_space=pltpu.VMEM)] * parts,
        scratch_shapes=scratch
        + [
            pltpu.SemaphoreType.DMA((parts, 4)),
            pltpu.SemaphoreType.DMA((parts, 4)),
            pltpu.SemaphoreType.DMA((parts, 4)),
            pltpu.SemaphoreType.DMA((parts, 3, 4)),
            pltpu.SemaphoreType.DMA((parts, 3, 4)),
        ],
        compiler_params=pltpu.CompilerParams(
            collective_id=1, has_side_effects=True, vmem_limit_bytes=VMEM_LIMIT
        ),
        name="scatter_gradients",
    )(*grads)


def exchange_kernel(in_ref, out_ref, local_sem, send_sem, recv_sem):
    f, t = lax.axis_index("fsdp"), lax.axis_index("tp")
    greet([(f, lax.rem(t + step, 8)) for step in range(1, 8)])
    own = pltpu.make_async_copy(in_ref.at[t], out_ref.at[t], local_sem)
    copies = []
    for step in (4, 5, 3, 7, 1, 6, 2):
        target = lax.rem(t + step, 8)
        copy = pltpu.make_async_remote_copy(
            in_ref.at[target],
            out_ref.at[t],
            send_sem.at[step],
            recv_sem.at[step],
            device_id=(f, target),
            device_id_type=MESH,
        )
        copy.start()
        copies.append(copy)
    own.start()
    own.wait()
    for copy in copies:
        copy.wait()


def exchange(slabs, collective_id):
    return pl.pallas_call(
        exchange_kernel,
        out_shape=jax.ShapeDtypeStruct(slabs.shape, slabs.dtype),
        in_specs=[pl.BlockSpec(memory_space=pl.ANY)],
        out_specs=pl.BlockSpec(memory_space=pl.ANY),
        scratch_shapes=[
            pltpu.SemaphoreType.DMA,
            pltpu.SemaphoreType.DMA((8,)),
            pltpu.SemaphoreType.DMA((8,)),
        ],
        compiler_params=pltpu.CompilerParams(
            collective_id=collective_id, has_side_effects=True
        ),
        name="exchange_%d" % slabs.shape[-1],
    )(slabs)


NN = (((1,), (0,)), ((), ()))
NT = (((1,), (1,)), ((), ()))
TN = (((0,), (0,)), ((), ()))


def mm(a, b, dims=NN):
    return lax.dot_general(a, b, dims, preferred_element_type=F32)


def plain(kernel, name, grid, in_specs, out_specs, out_shape, scratch=()):
    return pl.pallas_call(
        kernel,
        grid=grid,
        in_specs=in_specs,
        out_specs=out_specs,
        out_shape=out_shape,
        scratch_shapes=list(scratch),
        compiler_params=pltpu.CompilerParams(vmem_limit_bytes=VMEM_LIMIT),
        name=name,
    )


def project_kernel(rows_ref, weight_ref, bias_ref, out_ref):
    out_ref[0] = (mm(rows_ref[...], weight_ref[0]) + bias_ref[0]).astype(BF16)


def project(rows, weights, bias):
    count, width = rows.shape
    return plain(
        project_kernel,
        "project",
        (8,),
        [
            pl.BlockSpec((count, width), lambda t: (0, 0)),
            pl.BlockSpec((1, width, 384), lambda t: (t, 0, 0)),
            pl.BlockSpec((1, 1, 384), lambda t: (t, 0, 0)),
        ],
        pl.BlockSpec((1, count, 384), lambda t: (t, 0, 0)),
        jax.ShapeDtypeStruct((8, count, 384), BF16),
    )(rows, weights, bias)


SCALE = 1.0 / math.sqrt(HD)


def softmax_columns(key_rows, queries):
    scores = mm(key_rows, queries, NT)
    shifted_scores = scores - jnp.max(scores, 0, keepdims=True)
    powers = jnp.exp(shifted_scores * SCALE)
    return powers * (1.0 / jnp.sum(powers, 0, keepdims=True))


def attend_kernel(qkv_ref, out_ref):
    queries, key_rows, value_rows = (qkv_ref[0, :, 128 * i : 128 * i + 128] for i in range(3))
    lane = lax.broadcasted_iota(jnp.int32, (1, 128), 1)
    halves = []
    for head in range(2):
        mine = jnp.where(lane // HD == head, 1.0, 0.0).astype(BF16)
        probs = softmax_columns(key_rows, queries * mine).astype(BF16)
        halves.append(mm(probs, value_rows, TN))
    out_ref[0] = jnp.where(lane < HD, halves[0], halves[1]).astype(BF16)


def attend(qkv):
    images, seq, _ = qkv.shape
    return plain(
        attend_kernel,
        "attend",
        (images,),
        [pl.BlockSpec((1, seq, 384), lambda m: (m, 0, 0))],
        pl.BlockSpec((1, seq, 128), lambda m: (m, 0, 0)),
        jax.ShapeDtypeStruct((images, seq, 128), BF16),
    )(qkv)


def attend_back_kernel(qkv_ref, grad_ref, out_ref):
    queries, key_rows, value_rows = (qkv_ref[0, :, 128 * i : 128 * i + 128] for i in range(3))
    grads = grad_ref[0]
    lane = lax.broadcasted_iota(jnp.int32, (1, 128), 1)
    results = []
    for head in range(2):
        mine = jnp.where(lane // HD == head, 1.0, 0.0).astype(BF16)
        own_queries, own_grads = queries * mine, grads * mine
        probs = softmax_columns(key_rows, own_queries)
        d_probs = mm(value_rows, own_grads, NT)
        inner = jnp.sum(probs * d_probs, 0, keepdims=True)
        d_scores = (probs * (d_probs - inner)).astype(BF16)
        results.append(
            (
                mm(d_scores, key_rows, TN) * SCALE,
                mm(d_scores, queries) * SCALE,
                mm(probs.astype(BF16), grads),
            )
        )
    for i in range(3):
        out_ref[0, :, 128 * i : 128 * i + 128] = jnp.where(
            lane < HD, results[0][i], results[1][i]
        ).astype(BF16)


def attend_back(qkv, grads):
    images, seq, _ = qkv.shape
    return plain(
        attend_back_kernel,
        "attend_back",
        (images,),
        [
            pl.BlockSpec((1, seq, 384), lambda m: (m, 0, 0)),
            pl.BlockSpec((1, seq, 128), lambda m: (m, 0, 0)),
        ],
        pl.BlockSpec((1, seq, 384), lambda m: (m, 0, 0)),
        jax.ShapeDtypeStruct((images, seq, 384), BF16),
    )(qkv, grads)


def feed_forward_kernel(
    rows_ref,
    grads_ref,
    rows_t_ref,
    grads_t_ref,
    up_ref,
    down_ref,
    bias_ref,
    out_ref,
    back_ref,
    grad_up_ref,
    grad_down_ref,
    grad_bias_ref,
):
    step = pl.program_id(0)
    up_weight, down_weight = up_ref[0], down_ref[0]
    up_proj = mm(rows_ref[...], up_weight) + bias_ref[0]
    gate = jax.nn.sigmoid(1.702 * up_proj)
    activated = (up_proj * gate).astype(BF16)
    d_act = mm(grads_ref[...], down_weight)
    d_up_wide = d_act * (gate + 1.702 * up_proj * gate * (1.0 - gate))
    d_up = d_up_wide.astype(BF16)
    grad_bias_ref[0] = jnp.sum(d_up.astype(F32), 0, keepdims=True)
    forward = mm(activated, down_weight, NT)
    backward = mm(d_up, up_weight, NT)

    @pl.when(step == 0)
    def _():
        out_ref[...] = forward
        back_ref[...] = backward

    @pl.when(step > 0)
    def _():
        out_ref[...] += forward
        back_ref[...] += backward

    grad_up_ref[0] = mm(rows_t_ref[...], d_up).astype(BF16)
    grad_down_ref[0] = mm(grads_t_ref[...], activated).astype(BF16)


def feed_forward(rows, grads, up_weights, down_weights, bias):
    count, width = rows.shape
    hidden = up_weights.shape[2]
    whole = pl.BlockSpec((count, width), lambda t: (0, 0))
    turned = pl.BlockSpec((width, count), lambda t: (0, 0))
    slab = pl.BlockSpec((1, width, hidden), lambda t: (t, 0, 0))
    line = pl.BlockSpec((1, 1, hidden), lambda t: (t, 0, 0))
    return plain(
        feed_forward_kernel,
        "feed_forward",
        (8,),
        [whole, whole, turned, turned, slab, slab, line],
        [whole, whole, slab, slab, line],
        [
            jax.ShapeDtypeStruct((count, width), F32),
            jax.ShapeDtypeStruct((count, width), F32),
            jax.ShapeDtypeStruct((8, width, hidden), BF16),
            jax.ShapeDtypeStruct((8, width, hidden), BF16),
            jax.ShapeDtypeStruct((8, 1, hidden), F32),
        ],
    )(rows, grads, rows.T, grads.T, up_weights, down_weights, bias)


def project_back_kernel(
    grads_ref, attended_ref, weight_ref, rows_t_ref, middle_t_ref, back_ref, grad_ref
):
    step = pl.program_id(0)
    grads = grads_ref[0]
    backward = mm(grads, weight_ref[0], NT)

    @pl.when(step == 0)
    def _():
        back_ref[...] = backward

    @pl.when(step > 0)
    def _():
        back_ref[...] += backward

    grad_ref[0, :, :384] = mm(rows_t_ref[...], grads).astype(BF16)
    grad_ref[0, :, 384:] = mm(middle_t_ref[...], attended_ref[0]).astype(BF16)


def project_back(grads, attended, weights, rows, middle):
    count, width = rows.shape
    turned = pl.BlockSpec((width, count), lambda t: (0, 0))
    return plain(
        project_back_kernel,
        "project_back",
        (8,),
        [
            pl.BlockSpec((1, count, 384), lambda t: (t, 0, 0)),
            pl.BlockSpec((1, count, 128), lambda t: (t, 0, 0)),
            pl.BlockSpec((1, width, 384), lambda t: (t, 0, 0)),
            turned,
            turned,
        ],
        [
            pl.BlockSpec((count, width), lambda t: (0, 0)),
            pl.BlockSpec((1, width, 512), lambda t: (t, 0, 0)),
        ],
        [
            jax.ShapeDtypeStruct((count, width), F32),
            jax.ShapeDtypeStruct((8, width, 512), BF16),
        ],
    )(grads, attended, weights, rows.T, middle.T)


def norm_stats(values):
    average = jnp.mean(values, -1, keepdims=True)
    centered = values - average
    inverse = lax.rsqrt(jnp.mean(centered * centered, -1, keepdims=True) + EPSILON)
    return (centered * inverse, inverse)


def norm_back(upstream, normed, inverse, gain_vector):
    scaled = upstream * gain_vector
    return inverse * (
        scaled
        - jnp.mean(scaled, -1, keepdims=True)
        - normed * jnp.mean(scaled * normed, -1, keepdims=True)
    )


def per_device(
    inputs,
    cotangent,
    valid_slots,
    ln1_gain,
    ln1_bias,
    qkv_weight,
    qv_bias,
    out_weight,
    out_bias,
    ln2_gain,
    ln2_bias,
    fc1_weight,
    fc1_bias,
    fc2_weight,
    fc2_bias,
):
    micro, _, local_seq, width = inputs.shape
    tokens = micro * local_seq
    padded = -(-tokens // 16) * 16

    def pad(rows):
        return jnp.pad(rows, ((0, padded - tokens), (0, 0)))

    attention_block = jnp.concatenate(
        [qkv_weight[0], qkv_weight[1], qkv_weight[2], out_weight.T], axis=1
    )
    small = jnp.concatenate(
        [ln1_gain, ln1_bias, out_bias, ln2_gain, ln2_bias, fc2_bias]
        + [qv_bias.reshape(-1), fc1_bias.reshape(-1)]
    )
    small = jnp.pad(small.reshape(1, 96), ((0, 15), (0, 32)))
    gathered = gather_weights((attention_block, fc1_weight, fc2_weight.T, small))
    attention_w, up_w, down_w = (entry.reshape(8, width, 512) for entry in gathered[:3])
    vectors = gathered[3].reshape(8, 16, 16, 128)[:, :, 0, :96].astype(F32)
    gain_one, bias_one, bias_out, gain_two, bias_two, bias_last = (
        vectors[:, :, :48].reshape(8, 16, 6, 8).transpose(2, 1, 0, 3).reshape(6, width)
    )
    pair_bias = vectors[:, :, 48:64].reshape(8, 16, 2, 2, 4).transpose(2, 0, 3, 1, 4)
    pair_bias = pair_bias.reshape(2, 8, 1, 128)
    hidden_bias = vectors[:, :, 64:].reshape(8, 16, 8, 4).transpose(0, 2, 1, 3).reshape(8, 1, 512)
    project_bias = jnp.concatenate(
        [pair_bias[0], jnp.zeros((8, 1, 128), F32), pair_bias[1]], axis=-1
    )

    def to_images(slabs):
        columns = slabs.shape[-1]
        rows = slabs[:, :tokens].reshape(8, micro, local_seq, columns)
        return rows.transpose(1, 0, 2, 3).reshape(micro, 8 * local_seq, columns)

    def to_slabs(images):
        columns = images.shape[-1]
        rows = images.reshape(micro, 8, local_seq, columns).transpose(1, 0, 2, 3)
        rows = rows.reshape(8, tokens, columns)
        return jnp.pad(rows, ((0, 0), (0, padded - tokens), (0, 0)))

    block_rows = inputs.reshape(tokens, width).astype(F32)
    normed_one, inverse_one = norm_stats(block_rows)
    low_one = pad((normed_one * gain_one + bias_one).astype(BF16))
    qkv = to_images(exchange(project(low_one, attention_w, project_bias), 2))
    attended = exchange(to_slabs(attend(qkv)), 3)
    out_w = attention_w[:, :, 384:]
    branch = jnp.einsum("tnc,tdc->nd", attended, out_w, preferred_element_type=F32)[:tokens]
    middle = block_rows + branch + bias_out
    normed_two, inverse_two = norm_stats(middle)
    low_two = pad((normed_two * gain_two + bias_two).astype(BF16))
    slot_weight = valid_slots.astype(F32).reshape(micro, 1, 1)
    upstream = (cotangent.reshape(micro, local_seq, width).astype(F32) * slot_weight).reshape(
        tokens, width
    )
    upstream_low = pad(upstream.astype(BF16))
    mlp_out, d_norm_two, grad_up, grad_down, grad_hidden = feed_forward(
        low_two, upstream_low, up_w, down_w, hidden_bias
    )
    mlp_out, d_norm_two = mlp_out[:tokens], d_norm_two[:tokens]
    result = (middle + mlp_out + bias_last).astype(BF16)
    d_middle = upstream + norm_back(d_norm_two, normed_two, inverse_two, gain_two)
    middle_low = pad(d_middle.astype(BF16))
    d_attended = jnp.einsum("nd,tdc->tnc", middle_low, out_w, preferred_element_type=F32)
    d_attended = to_images(exchange(d_attended.astype(BF16), 3))
    d_project = exchange(to_slabs(attend_back(qkv, d_attended)), 2)
    d_norm_one, grad_attention = project_back(
        d_project, attended, attention_w, low_one, middle_low
    )
    d_norm_one = d_norm_one[:tokens]
    grad_rows = d_middle + norm_back(d_norm_one, normed_one, inverse_one, gain_one)
    pair_sums = jnp.sum(d_project.astype(F32), 1)
    pair_sums = jnp.stack([pair_sums[:, :128], pair_sums[:, 256:]])
    vector_sums = jnp.stack(
        [
            jnp.sum(d_norm_one * normed_one, 0),
            jnp.sum(d_norm_one, 0),
            jnp.sum(d_middle, 0),
            jnp.sum(d_norm_two * normed_two, 0),
            jnp.sum(d_norm_two, 0),
            jnp.sum(upstream, 0),
        ]
    )
    small_grads = jnp.concatenate(
        [
            vector_sums.reshape(6, 16, 8, 8).transpose(2, 1, 0, 3).reshape(8, 16, 48),
            pair_sums.reshape(2, 8, 2, 16, 4).transpose(1, 3, 0, 2, 4).reshape(8, 16, 16),
            grad_hidden.reshape(8, 8, 16, 4).transpose(0, 2, 1, 3).reshape(8, 16, 32),
        ],
        axis=-1,
    )
    small_grads = jnp.pad(small_grads[:, :, None], ((0, 0), (0, 0), (0, 15), (0, 32)))
    lead = (4, 2, 2, 4, 2)
    sums = scatter_gradients(
        (
            grad_attention.reshape(lead + (64, 512)),
            grad_up.reshape(lead + (64, 512)),
            grad_down.reshape(lead + (64, 512)),
            small_grads.reshape(lead + (16, 128)),
        )
    )
    own_attention, own_up, own_down, own_small = sums
    own_small = own_small[0]
    vector_grads = own_small[:48].reshape(6, 8)
    return (
        result.reshape(inputs.shape),
        grad_rows.astype(BF16).reshape(inputs.shape),
        vector_grads[0],
        vector_grads[1],
        jnp.stack([own_attention[:, 128 * i : 128 * i + 128] for i in range(3)]),
        own_small[48:64].reshape(2, 2, 4),
        own_attention[:, 384:].T,
        vector_grads[2],
        vector_grads[3],
        vector_grads[4],
        own_up,
        own_small[64:96].reshape(8, 4),
        own_down.T,
        vector_grads[5],
    )


def solution(mesh):
    in_specs = (
        P(None, "fsdp", "tp", None),
        P(None, "fsdp", "tp", None),
        P(None, "fsdp"),
        P(("fsdp", "tp")),
        P(("fsdp", "tp")),
        P(None, "fsdp", "tp"),
        P(None, "tp", "fsdp"),
        P("tp", "fsdp"),
        P(("fsdp", "tp")),
        P(("fsdp", "tp")),
        P(("fsdp", "tp")),
        P("fsdp", "tp"),
        P("tp", "fsdp"),
        P("tp", "fsdp"),
        P(("fsdp", "tp")),
    )
    out_specs = (
        P(None, "fsdp", "tp", None),
        P(None, "fsdp", "tp", None),
        P(("fsdp", "tp")),
        P(("fsdp", "tp")),
        P(None, "fsdp", "tp"),
        P(None, "tp", "fsdp"),
        P("tp", "fsdp"),
        P(("fsdp", "tp")),
        P(("fsdp", "tp")),
        P(("fsdp", "tp")),
        P("fsdp", "tp"),
        P("tp", "fsdp"),
        P("tp", "fsdp"),
        P(("fsdp", "tp")),
    )
    return jax.shard_map(
        per_device, mesh=mesh, in_specs=in_specs, out_specs=out_specs, check_vma=False
    )
```

time: 1870 us -> 370 us (0.20)
  waiting for transfers between devices: 1350 us -> 0 us
  Pallas kernels: 0 us -> 275 us
  blocking collectives: 259 us -> 0 us
  matrix products: 127 us -> 5.52 us
  other arithmetic: 40.3 us -> 16.9 us
  between operations: 21 us -> 1.21 us
    reduce_scatter x21 -> x0, waiting for transfers between devices: 940 us -> none  [the longest x3 208 us: per_device(): lax.psum_scatter(grad_fc2.astype(jnp.bfloat16), 'fsdp', scatter_dimension...]
    all_gather x14 -> x0, waiting for transfers between devices: 330 us -> none  [the longest x3 112 us: per_device(): lax.all_gather(upstream_low, 'tp', axis=1, tiled=True)]
    pallas_call x0 -> x11, Pallas kernels: none -> 275 us  [the longest x1 76.9 us: gather_weights(): pl.pallas_call(gather_kernel, out_shape=[jax.ShapeDtypeStruct((4, 2, 2, 4...]
    unnamed x3 -> x0, blocking collectives: 169 us -> none
    dot_general x54 -> x2, matrix products: 127 us -> 5.52 us  [the longest x1 3.04 us: per_device(): jnp.einsum('nd,tdc->tnc', middle_low, out_w, preferred_element_type=F32)]
    all_gather x4 -> x0, blocking collectives: 90.2 us -> none  [the longest x1 24.2 us: per_device(): lax.all_gather(fc1_bias, 'fsdp', axis=1, tiled=True)]
    unnamed x37 -> x0, waiting for transfers between devices: 83.7 us -> none
  transfers between devices with their start and end apart: 36 -> 0, of which waited for: 31 -> 0; matrix products, arithmetic and copies ran while one was open for 10% -> 0% of each run, Pallas kernels for 0% -> 0%
where the time goes in v1:
time: 370 us; the launch traced here: 368 us
  Pallas kernels  275 us (74%)
  local copies, waits for them, and re-layouts  68.6 us (19%)
  other arithmetic  16.9 us (5%)
  matrix products  5.52 us (1%)
    pallas_call x1, Pallas kernels, gather_weights(): pl.pallas_call(gather_kernel, out_shape=[jax.ShapeDtypeStruct((4, 2, 2, 4...  76.9 us
    pallas_call x1, Pallas kernels, scatter_gradients(): pl.pallas_call(scatter_kernel, out_shape=[jax.ShapeDtypeStruct(block, F32...  74.7 us
    pallas_call x4, Pallas kernels, exchange(): pl.pallas_call(exchange_kernel, out_shape=jax.ShapeDtypeStruct(slabs.shap...  61.7 us
    pallas_call x1, Pallas kernels, feed_forward(): plain(feed_forward_kernel, 'feed_forward', (8,), [whole, whole, turned, t...  21.9 us
    pallas_call x1, Pallas kernels, project_back(): plain(project_back_kernel, 'project_back', (8,), [pl.BlockSpec((1, count,...  13 us
    unnamed x63, local copies, waits for them, and re-layouts  12.2 us
    pallas_call x1, Pallas kernels, attend_back(): plain(attend_back_kernel, 'attend_back', (images,), [pl.BlockSpec((1, seq...  11.8 us
    pallas_call x1, Pallas kernels, project(): plain(project_kernel, 'project', (8,), [pl.BlockSpec((count, width), lamb...  7.97 us

profile of v1, /device:TPU:0, one launch (start us, length us, event | category | flops | bytes accessed | tf_op | source)
XLA Modules:
  0.0 367.7 jit_solution(5797453213298933995)
XLA Ops:
  0.7 0.8 slice_bitcast_fusion.7
  1.5 1.4 pad_maximum_fusion.1.refs_0_
  2.8 0.8 copy.95
  3.7 0.8 reshape.260
  4.4 4.1 %concatenate.15 = bf16[96]{0:T(256)(128)(2,1)S(1)} concatenate(bf16[8]{0:T(256)(128)(2,1)} %param.18, bf16[8]{0:T(256)(128)(2,1)} %param.19, bf16[8]{0:T(256)(128)(2,1)} %param.23, bf16[8]{0:T(256)(128)(2,1)} %param.24, bf16[8]{0:T(256)(128)(2,1)} %param.25, bf16[8]{0:T(256)(128)(2,1)} %param.29, bf16[16]{0:T(256)(128)(2,1)S(1)} %reshape.260, bf16[32]{0:T(256)(128)(2,1)S(1)} %reshape.261), dimensions={0} | concatenate | bytes 384 | tf_op jit(solution)/shard_map/concatenate | solution.py:659
  9.1 76.9 %gather_weights.1 = (bf16[4,2,2,4,2,64,512]{6,5,4,3,2,1,0:T(8,128)(2,1)}, bf16[4,2,2,4,2,64,512]{6,5,4,3,2,1,0:T(8,128)(2,1)}, bf16[4,2,2,4,2,64,512]{6,5,4,3,2,...) custom-call(bf16[64,512]{1,0:T(8,128)(2,1)} %pad_maximum_fusion.1.refs_0_, bf16[64,512]{1,0:T(8,128)(2,1)} %refs_1_.1, ...), custom_call_target="tpu_custom_call" | custom-call | tf_op jit(solution)/shard_map/gather_weights/pallas_call | solution.py:154
  86.1 1.0 slice.148
  89.9 0.8 pad.30.clone.rows_ref
  91.8 8.0 %project.1.in_ref = bf16[8,224,384]{2,1,0:T(8,128)(2,1)} custom-call(bf16[224,1024]{1,0:T(8,128)(2,1)} %pad.30.clone.rows_ref, bf16[8,1024,512]{2,1,0:T(8,128)(2,1)} %bitcast.132, f32[8,1,384]{2,1,0:T(1,128)} %pad_maximum_fusion.3.bias_ref), custom_call_target="tpu_custom_call" | custom-call | tf_op jit(solution)/shard_map/project/pallas_call | solution.py:422
  99.7 21.4 %exchange_384.2 = bf16[8,224,384]{2,1,0:T(8,128)(2,1)} custom-call(bf16[8,224,384]{2,1,0:T(8,128)(2,1)} %project.1.in_ref), custom_call_target="tpu_custom_call" | custom-call | tf_op jit(solution)/shard_map/exchange_384/pallas_call | solution.py:377
  121.1 1.3 slice-done
  122.4 1.2 copy.105
  123.6 7.4 %attend.1 = bf16[3,576,128]{2,1,0:T(8,128)(2,1)} custom-call(bf16[3,576,384]{2,1,0:T(8,128)(2,1)} %bitcast.136), custom_call_target="tpu_custom_call" | custom-call | tf_op jit(solution)/shard_map/attend/pallas_call | solution.py:459
  131.0 1.0 copy.106
  132.1 0.8 pad.31.in_ref
  132.9 10.3 %exchange_128.2.attended_ref = bf16[8,224,128]{2,1,0:T(8,128)(2,1)} custom-call(bf16[8,224,128]{2,1,0:T(8,128)(2,1)} %pad.31.in_ref), custom_call_target="tpu_custom_call" | custom-call | tf_op jit(solution)/shard_map/exchange_128/pallas_call | solution.py:377
  143.2 2.5 fusion.4
  146.4 0.8 copy.110
  147.3 0.8 copy.111
  148.2 1.2 add_convert_fusion.1
  150.2 1.1 bitcast_convert_fusion
  151.2 1.5 copy.113
  152.7 0.8 multiply_convert_fusion
  153.5 0.8 copy-done.7
  154.3 2.2 pad_bitcast_fusion.1
  156.5 2.0 copy.148
  158.5 1.8 pad.32.clone.rows_ref
  161.3 2.0 copy.149
  163.3 1.8 pad.33.clone.grads_ref
  165.2 21.9 %feed_forward.1 = (f32[224,1024]{1,0:T(8,128)}, f32[224,1024]{1,0:T(8,128)}, bf16[8,1024,512]{2,1,0:T(8,128)(2,1)}, bf16[8,1024,512]{2,1,0:T(8,128)(2,1)}, f32[8,1,512]{2,1,0:T(1,128)}) custom-call(bf16[224,1024]{1,0:T(8,128)(2,1)} %pad.32.clone.rows_ref, bf16[224,1024]{1,0:T(8,128)(2,1)} %pad.33.clone.grads_ref, ...), custom_call_target="tpu_custom_call" | custom-call | tf_op jit(solution)/shard_map/feed_forward/pallas_call | solution.py:556
  187.1 2.6 copy.122
  189.7 2.4 multiply_reduce_fusion
  192.1 2.5 copy.119
  194.8 3.5 fusion.22
  198.3 1.0 copy-done.1
  199.4 3.0 fusion.10.in_ref
  202.4 9.1 %exchange_128.3 = bf16[8,224,128]{2,1,0:T(8,128)(2,1)} custom-call(bf16[8,224,128]{2,1,0:T(8,128)(2,1)} %fusion.10.in_ref), custom_call_target="tpu_custom_call" | custom-call | tf_op jit(solution)/shard_map/exchange_128/pallas_call | solution.py:377
  211.5 1.0 slice.132
  212.6 0.8 copy.124
  213.4 11.8 %attend_back.1 = bf16[3,576,384]{2,1,0:T(8,128)(2,1)} custom-call(bf16[3,576,384]{2,1,0:T(8,128)(2,1)} %bitcast.137, bf16[3,576,128]{2,1,0:T(8,128)(2,1)} %bitcast.150), custom_call_target="tpu_custom_call" | custom-call | tf_op jit(solution)/shard_map/attend_back/pallas_call | solution.py:496
  225.2 1.5 copy.125
  226.6 1.3 pad.35.in_ref
  227.9 21.0 %exchange_384.3.grads_ref = bf16[8,224,384]{2,1,0:T(8,128)(2,1)} custom-call(bf16[8,224,384]{2,1,0:T(8,128)(2,1)} %pad.35.in_ref), custom_call_target="tpu_custom_call" | custom-call | tf_op jit(solution)/shard_map/exchange_384/pallas_call | solution.py:377
  248.9 0.9 pad_bitcast_fusion.middle_t_ref
  249.8 0.9 pad_bitcast_fusion.3.rows_t_ref
  250.7 13.0 %project_back.1 = (f32[224,1024]{1,0:T(8,128)}, bf16[8,1024,512]{2,1,0:T(8,128)(2,1)}) custom-call(bf16[8,224,384]{2,1,0:T(8,128)(2,1)} %exchange_384.3.grads_ref, bf16[8,224,128]{2,1,0:T(8,128)(2,1)} %exchange_128.2.attended_ref, bf16[8,1024,512]{2,1,0:T(8,128)(2,1)} %bitcast.135, bf16[1024,224]{1,0:T(8,128)(2,1)} %pad_bitcast_fusion.3.rows_t_ref, ...), custom_call_target="tpu_custom_call" | custom-call | tf_op jit(solution)/shard_map/project_back/pallas_call | solution.py:594
  263.8 1.5 copy.126
  265.3 1.2 multiply_reduce_fusion.1
  266.6 0.8 stack.42
  268.0 0.8 stack.43
  269.4 0.8 stack.44
  270.8 0.8 stack.45
  272.9 1.2 multiply_reduce_fusion.5
  274.9 1.9 copy.128
  276.7 1.0 copy.134
  278.9 1.1 pad.36.clone
  280.0 74.7 %scatter_gradients.1 = (f32[64,512]{1,0:T(8,128)}, f32[64,512]{1,0:T(8,128)}, f32[64,512]{1,0:T(8,128)}, f32[16,128]{1,0:T(8,128)}) custom-call(bf16[4,2,2,4,2,64,512]{6,5,4,3,2,1,0:T(8,128)(2,1)} %bitcast.140, bf16[4,2,2,4,2,64,512]{6,5,4,3,2,1,0:T(8,128)(2,1)} %bitcast.138, bf16[4,2,2,4,2,64,512]{6,5,4,3,2,1,0:T(8,128)(2,1)} %bitcast.139, ...), custom_call_target="tpu_custom_call" | custom-call | tf_op jit(solution)/shard_map/scatter_gradients/pallas_call | solution.py:333
  354.7 1.4 slice_bitcast_fusion.1
  356.8 0.8 slice_reduce_fusion.2
  358.3 1.5 slice_bitcast_fusion.8
  359.8 0.8 slice_reduce_fusion.3
  361.3 1.1 add_convert_fusion
  362.4 2.0 copy.127
  364.4 2.0 copy.121
  (126 shorter events, 15.7 us)
Async XLA Ops:
  0.6 87.6 %copy-start.8 = (bf16[3,1,72,1024]{3,2,1,0:T(8,128)(2,1)S(1)}, bf16[3,1,72,1024]{3,2,1,0:T(8,128)(2,1)}, u32[]{:S(2)}) copy-start(bf16[3,1,72,1024]{3,2,1,0:T(8,128)(2,1)} %param.15) | copy-start | bytes 1327108
  89.3 1.8 copy-start.14
  89.7 10.0 %copy-start.5 = (bf16[216,1024]{0,1:T(8,128)(2,1)}, bf16[216,1024]{0,1:T(8,128)(2,1)S(1)}, u32[]{:S(2)}) copy-start(bf16[216,1024]{0,1:T(8,128)(2,1)S(1)} %add_convert_fusion.2) | copy-start | bytes 1327108
  121.1 1.3 slice-start
  143.2 2.5 copy-start.11
  146.1 3.3 copy-start.24
  146.1 4.0 %copy-start.9 = (bf16[3,1,72,1024]{3,2,1,0:T(8,128)(2,1)S(1)}, bf16[3,1,72,1024]{3,2,1,0:T(8,128)(2,1)}, u32[]{:S(2)}) copy-start(bf16[3,1,72,1024]{3,2,1,0:T(8,128)(2,1)} %param.16) | copy-start | bytes 1327108
  146.3 4.9 %copy-start.16 = (f32[216]{0:T(256)}, f32[216]{0:T(256)S(1)}, u32[]{:S(2)}) copy-start(f32[216]{0:T(256)S(1)} %add_rsqrt_fusion.1) | copy-start | bytes 2596
  149.4 1.8 copy-start.23
  153.5 0.8 copy-start.7
  165.2 24.5 %copy-start.17 = (f32[216]{0:T(256)S(1)}, f32[216]{0:T(256)}, u32[]{:S(2)}) copy-start(f32[216]{0:T(256)} %copy-done.16) | copy-start | bytes 2596
  189.7 4.9 %copy-start.10 = (f32[1,16,8,8]{1,3,0,2:T(8,128)S(1)}, f32[1,16,8,8]{1,3,0,2:T(8,128)}, u32[]{:S(2)}) copy-start(f32[1,16,8,8]{1,3,0,2:T(8,128)} %get-tuple-element.99) | copy-start | bytes 12292
  189.7 5.1 %copy-start.20 = (f32[216]{0:T(256)S(1)}, f32[216]{0:T(256)}, u32[]{:S(2)}) copy-start(f32[216]{0:T(256)} %mul.129) | copy-start | bytes 2596
  198.3 1.0 copy-start.1
  227.9 21.9 %copy-start.6 = (bf16[216,1024]{0,1:T(8,128)(2,1)S(1)}, bf16[216,1024]{0,1:T(8,128)(2,1)}, u32[]{:S(2)}) copy-start(bf16[216,1024]{0,1:T(8,128)(2,1)} %copy-done.5) | copy-start | bytes 1327108
  250.7 14.6 %copy-start.15 = (f32[216]{0:T(256)S(1)}, f32[216]{0:T(256)}, u32[]{:S(2)}) copy-start(f32[216]{0:T(256)} %copy-done.14) | copy-start | bytes 2596
  263.8 8.4 %copy-start.18 = (f32[1024]{0:T(1024)S(1)}, f32[1024]{0:T(1024)}, u32[]{:S(2)}) copy-start(f32[1024]{0:T(1024)} %get-tuple-element.92) | copy-start | bytes 12292
  265.3 11.4 %copy-start.3 = (f32[224,1024]{0,1:T(8,128)}, f32[224,1024]{0,1:T(8,128)S(1)}, u32[]{:S(2)}) copy-start(f32[224,1024]{0,1:T(8,128)S(1)} %copy.126) | copy-start | bytes 2752516
  265.3 12.4 %copy-start = (bf16[8,224,384]{2,1,0:T(8,128)(2,1)S(1)}, bf16[8,224,384]{2,1,0:T(8,128)(2,1)}, u32[]{:S(2)}) copy-start(bf16[8,224,384]{2,1,0:T(8,128)(2,1)} %exchange_384.3.grads_ref) | copy-start | bytes 4128772
  274.9 3.5 copy-start.19
  280.0 81.3 %copy-start.22 = (f32[216]{0:T(256)S(1)}, f32[216]{0:T(256)}, u32[]{:S(2)}) copy-start(f32[216]{0:T(256)} %get-tuple-element.89) | copy-start | bytes 2596
  280.0 81.3 %copy-start.21 = (f32[216]{0:T(256)S(1)}, f32[216]{0:T(256)}, u32[]{:S(2)}) copy-start(f32[216]{0:T(256)} %get-tuple-element.90) | copy-start | bytes 2596
  280.0 81.3 %copy-start.2 = (f32[216,1024]{0,1:T(8,128)S(1)}, f32[216,1024]{0,1:T(8,128)}, u32[]{:S(2)}) copy-start(f32[216,1024]{0,1:T(8,128)} %copy-done.1) | copy-start | bytes 2654212
  280.0 81.3 %copy-start.4 = (f32[224,1024]{0,1:T(8,128)S(1)}, f32[224,1024]{0,1:T(8,128)}, u32[]{:S(2)}) copy-start(f32[224,1024]{0,1:T(8,128)} %copy-done.3) | copy-start | bytes 2752516
  361.3 5.1 %copy-start.13 = (f32[64,512]{1,0:T(8,128)S(1)}, f32[64,512]{1,0:T(8,128)}, u32[]{:S(2)}) copy-start(f32[64,512]{1,0:T(8,128)} %get-tuple-element.148) | copy-start | bytes 393220
  361.3 5.8 %copy-start.12 = (f32[64,512]{1,0:T(8,128)S(1)}, f32[64,512]{1,0:T(8,128)}, u32[]{:S(2)}) copy-start(f32[64,512]{1,0:T(8,128)} %get-tuple-element.43) | copy-start | bytes 393220

commit v2 on v0

v2 whole, which is shorter than its diff:
```python
import functools
import math

import jax
import jax.numpy as jnp
from jax import lax
from jax.experimental import pallas as pl
from jax.experimental.pallas import tpu as pltpu
from jax.sharding import PartitionSpec as P

MESH = pl.DeviceIdType.MESH
HD = 64
SCALE = 1.0 / math.sqrt(HD)
EPSILON = 1e-05
BF16 = jnp.bfloat16
F32 = jnp.float32
VMEM_LIMIT = 62 * 2**20
MICRO, GROUP = 3, 8
ORDERS = (("x", "y", "z"), ("y", "z", "x"), ("z", "x", "y"))
SIZES = {"x": (4,), "z": (2, 2), "y": (4,)}
LEAD = (4, 2, 2, 4, 2)
STEPS = (1, -1, 2)
NN = (((1,), (0,)), ((), ()))
NT = (((1,), (1,)), ((), ()))
TN = (((0,), (0,)), ((), ()))


def mm(a, b, dims=NN):
    return lax.dot_general(a, b, dims, preferred_element_type=F32)


def place():
    f, t = lax.axis_index("fsdp"), lax.axis_index("tp")
    return {
        "x": t // 2,
        "y": lax.rem(f // 2, 4),
        "z": (f // 8) * 2 + lax.rem(t, 2),
        "c": lax.rem(f, 2),
    }


def device_at(spot):
    return (
        (spot["z"] // 2) * 8 + spot["y"] * 2 + spot["c"],
        spot["x"] * 2 + lax.rem(spot["z"], 2),
    )


def shifted(spot, axis, by):
    return {**spot, axis: lax.rem(spot[axis] + by + 4, 4)}


def sibling(spot):
    return {**spot, "c": 1 - spot["c"]}


def greet(me):
    f, t = lax.axis_index("fsdp"), lax.axis_index("tp")
    devices = [(f, lax.rem(t + step, GROUP)) for step in range(1, GROUP)]
    devices += [device_at(shifted(me, "y", by)) for by in STEPS]
    devices += [device_at(shifted(me, "z", 2))]
    devices += [device_at(shifted(me, "z", 2 * lax.rem(me["z"], 2) - 1))]
    devices += [device_at(sibling(me))]
    barrier = pltpu.get_barrier_semaphore()
    for device in devices:
        pl.semaphore_signal(barrier, inc=1, device_id=device, device_id_type=MESH)
    pl.semaphore_wait(barrier, len(devices))


def view(ref, spot, full, core=None, rows=slice(None)):
    whole = slice(None)
    index = [
        whole if "x" in full else spot["x"],
        whole if "z" in full else lax.rem(spot["z"], 2),
        whole if "z" in full else spot["z"] // 2,
        whole if "y" in full else spot["y"],
    ]
    if core is not None:
        index.append(core)
    return ref.at[tuple(index) + (rows,)]


def decode(number, spot, full):
    at = {}
    for axis in "yzx":
        if axis in full:
            parts = []
            for size in reversed(SIZES[axis]):
                parts.append(lax.rem(number, size))
                number = number // size
            at[axis] = tuple(reversed(parts))
    fixed = {"x": (spot["x"],), "z": (lax.rem(spot["z"], 2), spot["z"] // 2), "y": (spot["y"],)}
    index, inner = (), ()
    for axis in "xzy":
        index += at.get(axis, fixed[axis])
        inner += at.get(axis, ())
    return index, inner


def bundle_shape(full):
    shape = ()
    for axis in "xzy":
        shape += SIZES[axis] if axis in full else ()
    return shape


class Copies:
    def __init__(self, send, recv):
        self.send, self.recv = send, recv
        self.made = {}

    def start(self, name, src, dst, device):
        slot = len(self.made)
        self.made[name] = pltpu.make_async_remote_copy(
            src,
            dst,
            self.send.at[slot],
            self.recv.at[slot],
            device_id=device,
            device_id_type=MESH,
        )
        self.made[name].start()

    def arrived(self, name):
        self.made[name].wait_recv()

    def sent(self):
        for copy in self.made.values():
            copy.wait_send()


class Gather:
    slots = 38

    def __init__(self, me, order, block, out, send, recv, local):
        self.me, self.order, self.block, self.out = me, order, block, out
        self.copies = Copies(send, recv)
        self.local = local
        self.core = me["c"]
        self.half = out.shape[-2] // 2

    def piece(self, spot, full, rows=slice(None)):
        return view(self.out, spot, full, self.core, rows)

    def spread(self, name, spot, full, axis, by, rows=slice(None)):
        piece = self.piece(spot, full, rows)
        target = shifted(self.me, axis, by)
        self.copies.start(name, piece, piece, device_at(target))

    def share(self, name, spot, full):
        piece = self.piece(spot, full)
        self.copies.start(name, piece, piece, device_at(sibling(self.me)))

    def own(self):
        return pltpu.make_async_copy(
            self.block, view(self.out, self.me, "", self.core), self.local
        )

    def first(self):
        me, axis = self.me, self.order[0]
        self.own().start()
        for by in STEPS:
            target = shifted(me, axis, by)
            self.copies.start(
                ("first", by), self.block, self.piece(me, ""), device_at(target)
            )

    def second(self):
        full, axis = self.order[0], self.order[1]
        self.own().wait()
        for by in STEPS:
            self.copies.arrived(("first", by))
        for by in STEPS:
            self.spread(("second", by), self.me, full, axis, by)
        self.third(0)

    def third(self, group):
        full, axis = self.order[0], self.order[2]
        spot = self.spot(group)
        if group:
            self.copies.arrived(("second", STEPS[group - 1]))
        for by in (1, -1):
            self.spread(("near", group, by), spot, full, axis, by)
        self.share(("share", group), spot, full)

    def spot(self, group):
        return self.me if group == 0 else shifted(self.me, self.order[1], -STEPS[group - 1])

    def thirds(self):
        for group in (1, 2, 3):
            self.third(group)

    def far(self, groups=(0, 1, 2, 3)):
        full, axis = self.order[0], self.order[2]
        for group in groups:
            for way, by in enumerate((1, -1)):
                spot = shifted(self.spot(group), axis, -by)
                self.copies.arrived(("near", group, by))
                rows = pl.ds(way * self.half, self.half)
                self.spread(("far", group, by), spot, full, axis, by, rows)
                self.share(("share near", group, by), spot, full)

    def last(self):
        full, axis = self.order[0], self.order[2]
        for group in range(4):
            for by in (1, -1):
                self.copies.arrived(("far", group, by))
            self.share(("share far", group), shifted(self.spot(group), axis, 2), full)

    def done(self):
        for group in range(4):
            self.copies.arrived(("share", group))
            self.copies.arrived(("share near", group, 1))
            self.copies.arrived(("share near", group, -1))
            self.copies.arrived(("share far", group))

    def sent(self):
        self.copies.sent()


class Reduce:
    slots = 14

    def __init__(self, me, order, source, acc, sib, near, far, mid, tail, out, send, recv, local):
        self.me, self.order, self.source, self.acc, self.sib = me, order, source, acc, sib
        self.nears, self.fars, self.mid, self.tail, self.out = near, far, mid, tail, out
        self.copies = Copies(send, recv)
        self.local = local
        self.core = me["c"]
        self.half = acc.shape[-2] // 2
        self.inside = source is acc
        self.full = "".join(order[:2])

    def mine(self, spot, full, rows=slice(None)):
        return view(self.acc, spot, full, self.core if self.inside else None, rows)

    def chunk(self, by):
        return shifted(self.me, self.order[2], by)

    def fetch(self, slot, by):
        spot = self.chunk(by)
        return pltpu.make_async_copy(
            view(self.source, spot, self.full, self.core),
            view(self.acc, spot, self.full),
            self.local.at[slot],
        )

    def begin(self):
        for slot, by in enumerate((2, 1, -1, 0)):
            spot = self.chunk(by)
            if not self.inside:
                self.fetch(slot, by).start()
            self.copies.start(
                ("share", by),
                view(self.source, spot, self.full, 1 - self.core),
                view(self.sib, spot, self.full),
                device_at(sibling(self.me)),
            )

    def ready(self, slot, by):
        if not self.inside:
            self.fetch(slot, by).wait()
        self.copies.arrived(("share", by))

    def add(self, spot, full, sources, out=None):
        acc = self.acc
        count = math.prod(bundle_shape(full))

        def one(number, carry):
            index, inner = decode(number, spot, full)
            spot_in = index + ((self.core,) if self.inside else ())
            for first, rows, terms in sources:
                here = spot_in + (pl.ds(first, rows),)
                total = acc[here]
                if len(terms) > 1:
                    total = total.astype(F32)
                for ref, lead, base in terms:
                    place_in = index if lead is None else (lead,) + inner
                    term = ref[place_in + (pl.ds(base, rows),)]
                    total += term.astype(total.dtype)
                acc[here] = total.astype(acc.dtype)
            return carry

        if count == 1:
            one(0, 0)
        else:
            lax.fori_loop(0, count, one, 0)

    def stage_far(self):
        half = self.half
        spot = self.chunk(2)
        self.ready(0, 2)
        self.add(spot, self.full, [(0, 2 * half, [(self.sib, None, 0)])])
        for way, by in enumerate((1, -1)):
            target = shifted(self.me, self.order[2], by)
            rows = pl.ds(way * half, half)
            self.copies.start(
                ("far", by),
                self.mine(spot, self.full, rows),
                self.fars.at[way],
                device_at(target),
            )

    def stage_near(self):
        half = self.half
        for way, by in enumerate((1, -1)):
            spot = self.chunk(by)
            self.ready(1 + way, by)
            self.copies.arrived(("far", by))
            with_far = [(self.sib, None, way * half), (self.fars, way, 0)]
            without = [(self.sib, None, (1 - way) * half)]
            self.add(
                spot, self.full, [(way * half, half, with_far), ((1 - way) * half, half, without)]
            )
            self.copies.start(
                ("near", by),
                self.mine(spot, self.full),
                self.nears.at[way],
                device_at(spot),
            )

    def stage_mid(self):
        half, axis, full = self.half, self.order[1], self.order[0]
        self.ready(3, 0)
        self.copies.arrived(("near", 1))
        self.copies.arrived(("near", -1))
        terms = [(self.sib, None, 0), (self.nears, 0, 0), (self.nears, 1, 0)]
        self.add(self.me, self.full, [(0, 2 * half, terms)])
        for number, by in enumerate(STEPS):
            spot = shifted(self.me, axis, by)
            self.copies.start(
                ("mid", by),
                self.mine(spot, full),
                self.mid.at[number],
                device_at(spot),
            )

    def stage_tail(self):
        half, axis, full = self.half, self.order[0], self.order[0]
        for by in STEPS:
            self.copies.arrived(("mid", by))
        terms = [(self.mid, number, 0) for number in range(3)]
        self.add(self.me, full, [(0, 2 * half, terms)])
        for number, by in enumerate(STEPS):
            spot = shifted(self.me, axis, by)
            self.copies.start(
                ("tail", by),
                self.mine(spot, ""),
                self.tail.at[number],
                device_at(spot),
            )

    def stage_out(self):
        for by in STEPS:
            self.copies.arrived(("tail", by))
        index, _ = decode(0, self.me, "")
        index += (self.core,) if self.inside else ()
        total = self.acc[index].astype(F32)
        for number in range(3):
            total += self.tail[number].astype(F32)
        self.out[...] = total

    def sent(self):
        self.copies.sent()


def reduce_scratch(order, lanes, dtype, source_inside):
    full = bundle_shape(order[:2])
    kinds = [] if source_inside else [pltpu.VMEM((4, 2, 2, 4, 64, lanes), dtype)]
    return kinds + [
        pltpu.VMEM((4, 2, 2, 4, 64, lanes), dtype),
        pltpu.VMEM((2,) + full + (64, lanes), dtype),
        pltpu.VMEM((2,) + full + (32, lanes), dtype),
        pltpu.VMEM((3,) + bundle_shape(order[:1]) + (64, lanes), dtype),
        pltpu.VMEM((3, 64, lanes), dtype),
    ]


def norm_stats(values):
    average = jnp.mean(values, -1, keepdims=True)
    centered = values - average
    inverse = lax.rsqrt(jnp.mean(centered * centered, -1, keepdims=True) + EPSILON)
    return (centered * inverse, inverse)


def norm_back(upstream, normed, inverse, gain_vector):
    scaled = upstream * gain_vector
    return inverse * (
        scaled
        - jnp.mean(scaled, -1, keepdims=True)
        - normed * jnp.mean(scaled * normed, -1, keepdims=True)
    )


def softmax_columns(key_rows, queries, hidden):
    scores = mm(key_rows, queries, NT) + hidden
    powers = jnp.exp((scores - jnp.max(scores, 0, keepdims=True)) * SCALE)
    return powers * (1.0 / jnp.sum(powers, 0, keepdims=True))


def hidden_rows(seq, slot, tokens):
    row = lax.broadcasted_iota(jnp.int32, (seq, 1), 0)
    return jnp.where(lax.rem(row, slot) < tokens, 0.0, -1e30)


def head_lanes(head):
    lane = lax.broadcasted_iota(jnp.int32, (1, 128), 1)
    return jnp.where(lane // HD == head, 1.0, 0.0).astype(BF16)


def thirds(rows):
    return [rows[:, 128 * i : 128 * i + 128] for i in range(3)]


def attend(rows, hidden):
    queries, key_rows, value_rows = thirds(rows)

    def one_head(head, before):
        mine = head_lanes(head)
        probs = softmax_columns(key_rows, queries * mine, hidden).astype(BF16)
        return before + mm(probs, value_rows * mine, TN)

    return lax.fori_loop(0, 2, one_head, jnp.zeros(queries.shape, F32)).astype(BF16)


def attend_back(rows, grads, hidden):
    queries, key_rows, value_rows = thirds(rows)

    def one_head(head, before):
        mine = head_lanes(head)
        own_grads, own_queries = grads * mine, queries * mine
        probs = softmax_columns(key_rows, own_queries, hidden)
        d_probs = mm(value_rows, own_grads, NT)
        inner = jnp.sum(probs * d_probs, 0, keepdims=True)
        d_scores = (probs * (d_probs - inner)).astype(BF16)
        return (
            before[0] + mm(d_scores, key_rows * mine, TN),
            before[1] + mm(d_scores, own_queries),
            before[2] + mm(probs.astype(BF16), own_grads),
        )

    zero = jnp.zeros(queries.shape, F32)
    d_queries, d_keys, d_values = lax.fori_loop(0, 2, one_head, (zero, zero, zero))
    return [
        (d_queries * SCALE).astype(BF16),
        (d_keys * SCALE).astype(BF16),
        d_values.astype(BF16),
    ]


def padded_rows(ref, target):
    micro, tokens, width = ref.shape
    for m in range(micro):
        target[m, :tokens] = ref[m].astype(F32)
        target[m, tokens:] = jnp.zeros((target.shape[1] - tokens, width), F32)


def blocks_of(ref, index):
    value = ref[index // 2, lax.rem(index, 2)]
    return value.reshape(-1, value.shape[-1])


def forward_kernel(*refs):
    (
        x_ref,
        qkv_in,
        wide_1,
        wide_2,
        wide_3,
        small_in,
        low_out,
        images_out,
        attended_out,
        vectors_out,
        hidden_out,
        qkv_out,
        wide_out_1,
        wide_out_2,
        wide_out_3,
        rows,
        wq,
        wk,
        wv,
        small,
        bias,
        low,
        outbox,
        images,
        attended_box,
        attended,
        local_sem,
        gather_send,
        gather_recv,
        send_sem,
        recv_sem,
        back_send,
        back_recv,
        store_sem,
    ) = refs
    me = place()
    f, t = lax.axis_index("fsdp"), lax.axis_index("tp")
    greet(me)
    heads = [wq, wk, wv]
    narrow = [
        Gather(
            me,
            ORDERS[i],
            qkv_in.at[i],
            heads[i],
            gather_send.at[i],
            gather_recv.at[i],
            local_sem.at[i],
        )
        for i in range(3)
    ]
    vector = Gather(
        me, ORDERS[0], small_in, small, gather_send.at[3], gather_recv.at[3], local_sem.at[3]
    )
    wide = [
        Gather(
            me,
            ORDERS[i],
            (wide_1, wide_2, wide_3)[i],
            (wide_out_1, wide_out_2, wide_out_3)[i],
            gather_send.at[4 + i],
            gather_recv.at[4 + i],
            local_sem.at[4 + i],
        )
        for i in range(3)
    ]
    early = [vector] + narrow
    for part in early:
        part.first()
    padded_rows(x_ref, rows)
    values = rows[...].reshape(-1, rows.shape[-1])
    normed, _ = norm_stats(values)
    for part in early:
        part.second()
    for part in early:
        part.thirds()
    for part in wide:
        part.first()
    for part in early:
        part.far()
    for part in wide:
        part.second()
    vector.last()
    vector.done()
    table = jnp.sum(small[...].reshape(128, 32, 128).astype(F32), 1).astype(BF16)
    lane = lax.broadcasted_iota(jnp.int32, (128, 1024), 0)
    column = lax.broadcasted_iota(jnp.int32, (128, 1024), 1)
    row = lane
    owner = jnp.where(lax.rem(row, 16) * 8 + row // 16 == column // 8, 1.0, 0.0)
    for v in range(6):
        pick = jnp.where(lane == v * 8 + lax.rem(column, 8), 1.0, 0.0).astype(BF16)
        vectors_out[v : v + 1, :] = jnp.sum(mm(table, pick) * owner, 0, keepdims=True)
    vectors_out[6:8, :] = jnp.zeros((2, 1024), F32)

    def spread_bias(width, first):
        lane = lax.broadcasted_iota(jnp.int32, (128, width), 0)
        column = lax.broadcasted_iota(jnp.int32, (128, width), 1)
        pick = lane == first + (column // 64) * 4 + lax.rem(column, 4)
        owner = lax.rem(lane, 16) == lax.rem(column, 64) // 4
        values = mm(table, jnp.where(pick, 1.0, 0.0).astype(BF16))
        return jnp.sum(jnp.where(owner, values, 0.0).reshape(8, 16, width), 1)

    hidden_out[...] = spread_bias(512, 64)
    query_bias, value_bias = spread_bias(128, 48), spread_bias(128, 56)
    for i in range(8):
        bias[i, :, 0:128] = query_bias[i : i + 1]
        bias[i, :, 128:256] = jnp.zeros((1, 128), F32)
        bias[i, :, 256:384] = value_bias[i : i + 1]
    low[...] = (normed * vectors_out[0:1, :] + vectors_out[1:2, :]).astype(BF16)
    for part in narrow:
        part.last()
    for part in wide:
        part.thirds()
    for part in narrow:
        part.done()

    def letter(k):
        target = lax.rem(t + k + 1, GROUP)
        return pltpu.make_async_remote_copy(
            outbox.at[target],
            images.at[t],
            send_sem.at[k],
            recv_sem.at[k],
            device_id=(f, target),
            device_id_type=MESH,
        )

    def project(k, carry):
        target = lax.rem(t + k + 1, GROUP)
        weights = jnp.concatenate([blocks_of(w, target) for w in heads], axis=1)
        result = (mm(low[...], weights) + bias[target]).astype(BF16)
        outbox[target] = result.reshape(outbox.shape[1:])

        @pl.when(k < GROUP - 1)
        def _():
            letter(k).start()

        return carry

    lax.fori_loop(0, GROUP, project, 0)
    stores = [
        pltpu.make_async_copy(heads[i], qkv_out.at[i], store_sem.at[i]) for i in range(3)
    ] + [pltpu.make_async_copy(low, low_out, store_sem.at[3])]
    for store in stores:
        store.start()
    own = pltpu.make_async_copy(outbox.at[t], images.at[t], local_sem.at[7])
    own.start()
    own.wait()
    for part in wide:
        part.far((0,))
    for k in range(GROUP - 1):
        letter(k).wait_recv()
    keep = pltpu.make_async_copy(images, images_out, store_sem.at[4])
    keep.start()
    tokens, slot = x_ref.shape[1], rows.shape[1]
    hidden = hidden_rows(GROUP * slot, slot, tokens)

    def reply(m, k):
        target = lax.rem(t + k + 1, GROUP)
        return pltpu.make_async_remote_copy(
            attended_box.at[m, target],
            attended.at[t, m],
            back_send.at[m, k],
            back_recv.at[m, k],
            device_id=(f, target),
            device_id_type=MESH,
        )

    for m in range(MICRO):
        result = attend(images[:, m].reshape(GROUP * slot, 384), hidden)
        attended_box[m] = result.reshape(GROUP, slot, 128)
        for k in range(GROUP - 1):
            reply(m, k).start()
        attended[t, m] = attended_box[m, t]
        if m < MICRO - 1:
            for part in wide:
                part.far((1, 2, 3)[2 * m : 2 * m + 2])
    for part in wide:
        part.last()
    for m in range(MICRO):
        for k in range(GROUP - 1):
            reply(m, k).wait_recv()
    keep_attended = pltpu.make_async_copy(attended, attended_out, store_sem.at[5])
    keep_attended.start()
    for part in wide:
        part.done()
    for part in early + wide:
        part.sent()
    for k in range(GROUP - 1):
        letter(k).wait_send()
        for m in range(MICRO):
            reply(m, k).wait_send()
    for store in stores:
        store.wait()
    keep.wait()
    keep_attended.wait()


ANY = pl.BlockSpec(memory_space=pl.ANY)
VMEM = pl.BlockSpec(memory_space=pltpu.VMEM)


def forward(x, qkv_block, wide_blocks, small, slot):
    width = x.shape[-1]
    count = MICRO * slot
    lanes = qkv_block.shape[-1]
    wide = wide_blocks[0].shape[-1]
    images = (GROUP, MICRO, slot, 3 * lanes)
    attended = (GROUP, MICRO, slot, lanes)
    return pl.pallas_call(
        forward_kernel,
        out_shape=[
            jax.ShapeDtypeStruct((count, width), BF16),
            jax.ShapeDtypeStruct(images, BF16),
            jax.ShapeDtypeStruct(attended, BF16),
            jax.ShapeDtypeStruct((8, width), F32),
            jax.ShapeDtypeStruct((8, 512), F32),
            jax.ShapeDtypeStruct((3,) + LEAD + (64, lanes), BF16),
        ]
        + [jax.ShapeDtypeStruct(LEAD + (64, wide), BF16)] * 3,
        in_specs=[VMEM] + [ANY] * 5,
        out_specs=[ANY] * 3 + [VMEM] * 2 + [ANY] * 4,
        scratch_shapes=[
            pltpu.VMEM((MICRO, slot, width), F32),
            pltpu.VMEM(LEAD + (64, lanes), BF16),
            pltpu.VMEM(LEAD + (64, lanes), BF16),
            pltpu.VMEM(LEAD + (64, lanes), BF16),
            pltpu.VMEM(LEAD + (32, 128), BF16),
            pltpu.VMEM((GROUP, 1, 3 * lanes), F32),
            pltpu.VMEM((count, width), BF16),
            pltpu.VMEM(images, BF16),
            pltpu.VMEM(images, BF16),
            pltpu.VMEM((MICRO, GROUP, slot, lanes), BF16),
            pltpu.VMEM(attended, BF16),
            pltpu.SemaphoreType.DMA((8,)),
            pltpu.SemaphoreType.DMA((7, Gather.slots)),
            pltpu.SemaphoreType.DMA((7, Gather.slots)),
            pltpu.SemaphoreType.DMA((GROUP,)),
            pltpu.SemaphoreType.DMA((GROUP,)),
            pltpu.SemaphoreType.DMA((MICRO, GROUP)),
            pltpu.SemaphoreType.DMA((MICRO, GROUP)),
            pltpu.SemaphoreType.DMA((6,)),
        ],
        compiler_params=pltpu.CompilerParams(
            collective_id=0, has_side_effects=True, vmem_limit_bytes=VMEM_LIMIT
        ),
        name="forward",
    )(x, qkv_block, *wide_blocks, small)


def middle_kernel(
    x_ref,
    cot_ref,
    valid_ref,
    attended_ref,
    out_ref,
    wide_1,
    wide_2,
    wide_3,
    vectors_ref,
    hidden_ref,
    result_ref,
    d_middle_ref,
    low_middle_ref,
    d_attended_ref,
    grad_1,
    grad_2,
    grad_3,
    sums_ref,
    hidden_sums_ref,
    rows,
    middle,
    normed,
    inverse,
    low,
    low_t,
    upstream_low,
    upstream_t,
    forward_sum,
    back_sum,
):
    step = pl.program_id(0)
    micro, tokens, width = x_ref.shape
    count = micro * rows.shape[1]
    gain_two, bias_two = vectors_ref[3:4, :], vectors_ref[4:5, :]

    @pl.when(step == 0)
    def _():
        padded_rows(x_ref, rows)
        middle[...] = rows[...].reshape(count, width) + vectors_ref[2:3, :]

        def project(pair, carry):
            both = [attended_ref[2 * pair + i].reshape(count, 128) for i in range(2)]
            weights = [out_ref[2 * pair + i] for i in range(2)]
            middle[...] += mm(
                jnp.concatenate(both, axis=1), jnp.concatenate(weights, axis=1), NT
            )
            return carry

        lax.fori_loop(0, GROUP // 2, project, 0)
        normed[...], inverse[...] = norm_stats(middle[...])
        low[...] = (normed[...] * gain_two + bias_two).astype(BF16)
        low_t[...] = low[...].T
        for m in range(micro):
            slot = valid_ref[m, 0].astype(F32)
            rows[m, :tokens] = cot_ref[m].astype(F32) * slot
        values = rows[...].reshape(count, width)
        sums_ref[5:6, :] = jnp.sum(values, 0, keepdims=True)
        upstream_low[...] = values.astype(BF16)
        upstream_t[...] = upstream_low[...].T
        forward_sum[...] = jnp.zeros_like(forward_sum)
        back_sum[...] = jnp.zeros_like(back_sum)

    up_weight = jnp.concatenate([wide_1[0, :, 128:], wide_2[0, :, :256]], axis=1)
    down_weight = jnp.concatenate([wide_2[0, :, 256:], wide_3[0]], axis=1)
    up_proj = mm(low[...], up_weight) + hidden_ref[0]
    gate = jax.nn.sigmoid(1.702 * up_proj)
    activated = (up_proj * gate).astype(BF16)
    d_act = mm(upstream_low[...], down_weight)
    d_up = (d_act * (gate + 1.702 * up_proj * gate * (1.0 - gate))).astype(BF16)
    hidden_sums_ref[0] = jnp.sum(d_up.astype(F32), 0, keepdims=True)
    forward_sum[...] += mm(activated, down_weight, NT)
    back_sum[...] += mm(d_up, up_weight, NT)
    grad_up = mm(low_t[...], d_up).astype(BF16)
    grad_1[0] = grad_up[:, :384]
    grad_2[0, :, :128] = grad_up[:, 384:]
    grad_down = mm(upstream_t[...], activated).astype(BF16)
    grad_2[0, :, 128:] = grad_down[:, :256]
    grad_3[0] = grad_down[:, 256:]

    @pl.when(step == GROUP - 1)
    def _():
        output = (middle[...] + forward_sum[...] + vectors_ref[5:6, :]).reshape(rows.shape)
        result_ref[...] = output[:, :tokens].astype(BF16)
        d_norm = back_sum[...]
        upstream = rows[...].reshape(count, width)
        d_middle = upstream + norm_back(d_norm, normed[...], inverse[...], gain_two)
        d_middle_ref[...] = d_middle
        low_middle = d_middle.astype(BF16)
        low_middle_ref[...] = low_middle
        sums_ref[0:2, :] = jnp.zeros((2, width), F32)
        sums_ref[2:3, :] = jnp.sum(d_middle, 0, keepdims=True)
        sums_ref[3:4, :] = jnp.sum(d_norm * normed[...], 0, keepdims=True)
        sums_ref[4:5, :] = jnp.sum(d_norm, 0, keepdims=True)
        sums_ref[6:8, :] = jnp.zeros((2, width), F32)

        def project_back(pair, carry):
            weights = [out_ref[2 * pair + i] for i in range(2)]
            both = mm(low_middle_ref[...], jnp.concatenate(weights, axis=1)).astype(BF16)
            for i in range(2):
                d_attended_ref[2 * pair + i] = both[:, 128 * i : 128 * i + 128].reshape(
                    d_attended_ref.shape[1:]
                )
            return carry

        lax.fori_loop(0, GROUP // 2, project_back, 0)


def middle_part(x, cotangent, valid, attended, wide, vectors, hidden):
    micro, tokens, width = x.shape
    slot = attended.shape[2]
    count = micro * slot
    whole = lambda shape: pl.BlockSpec(shape, lambda t: (0,) * len(shape))
    slab = lambda lanes: pl.BlockSpec((1, width, lanes), lambda t: (t, 0, 0))
    line = pl.BlockSpec((1, 1, 512), lambda t: (t, 0, 0))
    return pl.pallas_call(
        middle_kernel,
        grid=(GROUP,),
        in_specs=[
            whole(x.shape),
            whole(x.shape),
            pl.BlockSpec(memory_space=pltpu.SMEM),
            whole(attended.shape),
            whole((GROUP, width, 128)),
            slab(384),
            slab(384),
            slab(384),
            whole(vectors.shape),
            line,
        ],
        out_specs=[
            whole(x.shape),
            whole((count, width)),
            whole((count, width)),
            whole(attended.shape),
            slab(384),
            slab(384),
            slab(256),
            whole((8, width)),
            line,
        ],
        out_shape=[
            jax.ShapeDtypeStruct(x.shape, BF16),
            jax.ShapeDtypeStruct((count, width), F32),
            jax.ShapeDtypeStruct((count, width), BF16),
            jax.ShapeDtypeStruct(attended.shape, BF16),
            jax.ShapeDtypeStruct((GROUP, width, 384), BF16),
            jax.ShapeDtypeStruct((GROUP, width, 384), BF16),
            jax.ShapeDtypeStruct((GROUP, width, 256), BF16),
            jax.ShapeDtypeStruct((8, width), F32),
            jax.ShapeDtypeStruct((GROUP, 1, 512), F32),
        ],
        scratch_shapes=[
            pltpu.VMEM((micro, slot, width), F32),
            pltpu.VMEM((count, width), F32),
            pltpu.VMEM((count, width), F32),
            pltpu.VMEM((count, 1), F32),
            pltpu.VMEM((count, width), BF16),
            pltpu.VMEM((width, count), BF16),
            pltpu.VMEM((count, width), BF16),
            pltpu.VMEM((width, count), BF16),
            pltpu.VMEM((count, width), F32),
            pltpu.VMEM((count, width), F32),
        ],
        compiler_params=pltpu.CompilerParams(vmem_limit_bytes=VMEM_LIMIT),
        name="middle",
    )(x, cotangent, valid, attended, wide[0], *wide, vectors, hidden)


def backward_kernel(*refs):
    (
        d_attended_in,
        images_in,
        low_in,
        low_middle_in,
        attended_in,
        d_middle_ref,
        x_ref,
        vectors_ref,
        sums_ref,
        hidden_sums_ref,
        qkv_in,
        grad_1,
        grad_2,
        grad_3,
        input_grad_out,
        sum_1,
        sum_2,
        sum_3,
        sum_o,
        sum_q,
        sum_k,
        sum_v,
        payload_out,
        rows,
        wq,
        wk,
        wv,
        low,
        low_middle,
        attended,
        images,
        d_attended,
        outbox,
        d_images,
        d_norm,
        go,
        gq,
        gk,
        gv,
        payload,
        payload_in,
        *rest,
    ) = refs
    rest = list(rest)
    me = place()
    f, t = lax.axis_index("fsdp"), lax.axis_index("tp")
    greet(me)
    kinds = [
        (grad_1, None, sum_1, 0),
        (grad_2, None, sum_2, 1),
        (grad_3, None, sum_3, 2),
        (go, go, sum_o, 2),
        (gq, gq, sum_q, 0),
        (gk, gk, sum_k, 1),
        (gv, gv, sum_v, 2),
    ]
    pieces = []
    for source, acc, out, _ in kinds:
        if acc is None:
            acc = rest.pop(0)
        pieces.append([source, acc] + [rest.pop(0) for _ in range(5)] + [out])
    (
        load_sem,
        fetch_sem,
        reduce_send,
        reduce_recv,
        send_sem,
        recv_sem,
        back_send,
        back_recv,
        sum_send,
        sum_recv,
    ) = rest
    parts = [
        Reduce(
            me,
            ORDERS[kinds[i][3]],
            *pieces[i],
            reduce_send.at[i],
            reduce_recv.at[i],
            fetch_sem.at[i],
        )
        for i in range(7)
    ]
    wide, late = parts[:4], parts[4:]
    heads = [wq, wk, wv]

    def letter(k):
        target = lax.rem(t + k + 1, GROUP)
        return pltpu.make_async_remote_copy(
            d_attended_in.at[target],
            d_attended.at[t],
            send_sem.at[k],
            recv_sem.at[k],
            device_id=(f, target),
            device_id_type=MESH,
        )

    for k in range(GROUP - 1):
        letter(k).start()
    loads = [
        (d_attended_in.at[t], d_attended.at[t]),
        (images_in, images),
        (low_middle_in, low_middle),
        (attended_in, attended),
        (low_in, low),
        (qkv_in.at[0], wq),
        (qkv_in.at[1], wk),
        (qkv_in.at[2], wv),
    ]
    loads = [
        pltpu.make_async_copy(src, dst, load_sem.at[i]) for i, (src, dst) in enumerate(loads)
    ]
    for load in loads:
        load.start()
    for part in wide[:3]:
        part.begin()
    loads[2].wait()
    loads[3].wait()
    turned = low_middle[...].T
    count = low_middle.shape[0]

    def out_gradient(index, carry):
        result = mm(turned, attended[index].reshape(count, 128)).astype(BF16)
        go[index // 2, lax.rem(index, 2)] = result.reshape(go.shape[2:])
        return carry

    lax.fori_loop(0, GROUP, out_gradient, 0)
    wide[3].begin()
    for part in wide:
        part.stage_far()
    loads[0].wait()
    loads[1].wait()
    for k in range(GROUP - 1):
        letter(k).wait_recv()
    tokens, slot = x_ref.shape[1], rows.shape[1]
    hidden = hidden_rows(GROUP * slot, slot, tokens)

    def reply(m, k):
        target = lax.rem(t + k + 1, GROUP)
        return pltpu.make_async_remote_copy(
            outbox.at[m, target],
            d_images.at[t, m],
            back_send.at[m, k],
            back_recv.at[m, k],
            device_id=(f, target),
            device_id_type=MESH,
        )

    for m in range(MICRO):
        results = attend_back(
            images[:, m].reshape(GROUP * slot, 384),
            d_attended[:, m].reshape(GROUP * slot, 128),
            hidden,
        )
        for i in range(3):
            outbox[m, :, :, 128 * i : 128 * i + 128] = results[i].reshape(GROUP, slot, 128)
        for k in range(GROUP - 1):
            reply(m, k).start()
        d_images[t, m] = outbox[m, t]
        if m == 0:
            for part in wide:
                part.stage_near()
    for part in wide:
        part.stage_mid()
    padded_rows(x_ref, rows)
    normed, inverse = norm_stats(rows[...].reshape(count, rows.shape[-1]))
    for load in loads[4:]:
        load.wait()
    low_t = low[...].T
    d_norm[...] = jnp.zeros_like(d_norm)
    for m in range(MICRO):
        for k in range(GROUP - 1):
            reply(m, k).wait_recv()
    for part in wide:
        part.stage_tail()

    def project_back(index, carry):
        grads = d_images[index].reshape(count, 384)
        weights = jnp.concatenate([blocks_of(w, index) for w in heads], axis=1)
        d_norm[...] += mm(grads, weights, NT)
        result = mm(low_t, grads).astype(BF16)
        for i, g in enumerate((gq, gk, gv)):
            g[index // 2, lax.rem(index, 2)] = result[:, 128 * i : 128 * i + 128].reshape(
                g.shape[2:]
            )
        return carry

    lax.fori_loop(0, GROUP, project_back, 0)
    for part in late:
        part.begin()
    gain_one = vectors_ref[0:1, :]
    gradient = d_norm[...]
    payload[0, 0:8, :] = sums_ref[...]
    payload[0, 0:1, :] = jnp.sum(gradient * normed, 0, keepdims=True)
    payload[0, 1:2, :] = jnp.sum(gradient, 0, keepdims=True)
    for index in range(GROUP):
        grads = jnp.sum(d_images[index].reshape(count, 384).astype(F32), 0, keepdims=True)
        payload[0, 6:7, 128 * index : 128 * index + 128] = grads[:, :128]
        payload[0, 7:8, 128 * index : 128 * index + 128] = grads[:, 256:]
        at = 8 + index // 2
        payload[0, at : at + 1, 512 * (index % 2) : 512 * (index % 2) + 512] = hidden_sums_ref[
            index
        ]
    payload[0, 12:16, :] = jnp.zeros((4, payload.shape[-1]), F32)

    rounds = [[shifted(me, axis, by) for by in STEPS] for axis in "xyz"] + [[sibling(me)]]

    def tell(number, i):
        return pltpu.make_async_remote_copy(
            payload.at[number],
            payload_in.at[number, i],
            sum_send.at[number, i],
            sum_recv.at[number, i],
            device_id=device_at(rounds[number][i]),
            device_id_type=MESH,
        )

    def speak(number):
        for i in range(len(rounds[number])):
            tell(number, i).start()

    def hear(number):
        total = payload[number]
        for i in range(len(rounds[number])):
            tell(number, i).wait_recv()
            total += payload_in[number, i]
        payload[number + 1] = total

    speak(0)
    for part in wide:
        part.stage_out()
    for part in late:
        part.stage_far()
    hear(0)
    speak(1)
    result = d_middle_ref[...] + norm_back(gradient, normed, inverse, gain_one)
    input_grad_out[...] = result.reshape(rows.shape)[:, :tokens].astype(BF16)
    hear(1)
    speak(2)
    for part in late:
        part.stage_near()
    hear(2)
    speak(3)
    for part in late:
        part.stage_mid()
    hear(3)
    payload_out[...] = payload[4]
    for part in late:
        part.stage_tail()
    for part in late:
        part.stage_out()
    for part in parts:
        part.sent()
    for k in range(GROUP - 1):
        letter(k).wait_send()
        for m in range(MICRO):
            reply(m, k).wait_send()
    for number in range(4):
        for i in range(len(rounds[number])):
            tell(number, i).wait_send()


def backward(
    d_attended, images, low, low_middle, attended, d_middle, x, vectors, sums, hidden_sums, qkv, grads
):
    width = x.shape[-1]
    count = low.shape[0]
    slot = count // MICRO
    lanes = [g.shape[-1] for g in grads]
    orders = (0, 1, 2, 2, 0, 1, 2)
    scratch = []
    for i in range(7):
        scratch += reduce_scratch(ORDERS[orders[i]], lanes[i] if i < 3 else 128, BF16, i >= 3)
    return pl.pallas_call(
        backward_kernel,
        out_shape=[jax.ShapeDtypeStruct(x.shape, BF16)]
        + [jax.ShapeDtypeStruct((64, n), F32) for n in lanes + [128] * 4]
        + [jax.ShapeDtypeStruct((16, width), F32)],
        in_specs=[ANY] * 5 + [VMEM] * 5 + [ANY] * 4,
        out_specs=[VMEM] * 9,
        scratch_shapes=[
            pltpu.VMEM((MICRO, slot, width), F32),
            pltpu.VMEM(LEAD + (64, 128), BF16),
            pltpu.VMEM(LEAD + (64, 128), BF16),
            pltpu.VMEM(LEAD + (64, 128), BF16),
            pltpu.VMEM(low.shape, BF16),
            pltpu.VMEM(low_middle.shape, BF16),
            pltpu.VMEM(attended.shape, BF16),
            pltpu.VMEM(images.shape, BF16),
            pltpu.VMEM(d_attended.shape, BF16),
            pltpu.VMEM((MICRO, GROUP, slot, 384), BF16),
            pltpu.VMEM(images.shape, BF16),
            pltpu.VMEM((count, width), F32),
            pltpu.VMEM(LEAD + (64, 128), BF16),
            pltpu.VMEM(LEAD + (64, 128), BF16),
            pltpu.VMEM(LEAD + (64, 128), BF16),
            pltpu.VMEM(LEAD + (64, 128), BF16),
            pltpu.VMEM((5, 16, width), F32),
            pltpu.VMEM((4, 3, 16, width), F32),
        ]
        + scratch
        + [
            pltpu.SemaphoreType.DMA((8,)),
            pltpu.SemaphoreType.DMA((7, 4)),
            pltpu.SemaphoreType.DMA((7, Reduce.slots)),
            pltpu.SemaphoreType.DMA((7, Reduce.slots)),
            pltpu.SemaphoreType.DMA((GROUP,)),
            pltpu.SemaphoreType.DMA((GROUP,)),
            pltpu.SemaphoreType.DMA((MICRO, GROUP)),
            pltpu.SemaphoreType.DMA((MICRO, GROUP)),
            pltpu.SemaphoreType.DMA((4, 3)),
            pltpu.SemaphoreType.DMA((4, 3)),
        ],
        compiler_params=pltpu.CompilerParams(
            collective_id=1, has_side_effects=True, vmem_limit_bytes=VMEM_LIMIT
        ),
        name="backward",
    )(
        d_attended,
        images,
        low,
        low_middle,
        attended,
        d_middle,
        x,
        vectors,
        sums,
        hidden_sums,
        qkv,
        *(g.reshape(LEAD + (64, g.shape[-1])) for g in grads),
    )


def per_device(
    inputs,
    cotangent,
    valid_slots,
    ln1_gain,
    ln1_bias,
    qkv_weight,
    qv_bias,
    out_weight,
    out_bias,
    ln2_gain,
    ln2_bias,
    fc1_weight,
    fc1_bias,
    fc2_weight,
    fc2_bias,
):
    micro, _, tokens, width = inputs.shape
    slot = -(-tokens // 16) * 16
    x = inputs.reshape(micro, tokens, width)
    small = jnp.concatenate(
        [ln1_gain, ln1_bias, out_bias, ln2_gain, ln2_bias, fc2_bias]
        + [qv_bias.reshape(-1), fc1_bias.reshape(-1)]
    )
    small = jnp.pad(small.reshape(1, 96), ((0, 31), (0, 32)))
    down = fc2_weight.T
    wide_blocks = [
        jnp.concatenate([out_weight.T, fc1_weight[:, :256]], axis=1),
        jnp.concatenate([fc1_weight[:, 256:], down[:, :128]], axis=1),
        down[:, 128:],
    ]
    low, images, attended, vectors, hidden, qkv, *wide = forward(
        x, qkv_weight, wide_blocks, small, slot
    )
    wide = [w.reshape(GROUP, width, 384) for w in wide]
    result, d_middle, low_middle, d_attended, *grads, sums, hidden_sums = middle_part(
        x,
        cotangent.reshape(x.shape),
        valid_slots,
        attended,
        wide,
        vectors,
        hidden.reshape(GROUP, 1, 512),
    )
    input_grad, sum_1, sum_2, sum_3, sum_o, sum_q, sum_k, sum_v, total = backward(
        d_attended,
        images,
        low,
        low_middle,
        attended,
        d_middle,
        x,
        vectors,
        sums,
        hidden_sums,
        qkv,
        grads,
    )
    f, t = lax.axis_index("fsdp"), lax.axis_index("tp")
    own = lax.dynamic_slice(total, (0, (f * 8 + t) * 8), (6, 8))
    pair = lax.dynamic_slice(total[6:8].reshape(2, 16, 64), (0, 2 * t, 4 * f), (2, 2, 4))
    hidden_grad = lax.dynamic_slice(total[8:12].reshape(64, 64), (8 * t, 4 * f), (8, 4))
    return (
        result.reshape(inputs.shape),
        input_grad.reshape(inputs.shape),
        own[0],
        own[1],
        jnp.stack([sum_q, sum_k, sum_v]),
        pair,
        sum_o.T,
        own[2],
        own[3],
        own[4],
        jnp.concatenate([sum_1, sum_2[:, :128]], axis=1),
        hidden_grad,
        jnp.concatenate([sum_2[:, 128:], sum_3], axis=1).T,
        own[5],
    )


def solution(mesh):
    in_specs = (
        P(None, "fsdp", "tp", None),
        P(None, "fsdp", "tp", None),
        P(None, "fsdp"),
        P(("fsdp", "tp")),
        P(("fsdp", "tp")),
        P(None, "fsdp", "tp"),
        P(None, "tp", "fsdp"),
        P("tp", "fsdp"),
        P(("fsdp", "tp")),
        P(("fsdp", "tp")),
        P(("fsdp", "tp")),
        P("fsdp", "tp"),
        P("tp", "fsdp"),
        P("tp", "fsdp"),
        P(("fsdp", "tp")),
    )
    out_specs = (
        P(None, "fsdp", "tp", None),
        P(None, "fsdp", "tp", None),
        P(("fsdp", "tp")),
        P(("fsdp", "tp")),
        P(None, "fsdp", "tp"),
        P(None, "tp", "fsdp"),
        P("tp", "fsdp"),
        P(("fsdp", "tp")),
        P(("fsdp", "tp")),
        P(("fsdp", "tp")),
        P("fsdp", "tp"),
        P("tp", "fsdp"),
        P("tp", "fsdp"),
        P(("fsdp", "tp")),
    )
    return jax.shard_map(
        per_device, mesh=mesh, in_specs=in_specs, out_specs=out_specs, check_vma=False
    )
```

time: 1870 us -> 261 us (0.14)
  waiting for transfers between devices: 1350 us -> 0 us
  blocking collectives: 259 us -> 0 us
  Pallas kernels: 0 us -> 232 us
  matrix products: 127 us -> 0 us
  other arithmetic: 40.3 us -> 5.86 us
  local copies, waits for them, and re-layouts: 54 us -> 21 us
  between operations: 21 us -> 0.68 us
    reduce_scatter x21 -> x0, waiting for transfers between devices: 940 us -> none  [the longest x3 208 us: per_device(): lax.psum_scatter(grad_fc2.astype(jnp.bfloat16), 'fsdp', scatter_dimension...]
    all_gather x14 -> x0, waiting for transfers between devices: 330 us -> none  [the longest x3 112 us: per_device(): lax.all_gather(upstream_low, 'tp', axis=1, tiled=True)]
    pallas_call x0 -> x3, Pallas kernels: none -> 232 us  [the longest x1 109 us: backward(): pl.pallas_call(backward_kernel, out_shape=[jax.ShapeDtypeStruct(x.shape,...]
    unnamed x3 -> x0, blocking collectives: 169 us -> none
    dot_general x54 -> x0, matrix products: 127 us -> none  [the longest x3 11.3 us: per_device(): jnp.einsum('nf,nd->fd', activated, seq_upstream, preferred_element_type=j...]
    all_gather x4 -> x0, blocking collectives: 90.2 us -> none  [the longest x1 24.2 us: per_device(): lax.all_gather(fc1_bias, 'fsdp', axis=1, tiled=True)]
    unnamed x37 -> x0, waiting for transfers between devices: 83.7 us -> none
    unnamed x282 -> x5, local copies, waits for them, and re-layouts: 27 us -> 5.91 us
  transfers between devices with their start and end apart: 36 -> 0, of which waited for: 31 -> 0; matrix products, arithmetic and copies ran while one was open for 10% -> 0% of each run, Pallas kernels for 0% -> 0%
where the time goes in v2:
time: 261 us; the launch traced here: 259 us
  Pallas kernels  232 us (89%)
  local copies, waits for them, and re-layouts  21 us (8%)
  other arithmetic  5.86 us (2%)
    pallas_call x1, Pallas kernels, backward(): pl.pallas_call(backward_kernel, out_shape=[jax.ShapeDtypeStruct(x.shape,...  109 us
    pallas_call x1, Pallas kernels, forward(): pl.pallas_call(forward_kernel, out_shape=[jax.ShapeDtypeStruct((count, wi...  95.8 us
    pallas_call x1, Pallas kernels, middle_part(): pl.pallas_call(middle_kernel, grid=(GROUP,), in_specs=[whole(x.shape), wh...  26.5 us
    unnamed x5, local copies, waits for them, and re-layouts  5.91 us

profile of v2, /device:TPU:0, one launch (start us, length us, event | category | flops | bytes accessed | tf_op | source)
XLA Modules:
  0.0 259.1 jit_solution(5912898595026603453)
XLA Ops:
  0.6 0.8 fusion
  1.4 0.7 slice.56
  2.1 1.4 pad_maximum_fusion.2
  3.5 1.4 slice.57.refs_4_
  4.9 0.8 copy.34
  5.7 0.1 reshape.79
  5.8 0.8 reshape.78
  6.5 4.1 %concatenate.17 = bf16[96]{0:T(256)(128)(2,1)S(1)} concatenate(bf16[8]{0:T(256)(128)(2,1)} %param.18, bf16[8]{0:T(256)(128)(2,1)} %param.19, bf16[8]{0:T(256)(128)(2,1)} %param.23, bf16[8]{0:T(256)(128)(2,1)} %param.24, bf16[8]{0:T(256)(128)(2,1)} %param.25, bf16[8]{0:T(256)(128)(2,1)} %param.29, bf16[16]{0:T(256)(128)(2,1)S(1)} %reshape.78, bf16[32]{0:T(256)(128)(2,1)S(1)} %reshape.79), dimensions={0} | concatenate | bytes 384 | tf_op jit(solution)/shard_map/concatenate | solution.py:1240
  10.6 0.6 pad.4.refs_5_
  11.3 95.8 %forward.1 = (bf16[240,1024]{1,0:T(8,128)(2,1)}, bf16[8,3,80,384]{3,2,1,0:T(8,128)(2,1)}, bf16[8,3,80,128]{3,2,1,0:T(8,128)(2,1)}, f32[8,1024]{1,0:T(8,128)}, f3...) custom-call(bf16[3,72,1024]{2,1,0:T(8,128)(2,1)} %bitcast.42, ...), custom_call_target="tpu_custom_call" | custom-call | tf_op jit(solution)/shard_map/forward/pallas_call | solution.py:674
  107.1 1.3 reshape.84.hidden_ref
  108.4 1.3 copy.35.valid_ref
  109.7 26.5 %middle.1 = (bf16[3,72,1024]{2,1,0:T(8,128)(2,1)}, f32[240,1024]{1,0:T(8,128)}, bf16[240,1024]{1,0:T(8,128)(2,1)}, bf16[8,3,80,128]{3,2,1,0:T(8,128)(2,1)}, bf16...) custom-call(bf16[3,72,1024]{2,1,0:T(8,128)(2,1)} %bitcast.43, ...), custom_call_target="tpu_custom_call" | custom-call | tf_op jit(solution)/shard_map/middle/pallas_call | solution.py:830
  136.3 109.2 %backward.1 = (bf16[3,72,1024]{2,1,0:T(8,128)(2,1)}, f32[64,384]{1,0:T(8,128)}, f32[64,384]{1,0:T(8,128)}, f32[64,256]{1,0:T(8,128)}, f32[64,128]{1,0:T(8,128)},...) custom-call(bf16[8,3,80,128]{3,2,1,0:T(8,128)(2,1)} %get-tuple-element.48.refs_0_, ...), custom_call_target="tpu_custom_call" | custom-call | tf_op jit(solution)/shard_map/backward/pallas_call | solution.py:1160
  245.5 0.8 slice.54
  246.3 1.5 maximum_bitcast_fusion
  247.8 0.8 slice.52
  248.6 1.6 pad_maximum_fusion
  250.1 1.4 pad_maximum_fusion.1
  251.6 0.8 slice.53
  252.3 0.1 reshape.91
  252.4 0.1 dynamic_slice.11
  252.5 0.7 copy.39
  253.2 0.8 slice.48
  253.9 0.1 reshape.90
  254.0 0.7 constant_dynamic-slice_fusion
  254.7 0.7 constant_dynamic-slice_fusion.1
  255.4 0.5 slice_bitcast_fusion
  255.9 1.8 copy.42
  257.7 1.4 copy.43

commit v3 on v2

v3 whole, which is shorter than its diff:
```python
import functools
import math

import jax
import jax.numpy as jnp
from jax import lax
from jax.experimental import pallas as pl
from jax.experimental.pallas import tpu as pltpu
from jax.sharding import PartitionSpec as P

MESH = pl.DeviceIdType.MESH
HD = 64
SCALE = 1.0 / math.sqrt(HD)
EPSILON = 1e-05
BF16 = jnp.bfloat16
F32 = jnp.float32
VMEM_LIMIT = 62 * 2**20
MICRO, GROUP = 3, 8
ORDERS = (("x", "y", "z"), ("y", "z", "x"), ("z", "x", "y"))
SIZES = {"x": (4,), "z": (2, 2), "y": (4,)}
LEAD = (4, 2, 2, 4, 2)
STEPS = (1, -1, 2)
NN = (((1,), (0,)), ((), ()))
NT = (((1,), (1,)), ((), ()))
TN = (((0,), (0,)), ((), ()))


def mm(a, b, dims=NN):
    return lax.dot_general(a, b, dims, preferred_element_type=F32)


def place():
    f, t = lax.axis_index("fsdp"), lax.axis_index("tp")
    return {
        "x": t // 2,
        "y": lax.rem(f // 2, 4),
        "z": (f // 8) * 2 + lax.rem(t, 2),
        "c": lax.rem(f, 2),
    }


def device_at(spot):
    return (
        (spot["z"] // 2) * 8 + spot["y"] * 2 + spot["c"],
        spot["x"] * 2 + lax.rem(spot["z"], 2),
    )


def shifted(spot, axis, by):
    return {**spot, axis: lax.rem(spot[axis] + by + 4, 4)}


def sibling(spot):
    return {**spot, "c": 1 - spot["c"]}


def greet(me):
    f, t = lax.axis_index("fsdp"), lax.axis_index("tp")
    devices = [(f, lax.rem(t + step, GROUP)) for step in range(1, GROUP)]
    devices += [device_at(shifted(me, "y", by)) for by in STEPS]
    devices += [device_at(shifted(me, "z", 2))]
    devices += [device_at(shifted(me, "z", 2 * lax.rem(me["z"], 2) - 1))]
    devices += [device_at(sibling(me))]
    barrier = pltpu.get_barrier_semaphore()
    for device in devices:
        pl.semaphore_signal(barrier, inc=1, device_id=device, device_id_type=MESH)
    pl.semaphore_wait(barrier, len(devices))


def view(ref, spot, full, core=None, rows=slice(None)):
    whole = slice(None)
    index = [
        whole if "x" in full else spot["x"],
        whole if "z" in full else lax.rem(spot["z"], 2),
        whole if "z" in full else spot["z"] // 2,
        whole if "y" in full else spot["y"],
    ]
    if core is not None:
        index.append(core)
    return ref.at[tuple(index) + (rows,)]


def decode(number, spot, full):
    at = {}
    for axis in "yzx":
        if axis in full:
            parts = []
            for size in reversed(SIZES[axis]):
                parts.append(lax.rem(number, size))
                number = number // size
            at[axis] = tuple(reversed(parts))
    fixed = {"x": (spot["x"],), "z": (lax.rem(spot["z"], 2), spot["z"] // 2), "y": (spot["y"],)}
    index, inner = (), ()
    for axis in "xzy":
        index += at.get(axis, fixed[axis])
        inner += at.get(axis, ())
    return index, inner


def bundle_shape(full):
    shape = ()
    for axis in "xzy":
        shape += SIZES[axis] if axis in full else ()
    return shape


class Copies:
    def __init__(self, send, recv):
        self.send, self.recv = send, recv
        self.made = {}

    def start(self, name, src, dst, device):
        slot = len(self.made)
        self.made[name] = pltpu.make_async_remote_copy(
            src,
            dst,
            self.send.at[slot],
            self.recv.at[slot],
            device_id=device,
            device_id_type=MESH,
        )
        self.made[name].start()

    def arrived(self, name):
        self.made[name].wait_recv()

    def sent(self):
        for copy in self.made.values():
            copy.wait_send()


class Gather:
    slots = 38

    def __init__(self, me, order, block, out, send, recv, local):
        self.me, self.order, self.block, self.out = me, order, block, out
        self.copies = Copies(send, recv)
        self.local = local
        self.core = me["c"]
        self.half = out.shape[-2] // 2

    def piece(self, spot, full, rows=slice(None)):
        return view(self.out, spot, full, self.core, rows)

    def spread(self, name, spot, full, axis, by, rows=slice(None)):
        piece = self.piece(spot, full, rows)
        target = shifted(self.me, axis, by)
        self.copies.start(name, piece, piece, device_at(target))

    def share(self, name, spot, full):
        piece = self.piece(spot, full)
        self.copies.start(name, piece, piece, device_at(sibling(self.me)))

    def own(self):
        return pltpu.make_async_copy(
            self.block, view(self.out, self.me, "", self.core), self.local
        )

    def first(self):
        me, axis = self.me, self.order[0]
        self.own().start()
        for by in STEPS:
            target = shifted(me, axis, by)
            self.copies.start(
                ("first", by), self.block, self.piece(me, ""), device_at(target)
            )

    def second(self):
        full, axis = self.order[0], self.order[1]
        self.own().wait()
        for by in STEPS:
            self.copies.arrived(("first", by))
        for by in STEPS:
            self.spread(("second", by), self.me, full, axis, by)
        self.third(0)

    def third(self, group):
        full, axis = self.order[0], self.order[2]
        spot = self.spot(group)
        if group:
            self.copies.arrived(("second", STEPS[group - 1]))
        for by in (1, -1):
            self.spread(("near", group, by), spot, full, axis, by)
        self.share(("share", group), spot, full)

    def spot(self, group):
        return self.me if group == 0 else shifted(self.me, self.order[1], -STEPS[group - 1])

    def thirds(self):
        for group in (1, 2, 3):
            self.third(group)

    def far(self, groups=(0, 1, 2, 3)):
        full, axis = self.order[0], self.order[2]
        for group in groups:
            for way, by in enumerate((1, -1)):
                spot = shifted(self.spot(group), axis, -by)
                self.copies.arrived(("near", group, by))
                rows = pl.ds(way * self.half, self.half)
                self.spread(("far", group, by), spot, full, axis, by, rows)
                self.share(("share near", group, by), spot, full)

    def last(self):
        full, axis = self.order[0], self.order[2]
        for group in range(4):
            for by in (1, -1):
                self.copies.arrived(("far", group, by))
            self.share(("share far", group), shifted(self.spot(group), axis, 2), full)

    def done(self):
        for group in range(4):
            self.copies.arrived(("share", group))
            self.copies.arrived(("share near", group, 1))
            self.copies.arrived(("share near", group, -1))
            self.copies.arrived(("share far", group))

    def sent(self):
        self.copies.sent()


class Reduce:
    slots = 10

    def __init__(self, me, order, acc, near, far, mid, tail, send, recv):
        self.me, self.order, self.acc = me, order, acc
        self.nears, self.fars, self.mid, self.tail = near, far, mid, tail
        self.copies = Copies(send, recv)
        self.half = acc.shape[-2] // 2
        self.full = "".join(order[:2])

    def chunk(self, by):
        return shifted(self.me, self.order[2], by)

    def add(self, spot, full, sources):
        acc = self.acc

        def one(number, carry):
            index, inner = decode(number, spot, full)
            for first, rows, terms in sources:
                here = index + (pl.ds(first, rows),)
                total = acc[here]
                if len(terms) > 1:
                    total = total.astype(F32)
                for ref, lead, base in terms:
                    term = ref[(lead,) + inner + (pl.ds(base, rows),)]
                    total += term.astype(total.dtype)
                acc[here] = total.astype(acc.dtype)
            return carry

        lax.fori_loop(0, math.prod(bundle_shape(full)), one, 0)

    def stage_far(self):
        spot = self.chunk(2)
        for way, by in enumerate((1, -1)):
            self.copies.start(
                ("far", by),
                view(self.acc, spot, self.full, None, pl.ds(way * self.half, self.half)),
                self.fars.at[way],
                device_at(self.chunk(by)),
            )

    def stage_near(self):
        half = self.half
        for way, by in enumerate((1, -1)):
            spot = self.chunk(by)
            self.copies.arrived(("far", by))
            self.add(spot, self.full, [(way * half, half, [(self.fars, way, 0)])])
            self.copies.start(
                ("near", by),
                view(self.acc, spot, self.full),
                self.nears.at[way],
                device_at(spot),
            )

    def spread(self, name, axis, full, target):
        for number, by in enumerate(STEPS):
            spot = shifted(self.me, axis, by)
            self.copies.start(
                (name, by), view(self.acc, spot, full), target.at[number], device_at(spot)
            )

    def stage_mid(self):
        self.copies.arrived(("near", 1))
        self.copies.arrived(("near", -1))
        terms = [(self.nears, 0, 0), (self.nears, 1, 0)]
        self.add(self.me, self.full, [(0, 2 * self.half, terms)])
        self.spread("mid", self.order[1], self.order[0], self.mid)

    def stage_tail(self):
        for by in STEPS:
            self.copies.arrived(("mid", by))
        terms = [(self.mid, number, 0) for number in range(3)]
        self.add(self.me, self.order[0], [(0, 2 * self.half, terms)])
        self.spread("tail", self.order[0], "", self.tail)

    def stage_out(self):
        for by in STEPS:
            self.copies.arrived(("tail", by))
        index, _ = decode(0, self.me, "")
        total = self.acc[index].astype(F32)
        for number in range(3):
            total += self.tail[number].astype(F32)
        return total

    def sent(self):
        self.copies.sent()


def reduce_scratch(order, lanes):
    full = bundle_shape(order[:2])
    return [
        pltpu.VMEM((4, 2, 2, 4, 64, lanes), BF16),
        pltpu.VMEM((2,) + full + (64, lanes), BF16),
        pltpu.VMEM((2,) + full + (32, lanes), BF16),
        pltpu.VMEM((3,) + bundle_shape(order[:1]) + (64, lanes), BF16),
        pltpu.VMEM((3, 64, lanes), BF16),
    ]


class Totals:
    def __init__(self, me, sums, inbox, send, recv):
        self.rounds = [[shifted(me, axis, by) for by in STEPS] for axis in "xyz"] + [[sibling(me)]]
        self.sums, self.inbox, self.send, self.recv = sums, inbox, send, recv
        self.made = {}

    def speak(self, number):
        for i, spot in enumerate(self.rounds[number]):
            copy = pltpu.make_async_remote_copy(
                self.sums.at[number],
                self.inbox.at[number, i],
                self.send.at[number, i],
                self.recv.at[number, i],
                device_id=device_at(spot),
                device_id_type=MESH,
            )
            copy.start()
            self.made[number, i] = copy

    def hear(self, number):
        total = self.sums[number]
        for i in range(len(self.rounds[number])):
            self.made[number, i].wait_recv()
            total += self.inbox[number, i]
        self.sums[number + 1] = total

    def pass_on(self, number):
        self.hear(number)
        self.speak(number + 1)

    def sent(self):
        for copy in self.made.values():
            copy.wait_send()


def norm_stats(values):
    average = jnp.mean(values, -1, keepdims=True)
    centered = values - average
    inverse = lax.rsqrt(jnp.mean(centered * centered, -1, keepdims=True) + EPSILON)
    return (centered * inverse, inverse)


def norm_back(upstream, normed, inverse, gain_vector):
    scaled = upstream * gain_vector
    return inverse * (
        scaled
        - jnp.mean(scaled, -1, keepdims=True)
        - normed * jnp.mean(scaled * normed, -1, keepdims=True)
    )


def softmax_columns(key_rows, queries, hidden):
    scores = mm(key_rows, queries, NT) + hidden
    powers = jnp.exp((scores - jnp.max(scores, 0, keepdims=True)) * SCALE)
    return powers * (1.0 / jnp.sum(powers, 0, keepdims=True))


def hidden_rows(seq, slot, tokens):
    row = lax.broadcasted_iota(jnp.int32, (seq, 1), 0)
    return jnp.where(lax.rem(row, slot) < tokens, 0.0, -1e30)


def head_lanes(head):
    lane = lax.broadcasted_iota(jnp.int32, (1, 128), 1)
    return jnp.where(lane // HD == head, 1.0, 0.0).astype(BF16)


def thirds(rows):
    return [rows[:, 128 * i : 128 * i + 128] for i in range(3)]


def attend(rows, hidden):
    queries, key_rows, value_rows = thirds(rows)

    def one_head(head, before):
        mine = head_lanes(head)
        probs = softmax_columns(key_rows, queries * mine, hidden).astype(BF16)
        return before + mm(probs, value_rows * mine, TN)

    return lax.fori_loop(0, 2, one_head, jnp.zeros(queries.shape, F32)).astype(BF16)


def attend_back(rows, grads, hidden):
    queries, key_rows, value_rows = thirds(rows)

    def one_head(head, before):
        mine = head_lanes(head)
        own_grads, own_queries = grads * mine, queries * mine
        probs = softmax_columns(key_rows, own_queries, hidden)
        d_probs = mm(value_rows, own_grads, NT)
        inner = jnp.sum(probs * d_probs, 0, keepdims=True)
        d_scores = (probs * (d_probs - inner)).astype(BF16)
        return (
            before[0] + mm(d_scores, key_rows * mine, TN),
            before[1] + mm(d_scores, own_queries),
            before[2] + mm(probs.astype(BF16), own_grads),
        )

    zero = jnp.zeros(queries.shape, F32)
    d_queries, d_keys, d_values = lax.fori_loop(0, 2, one_head, (zero, zero, zero))
    return [
        (d_queries * SCALE).astype(BF16),
        (d_keys * SCALE).astype(BF16),
        d_values.astype(BF16),
    ]


def padded_rows(ref, target):
    micro, tokens, width = ref.shape
    for m in range(micro):
        target[m, :tokens] = ref[m].astype(F32)
        target[m, tokens:] = jnp.zeros((target.shape[1] - tokens, width), F32)


def blocks_of(ref, index):
    value = ref[index // 2, lax.rem(index, 2)]
    return value.reshape(-1, value.shape[-1])


def half_planes(ref, value, kind, count):
    padded = jnp.concatenate(
        [value, jnp.zeros((ref.shape[-1] - count, value.shape[1]), value.dtype)], axis=0
    )
    ref[kind] = padded.T.reshape(ref.shape[1:])


def forward_kernel(*refs):
    (
        x_ref,
        cot_ref,
        valid_ref,
        qkv_in,
        out_in,
        fc1_in,
        fc2_in,
        small_in,
        result_out,
        d_middle_out,
        vectors,
        sums_out,
        d_attended_out,
        images_out,
        attended_out,
        turned_out,
        act_out,
        dup_out,
        qkv_out,
        rows,
        upstream,
        wq,
        wk,
        wv,
        wide_y,
        wide_x,
        wide_z,
        stage_y,
        stage_x,
        stage_z,
        small,
        bias,
        hidden_bias,
        low,
        outbox,
        images,
        attended_box,
        attended,
        middle,
        normed_two,
        low_two,
        upstream_low,
        turned,
        forward_sum,
        back_sum,
        act_box,
        dup_box,
        hidden_sums,
        local_sem,
        gather_send,
        gather_recv,
        send_sem,
        recv_sem,
        back_send,
        back_recv,
        store_sem,
        sib_send,
        sib_recv,
        ff_local,
        ff_send,
        ff_recv,
    ) = refs
    me = place()
    f, t = lax.axis_index("fsdp"), lax.axis_index("tp")
    core = me["c"]
    other = device_at(sibling(me))
    micro, tokens, width = x_ref.shape
    slot = rows.shape[1]
    count = micro * slot
    greet(me)
    heads = [wq, wk, wv]

    def gather(i, order, block, out):
        return Gather(
            me, order, block, out, gather_send.at[i], gather_recv.at[i], local_sem.at[i]
        )

    narrow = [gather(i, ORDERS[i], qkv_in.at[i], heads[i]) for i in range(3)]
    vector = gather(3, ORDERS[0], small_in, small)
    part_y = gather(4, ORDERS[2], stage_y, wide_y)
    part_x = gather(5, ORDERS[1], stage_x, wide_x)
    part_z = gather(6, ORDERS[0], stage_z, wide_z)
    wide = [part_z, part_y, part_x]
    early = [vector] + narrow
    stores = []

    def store(src, dst):
        copy = pltpu.make_async_copy(src, dst, store_sem.at[len(stores)])
        copy.start()
        stores.append(copy)

    shared = []

    def share(src, dst):
        slot_of = len(shared)
        copy = pltpu.make_async_remote_copy(
            src,
            dst,
            sib_send.at[slot_of],
            sib_recv.at[slot_of],
            device_id=other,
            device_id_type=MESH,
        )
        copy.start()
        shared.append(copy)

    def turn(kind, value):
        half_planes(turned, value, kind, count)
        store(turned.at[kind, :, core], turned_out.at[kind, 0])
        share(turned.at[kind, :, 1 - core], turned_out.at[kind, 1])

    for part in early:
        part.first()
    padded_rows(x_ref, rows)
    normed, _ = norm_stats(rows[...].reshape(count, width))
    for part in early:
        part.second()
    fc2_t = fc2_in[...].T
    stage_y[:, :512] = fc1_in[...]
    stage_y[:, 512:] = fc2_t[:, :128]
    stage_x[...] = fc2_t[:, 128:384]
    stage_z[:, :128] = fc2_t[:, 384:]
    stage_z[:, 128:] = out_in[...].T
    for part in early:
        part.thirds()
    for part in wide:
        part.first()
    for part in early:
        part.far()
    for part in wide:
        part.second()
    vector.last()
    vector.done()
    table = jnp.sum(small[...].reshape(128, 32, 128).astype(F32), 1).astype(BF16)
    lane = lax.broadcasted_iota(jnp.int32, (128, 1024), 0)
    column = lax.broadcasted_iota(jnp.int32, (128, 1024), 1)
    owner = jnp.where(lax.rem(lane, 16) * 8 + lane // 16 == column // 8, 1.0, 0.0)
    for v in range(6):
        pick = jnp.where(lane == v * 8 + lax.rem(column, 8), 1.0, 0.0).astype(BF16)
        vectors[v : v + 1, :] = jnp.sum(mm(table, pick) * owner, 0, keepdims=True)
    vectors[6:8, :] = jnp.zeros((2, 1024), F32)

    def spread_bias(lanes, first):
        lane = lax.broadcasted_iota(jnp.int32, (128, lanes), 0)
        column = lax.broadcasted_iota(jnp.int32, (128, lanes), 1)
        pick = lane == first + (column // 64) * 4 + lax.rem(column, 4)
        owner = lax.rem(lane, 16) == lax.rem(column, 64) // 4
        values = mm(table, jnp.where(pick, 1.0, 0.0).astype(BF16))
        return jnp.sum(jnp.where(owner, values, 0.0).reshape(8, 16, lanes), 1)

    hidden_value = spread_bias(512, 64)
    query_bias, value_bias = spread_bias(128, 48), spread_bias(128, 56)
    for i in range(GROUP):
        hidden_bias[i] = hidden_value[i : i + 1]
        bias[i, :, 0:128] = query_bias[i : i + 1]
        bias[i, :, 128:256] = jnp.zeros((1, 128), F32)
        bias[i, :, 256:384] = value_bias[i : i + 1]
    low[...] = (normed * vectors[0:1, :] + vectors[1:2, :]).astype(BF16)
    for part in narrow:
        part.last()
    for part in wide:
        part.thirds()
    for part in narrow:
        part.done()

    def letter(k, m):
        target = lax.rem(t + k + 1, GROUP)
        return pltpu.make_async_remote_copy(
            outbox.at[target, m],
            images.at[t, m],
            send_sem.at[k, m],
            recv_sem.at[k, m],
            device_id=(f, target),
            device_id_type=MESH,
        )

    def project(k, carry):
        target = lax.rem(t + k + 1, GROUP)
        weights = jnp.concatenate([blocks_of(w, target) for w in heads], axis=1)
        result = (mm(low[...], weights) + bias[target]).astype(BF16)
        outbox[target] = result.reshape(outbox.shape[1:])

        @pl.when(k < GROUP - 1)
        def _():
            letter(k, 0).start()

        return carry

    lax.fori_loop(0, GROUP, project, 0)
    for m in range(1, MICRO):
        for k in range(GROUP - 1):
            letter(k, m).start()
    own = pltpu.make_async_copy(outbox.at[t], images.at[t], local_sem.at[7])
    own.start()
    for i in range(3):
        store(heads[i], qkv_out.at[i])
    for part in wide:
        part.far((0,))
    turn(0, low[...])
    for m in range(micro):
        scale = valid_ref[m, 0].astype(F32)
        upstream[m, :tokens] = cot_ref[m].astype(F32) * scale
        upstream[m, tokens:] = jnp.zeros((slot - tokens, width), F32)
    upstream_rows = upstream[...].reshape(count, width)
    sums_out[3:4, :] = jnp.sum(upstream_rows, 0, keepdims=True)
    upstream_low[...] = upstream_rows.astype(BF16)
    turn(1, upstream_low[...])
    own.wait()
    hidden = hidden_rows(GROUP * slot, slot, tokens)

    def reply(m, k):
        target = lax.rem(t + k + 1, GROUP)
        return pltpu.make_async_remote_copy(
            attended_box.at[m, target],
            attended.at[t, m],
            back_send.at[m, k],
            back_recv.at[m, k],
            device_id=(f, target),
            device_id_type=MESH,
        )

    for m in range(MICRO):
        for k in range(GROUP - 1):
            letter(k, m).wait_recv()
        result = attend(images[:, m].reshape(GROUP * slot, 384), hidden)
        attended_box[m] = result.reshape(GROUP, slot, 128)
        for k in range(GROUP - 1):
            reply(m, k).start()
        attended[t, m] = attended_box[m, t]
        if m < MICRO - 1:
            for part in wide:
                part.far((1, 2, 3)[2 * m : 2 * m + 2])
    store(images, images_out)
    part_z.last()
    for m in range(MICRO):
        for k in range(GROUP - 1):
            reply(m, k).wait_recv()
    store(attended, attended_out.at[0])
    share(attended, attended_out.at[1])
    part_z.done()
    part_y.last()
    part_x.last()
    middle[...] = rows[...].reshape(count, width) + vectors[2:3, :]

    def out_weights(pair):
        both = [blocks_of(wide_z, 2 * pair + i)[:, 128:] for i in range(2)]
        return jnp.concatenate(both, axis=1)

    def out_project(pair, carry):
        both = [attended[2 * pair + i].reshape(count, 128) for i in range(2)]
        middle[...] += mm(jnp.concatenate(both, axis=1), out_weights(pair), NT)
        return carry

    lax.fori_loop(0, GROUP // 2, out_project, 0)
    normed, inverse = norm_stats(middle[...])
    normed_two[...] = normed
    low_two[...] = (normed * vectors[3:4, :] + vectors[4:5, :]).astype(BF16)
    turn(2, low_two[...])
    forward_sum[...] = jnp.zeros_like(forward_sum)
    back_sum[...] = jnp.zeros_like(back_sum)
    part_y.done()
    part_x.done()

    def copies(i):
        result = []
        for n, (box, out) in enumerate(((act_box, act_out), (dup_box, dup_out))):
            result.append(pltpu.make_async_copy(box.at[i], out.at[0, i], ff_local.at[n, i]))
            result.append(
                pltpu.make_async_remote_copy(
                    box.at[i],
                    out.at[1, i],
                    ff_send.at[n, i],
                    ff_recv.at[n, i],
                    device_id=other,
                    device_id_type=MESH,
                )
            )
        return result

    def feed_forward(i, carry):
        first = blocks_of(wide_y, i)
        up_weight = first[:, :512]
        down_weight = jnp.concatenate(
            [first[:, 512:], blocks_of(wide_x, i), blocks_of(wide_z, i)[:, :128]], axis=1
        )
        up_proj = mm(low_two[...], up_weight) + hidden_bias[i]
        gate = jax.nn.sigmoid(1.702 * up_proj)
        activated = (up_proj * gate).astype(BF16)
        d_act = mm(upstream_low[...], down_weight)
        d_up = (d_act * (gate + 1.702 * up_proj * gate * (1.0 - gate))).astype(BF16)
        for j in range(4):
            act_box[i, count * j : count * (j + 1)] = activated[:, 128 * j : 128 * (j + 1)]
            dup_box[i, count * j : count * (j + 1)] = d_up[:, 128 * j : 128 * (j + 1)]
        for copy in copies(i):
            copy.start()
        hidden_sums[i] = jnp.sum(d_up.astype(F32), 0, keepdims=True)
        forward_sum[...] += mm(activated, down_weight, NT)
        back_sum[...] += mm(d_up, up_weight, NT)
        return carry

    lax.fori_loop(0, GROUP, feed_forward, 0)
    d_norm = back_sum[...]
    normed = normed_two[...]
    d_middle = upstream[...].reshape(count, width) + norm_back(
        d_norm, normed, inverse, vectors[3:4, :]
    )
    d_middle_out[...] = d_middle
    low[...] = d_middle.astype(BF16)

    def project_back(pair, carry):
        both = mm(low[...], out_weights(pair)).astype(BF16)
        for i in range(2):
            d_attended_out[2 * pair + i] = both[:, 128 * i : 128 * i + 128].reshape(
                d_attended_out.shape[1:]
            )
        return carry

    lax.fori_loop(0, GROUP // 2, project_back, 0)
    turn(3, low[...])
    sums_out[0:1, :] = jnp.sum(d_middle, 0, keepdims=True)
    sums_out[1:2, :] = jnp.sum(d_norm * normed, 0, keepdims=True)
    sums_out[2:3, :] = jnp.sum(d_norm, 0, keepdims=True)
    for i in range(GROUP):
        at = 4 + i // 2
        sums_out[at : at + 1, 512 * (i % 2) : 512 * (i % 2) + 512] = hidden_sums[i]
    output = (middle[...] + forward_sum[...] + vectors[5:6, :]).reshape(rows.shape)
    result_out[...] = output[:, :tokens].astype(BF16)
    for copy in shared:
        copy.wait()
    for i in range(GROUP):
        for copy in copies(i):
            copy.wait()
    for part in early + wide:
        part.sent()
    for k in range(GROUP - 1):
        for m in range(MICRO):
            letter(k, m).wait_send()
            reply(m, k).wait_send()
    for copy in stores:
        copy.wait()


ANY = pl.BlockSpec(memory_space=pl.ANY)
VMEM = pl.BlockSpec(memory_space=pltpu.VMEM)
SMEM = pl.BlockSpec(memory_space=pltpu.SMEM)
WIDE = (640, 256, 256)


def forward(x, cotangent, valid, qkv_block, out_block, fc1_block, fc2_block, small, slot):
    width = x.shape[-1]
    count = MICRO * slot
    images = (GROUP, MICRO, slot, 384)
    attended = (GROUP, MICRO, slot, 128)
    acts = (2, GROUP, 4 * count, 128)
    return pl.pallas_call(
        forward_kernel,
        out_shape=[
            jax.ShapeDtypeStruct(x.shape, BF16),
            jax.ShapeDtypeStruct((count, width), F32),
            jax.ShapeDtypeStruct((8, width), F32),
            jax.ShapeDtypeStruct((8, width), F32),
            jax.ShapeDtypeStruct(attended, BF16),
            jax.ShapeDtypeStruct(images, BF16),
            jax.ShapeDtypeStruct((2,) + attended, BF16),
            jax.ShapeDtypeStruct((4, 2, 8, 64, 256), BF16),
            jax.ShapeDtypeStruct(acts, BF16),
            jax.ShapeDtypeStruct(acts, BF16),
            jax.ShapeDtypeStruct((3,) + LEAD + (64, 128), BF16),
        ],
        in_specs=[VMEM, VMEM, SMEM, ANY, VMEM, VMEM, VMEM, ANY],
        out_specs=[VMEM] * 5 + [ANY] * 6,
        scratch_shapes=[
            pltpu.VMEM((MICRO, slot, width), F32),
            pltpu.VMEM((MICRO, slot, width), F32),
            pltpu.VMEM(LEAD + (64, 128), BF16),
            pltpu.VMEM(LEAD + (64, 128), BF16),
            pltpu.VMEM(LEAD + (64, 128), BF16),
            pltpu.VMEM(LEAD + (64, WIDE[0]), BF16),
            pltpu.VMEM(LEAD + (64, WIDE[1]), BF16),
            pltpu.VMEM(LEAD + (64, WIDE[2]), BF16),
            pltpu.VMEM((64, WIDE[0]), BF16),
            pltpu.VMEM((64, WIDE[1]), BF16),
            pltpu.VMEM((64, WIDE[2]), BF16),
            pltpu.VMEM(LEAD + (32, 128), BF16),
            pltpu.VMEM((GROUP, 1, 384), F32),
            pltpu.VMEM((GROUP, 1, 512), F32),
            pltpu.VMEM((count, width), BF16),
            pltpu.VMEM(images, BF16),
            pltpu.VMEM(images, BF16),
            pltpu.VMEM((MICRO, GROUP, slot, 128), BF16),
            pltpu.VMEM(attended, BF16),
            pltpu.VMEM((count, width), F32),
            pltpu.VMEM((count, width), F32),
            pltpu.VMEM((count, width), BF16),
            pltpu.VMEM((count, width), BF16),
            pltpu.VMEM((4, 8, 2, 64, 256), BF16),
            pltpu.VMEM((count, width), F32),
            pltpu.VMEM((count, width), F32),
            pltpu.VMEM(acts[1:], BF16),
            pltpu.VMEM(acts[1:], BF16),
            pltpu.VMEM((GROUP, 1, 512), F32),
            pltpu.SemaphoreType.DMA((8,)),
            pltpu.SemaphoreType.DMA((7, Gather.slots)),
            pltpu.SemaphoreType.DMA((7, Gather.slots)),
            pltpu.SemaphoreType.DMA((GROUP, MICRO)),
            pltpu.SemaphoreType.DMA((GROUP, MICRO)),
            pltpu.SemaphoreType.DMA((MICRO, GROUP)),
            pltpu.SemaphoreType.DMA((MICRO, GROUP)),
            pltpu.SemaphoreType.DMA((9,)),
            pltpu.SemaphoreType.DMA((5,)),
            pltpu.SemaphoreType.DMA((5,)),
            pltpu.SemaphoreType.DMA((2, GROUP)),
            pltpu.SemaphoreType.DMA((2, GROUP)),
            pltpu.SemaphoreType.DMA((2, GROUP)),
        ],
        compiler_params=pltpu.CompilerParams(
            collective_id=0, has_side_effects=True, vmem_limit_bytes=VMEM_LIMIT
        ),
        name="forward",
    )(x, cotangent, valid, qkv_block, out_block, fc1_block, fc2_block, small)


def backward_kernel(*refs):
    (
        d_attended_in,
        images_in,
        attended_in,
        turned_in,
        act_in,
        dup_in,
        qkv_in,
        d_middle_ref,
        x_ref,
        vectors_ref,
        sums_ref,
        input_grad_out,
        qkv_grad,
        out_grad,
        fc1_grad,
        fc2_grad,
        totals_out,
        rows,
        pool,
        turned,
        attended,
        images,
        d_attended,
        outbox,
        d_images,
        d_norm,
        down_grad,
        sums,
        sums_in,
        *rest,
    ) = refs
    scratch, sems = rest[:30], rest[30:]
    (
        load_sem,
        reduce_send,
        reduce_recv,
        send_sem,
        recv_sem,
        back_send,
        back_recv,
        sib_send,
        sib_recv,
        sum_send,
        sum_recv,
    ) = sems
    me = place()
    f, t = lax.axis_index("fsdp"), lax.axis_index("tp")
    other = device_at(sibling(me))
    greet(me)
    tokens, slot = x_ref.shape[1], rows.shape[1]
    count = MICRO * slot
    parts = [
        Reduce(
            me,
            REDUCED[i][0],
            *scratch[5 * i : 5 * i + 5],
            reduce_send.at[i],
            reduce_recv.at[i],
        )
        for i in range(6)
    ]
    part_y, part_x, part_z = parts[:3]
    late = parts[3:]
    totals = [
        Totals(me, sums.at[i], sums_in.at[i], sum_send.at[i], sum_recv.at[i]) for i in range(2)
    ]

    def letter(k, m):
        target = lax.rem(t + k + 1, GROUP)
        return pltpu.make_async_remote_copy(
            d_attended_in.at[target, m],
            d_attended.at[t, m],
            send_sem.at[k, m],
            recv_sem.at[k, m],
            device_id=(f, target),
            device_id_type=MESH,
        )

    for m in range(MICRO):
        for k in range(GROUP - 1):
            letter(k, m).start()
    loads = {}

    def load(name, src, dst):
        loads[name] = pltpu.make_async_copy(src, dst, load_sem.at[len(loads)])
        loads[name].start()

    kept = pl.ds(0, 4 * count)
    load("turned", turned_in, turned)
    for i in range(2):
        load(("dup", i), dup_in.at[i], pool.at[2 + i, :, kept])
    for i in range(2):
        load(("act", i), act_in.at[i], pool.at[i, :, kept])
    load("attended", attended_in, attended)
    load("images", images_in, images)
    load("own", d_attended_in.at[t], d_attended.at[t])
    sums[0, 0] = sums_ref[...]
    totals[0].speak(0)
    loads["turned"].wait()

    def both_cores(kind, values):
        total = 0.0
        for i in range(2):
            left = turned[kind, i].reshape(512, 256)[:, :count]
            total += mm(left, values[i])
        return total.astype(BF16)

    def pooled(first, index, lanes):
        return [
            jnp.concatenate(
                [pool[first + i, index, count * j : count * (j + 1)] for j in lanes], axis=1
            )
            for i in range(2)
        ]

    def spot_of(index):
        return (index // 2, lax.rem(index, 2))

    def grads_y(index, carry):
        up = both_cores(2, pooled(2, index, range(4)))
        down = both_cores(1, pooled(0, index, (0,)))
        acc = part_y.acc
        acc[spot_of(index)] = jnp.concatenate([up, down], axis=1).reshape(acc.shape[2:])
        return carry

    def grads_xz(index, carry):
        down = both_cores(1, pooled(0, index, (1, 2, 3)))
        out = both_cores(3, [attended[i, index].reshape(count, 128) for i in range(2)])
        acc = part_x.acc
        acc[spot_of(index)] = down[:, :256].reshape(acc.shape[2:])
        acc = part_z.acc
        acc[spot_of(index)] = jnp.concatenate([down[:, 256:], out], axis=1).reshape(acc.shape[2:])
        return carry

    for i in range(2):
        loads["dup", i].wait()
        loads["act", i].wait()
    lax.fori_loop(0, GROUP, grads_y, 0)
    part_y.stage_far()
    loads["attended"].wait()
    lax.fori_loop(0, GROUP, grads_xz, 0)
    part_x.stage_far()
    part_z.stage_far()
    for i in range(3):
        load(("weight", i), qkv_in.at[i], pool.at[i])
    totals[0].pass_on(0)
    loads["images"].wait()
    loads["own"].wait()
    hidden = hidden_rows(GROUP * slot, slot, tokens)

    def reply(m, k):
        target = lax.rem(t + k + 1, GROUP)
        return pltpu.make_async_remote_copy(
            outbox.at[m, target],
            d_images.at[0, t, m],
            back_send.at[m, k],
            back_recv.at[m, k],
            device_id=(f, target),
            device_id_type=MESH,
        )

    for m in range(MICRO):
        for k in range(GROUP - 1):
            letter(k, m).wait_recv()
        results = attend_back(
            images[:, m].reshape(GROUP * slot, 384),
            d_attended[:, m].reshape(GROUP * slot, 128),
            hidden,
        )
        for i in range(3):
            outbox[m, :, :, 128 * i : 128 * i + 128] = results[i].reshape(GROUP, slot, 128)
        for k in range(GROUP - 1):
            reply(m, k).start()
        d_images[0, t, m] = outbox[m, t]
        if m == 0:
            part_y.stage_near()
            totals[0].pass_on(1)
        if m == 1:
            totals[0].pass_on(2)
    part_x.stage_near()
    part_z.stage_near()
    padded_rows(x_ref, rows)
    normed, inverse = norm_stats(rows[...].reshape(count, rows.shape[-1]))
    totals[0].hear(3)
    part_y.stage_mid()

    def share(k):
        source = lax.rem(t + k + 1, GROUP)
        return pltpu.make_async_remote_copy(
            d_images.at[0, source],
            d_images.at[1, source],
            sib_send.at[k],
            sib_recv.at[k],
            device_id=other,
            device_id_type=MESH,
        )

    share(GROUP - 1).start()
    for k in reversed(range(GROUP - 1)):
        for m in range(MICRO):
            reply(m, GROUP - 2 - k).wait_recv()
        share(k).start()
    for k in range(GROUP):
        share(k).wait_recv()

    def grads_late(index, carry):
        result = both_cores(0, [d_images[i, index].reshape(count, 384) for i in range(2)])
        for i, part in enumerate(late):
            part.acc[spot_of(index)] = result[:, 128 * i : 128 * i + 128].reshape(
                part.acc.shape[2:]
            )
        return carry

    lax.fori_loop(0, GROUP, grads_late, 0)
    for part in late:
        part.stage_far()
    part_x.stage_mid()
    part_z.stage_mid()
    for i in range(3):
        loads["weight", i].wait()
    d_norm[...] = jnp.zeros_like(d_norm)

    def project_back(index, carry):
        weights = jnp.concatenate([pool[i, index] for i in range(3)], axis=1)
        d_norm[...] += mm(d_images[0, index].reshape(count, 384), weights, NT)
        return carry

    lax.fori_loop(0, GROUP, project_back, 0)
    part_y.stage_tail()
    for part in late:
        part.stage_near()
    gradient = d_norm[...]
    sums[1, 0, 0:1, :] = jnp.sum(gradient * normed, 0, keepdims=True)
    sums[1, 0, 1:2, :] = jnp.sum(gradient, 0, keepdims=True)
    for index in range(GROUP):
        grads = jnp.sum(d_images[0, index].reshape(count, 384).astype(F32), 0, keepdims=True)
        sums[1, 0, 2:3, 128 * index : 128 * index + 128] = grads[:, :128]
        sums[1, 0, 3:4, 128 * index : 128 * index + 128] = grads[:, 256:]
    sums[1, 0, 4:8, :] = jnp.zeros((4, sums.shape[-1]), F32)
    totals[1].speak(0)
    part_x.stage_tail()
    part_z.stage_tail()
    result = d_middle_ref[...] + norm_back(gradient, normed, inverse, vectors_ref[0:1, :])
    input_grad_out[...] = result.reshape(rows.shape)[:, :tokens].astype(BF16)
    totals[1].pass_on(0)
    for part in late:
        part.stage_mid()
    totals[1].pass_on(1)
    wide = part_y.stage_out()
    fc1_grad[...] = wide[:, :512]
    down_grad[:, :128] = wide[:, 512:]
    down_grad[:, 128:384] = part_x.stage_out()
    wide = part_z.stage_out()
    down_grad[:, 384:] = wide[:, :128]
    out_grad[...] = wide[:, 128:].T
    fc2_grad[...] = down_grad[...].T
    for part in late:
        part.stage_tail()
    totals[1].pass_on(2)
    for i in range(3):
        qkv_grad[i] = late[i].stage_out()
    totals[1].hear(3)
    totals_out[0:8, :] = sums[0, 4]
    totals_out[8:16, :] = sums[1, 4]
    for part in parts:
        part.sent()
    for total in totals:
        total.sent()
    for k in range(GROUP):
        share(k).wait_send()
    for k in range(GROUP - 1):
        for m in range(MICRO):
            letter(k, m).wait_send()
            reply(m, k).wait_send()


REDUCED = (
    (ORDERS[2], WIDE[0]),
    (ORDERS[1], WIDE[1]),
    (ORDERS[0], WIDE[2]),
    (ORDERS[0], 128),
    (ORDERS[1], 128),
    (ORDERS[2], 128),
)


def backward(d_attended, images, attended, turned, act, dup, qkv, d_middle, x, vectors, sums, slot):
    width = x.shape[-1]
    count = MICRO * slot
    scratch = []
    for order, lanes in REDUCED:
        scratch += reduce_scratch(order, lanes)
    return pl.pallas_call(
        backward_kernel,
        out_shape=[
            jax.ShapeDtypeStruct(x.shape, BF16),
            jax.ShapeDtypeStruct((3, 64, 128), F32),
            jax.ShapeDtypeStruct((128, 64), F32),
            jax.ShapeDtypeStruct((64, 512), F32),
            jax.ShapeDtypeStruct((512, 64), F32),
            jax.ShapeDtypeStruct((16, width), F32),
        ],
        in_specs=[ANY] * 7 + [VMEM] * 4,
        out_specs=[VMEM] * 6,
        scratch_shapes=[
            pltpu.VMEM((MICRO, slot, width), F32),
            pltpu.VMEM((4, GROUP, width, 128), BF16),
            pltpu.VMEM(turned.shape, BF16),
            pltpu.VMEM(attended.shape, BF16),
            pltpu.VMEM(images.shape, BF16),
            pltpu.VMEM(d_attended.shape, BF16),
            pltpu.VMEM((MICRO, GROUP, slot, 384), BF16),
            pltpu.VMEM((2,) + images.shape, BF16),
            pltpu.VMEM((count, width), F32),
            pltpu.VMEM((64, 512), F32),
            pltpu.VMEM((2, 5, 8, width), F32),
            pltpu.VMEM((2, 4, 3, 8, width), F32),
        ]
        + scratch
        + [
            pltpu.SemaphoreType.DMA((11,)),
            pltpu.SemaphoreType.DMA((6, Reduce.slots)),
            pltpu.SemaphoreType.DMA((6, Reduce.slots)),
            pltpu.SemaphoreType.DMA((GROUP, MICRO)),
            pltpu.SemaphoreType.DMA((GROUP, MICRO)),
            pltpu.SemaphoreType.DMA((MICRO, GROUP)),
            pltpu.SemaphoreType.DMA((MICRO, GROUP)),
            pltpu.SemaphoreType.DMA((GROUP,)),
            pltpu.SemaphoreType.DMA((GROUP,)),
            pltpu.SemaphoreType.DMA((2, 4, 3)),
            pltpu.SemaphoreType.DMA((2, 4, 3)),
        ],
        compiler_params=pltpu.CompilerParams(
            collective_id=1, has_side_effects=True, vmem_limit_bytes=VMEM_LIMIT
        ),
        name="backward",
    )(d_attended, images, attended, turned, act, dup, qkv, d_middle, x, vectors, sums)


def per_device(
    inputs,
    cotangent,
    valid_slots,
    ln1_gain,
    ln1_bias,
    qkv_weight,
    qv_bias,
    out_weight,
    out_bias,
    ln2_gain,
    ln2_bias,
    fc1_weight,
    fc1_bias,
    fc2_weight,
    fc2_bias,
):
    micro, _, tokens, width = inputs.shape
    slot = -(-tokens // 16) * 16
    x = inputs.reshape(micro, tokens, width)
    small = jnp.concatenate(
        [ln1_gain, ln1_bias, out_bias, ln2_gain, ln2_bias, fc2_bias]
        + [qv_bias.reshape(-1), fc1_bias.reshape(-1)]
    )
    small = jnp.pad(small.reshape(1, 96), ((0, 31), (0, 32)))
    (
        result,
        d_middle,
        vectors,
        sums,
        d_attended,
        images,
        attended,
        turned,
        act,
        dup,
        qkv,
    ) = forward(
        x,
        cotangent.reshape(x.shape),
        valid_slots,
        qkv_weight,
        out_weight,
        fc1_weight,
        fc2_weight,
        small,
        slot,
    )
    input_grad, qkv_grad, out_grad, fc1_grad, fc2_grad, total = backward(
        d_attended,
        images,
        attended,
        turned,
        act,
        dup,
        qkv.reshape(3, GROUP, width, 128),
        d_middle,
        x,
        vectors,
        sums,
        slot,
    )
    f, t = lax.axis_index("fsdp"), lax.axis_index("tp")
    own = lax.dynamic_slice(total, (0, (f * 8 + t) * 8), (16, 8))
    pair = lax.dynamic_slice(total[10:12].reshape(2, 16, 64), (0, 2 * t, 4 * f), (2, 2, 4))
    hidden_grad = lax.dynamic_slice(total[4:8].reshape(64, 64), (8 * t, 4 * f), (8, 4))
    return (
        result.reshape(inputs.shape),
        input_grad.reshape(inputs.shape),
        own[8],
        own[9],
        qkv_grad,
        pair,
        out_grad,
        own[0],
        own[1],
        own[2],
        fc1_grad,
        hidden_grad,
        fc2_grad,
        own[3],
    )


def solution(mesh):
    in_specs = (
        P(None, "fsdp", "tp", None),
        P(None, "fsdp", "tp", None),
        P(None, "fsdp"),
        P(("fsdp", "tp")),
        P(("fsdp", "tp")),
        P(None, "fsdp", "tp"),
        P(None, "tp", "fsdp"),
        P("tp", "fsdp"),
        P(("fsdp", "tp")),
        P(("fsdp", "tp")),
        P(("fsdp", "tp")),
        P("fsdp", "tp"),
        P("tp", "fsdp"),
        P("tp", "fsdp"),
        P(("fsdp", "tp")),
    )
    out_specs = (
        P(None, "fsdp", "tp", None),
        P(None, "fsdp", "tp", None),
        P(("fsdp", "tp")),
        P(("fsdp", "tp")),
        P(None, "fsdp", "tp"),
        P(None, "tp", "fsdp"),
        P("tp", "fsdp"),
        P(("fsdp", "tp")),
        P(("fsdp", "tp")),
        P(("fsdp", "tp")),
        P("fsdp", "tp"),
        P("tp", "fsdp"),
        P("tp", "fsdp"),
        P(("fsdp", "tp")),
    )
    return jax.shard_map(
        per_device, mesh=mesh, in_specs=in_specs, out_specs=out_specs, check_vma=False
    )
```

time: 261 us -> 238 us (0.912)
  Pallas kernels: 232 us -> 213 us
  other arithmetic: 5.86 us -> 0 us
  local copies, waits for them, and re-layouts: 21 us -> 24.2 us
    pallas_call x2 -> x1, Pallas kernels: 122 us -> 111 us  [forward(): pl.pallas_call(forward_kernel, out_shape=[jax.ShapeDtypeStruct(x.shape, B...]
    unnamed x5 -> x13, local copies, waits for them, and re-layouts: 5.91 us -> 14.7 us
    pallas_call x1, Pallas kernels: 109 us -> 102 us  [backward(): pl.pallas_call(backward_kernel, out_shape=[jax.ShapeDtypeStruct(x.shape,...]
    slice x7 -> x2, local copies, waits for them, and re-layouts: 6.05 us -> 1.52 us  [the longest x1 0.76 us: per_device(): total[10:12].reshape(2, 16, 64)]
    concatenate x2 -> x0, other arithmetic: 2.92 us -> none  [the longest x1 1.56 us: per_device(): jnp.concatenate([sum_1, sum_2[:, :128]], axis=1)]
where the time goes in v3:
time: 238 us; the launch traced here: 237 us
  Pallas kernels  213 us (89%)
  local copies, waits for them, and re-layouts  24.2 us (10%)
    pallas_call x1, Pallas kernels, forward(): pl.pallas_call(forward_kernel, out_shape=[jax.ShapeDtypeStruct(x.shape, B...  111 us
    pallas_call x1, Pallas kernels, backward(): pl.pallas_call(backward_kernel, out_shape=[jax.ShapeDtypeStruct(x.shape,...  102 us
    unnamed x13, local copies, waits for them, and re-layouts  14.7 us

profile of v3, /device:TPU:0, one launch (start us, length us, event | category | flops | bytes accessed | tf_op | source)
XLA Modules:
  0.0 237.5 jit_solution(3578018999800780950)
XLA Ops:
  0.6 1.3 copy.39.refs_2_
  2.0 1.4 copy.40.refs_4_
  3.4 1.6 copy.41.refs_6_
  5.0 0.8 reshape.60
  5.8 0.8 copy.38
  6.5 0.1 reshape.61
  6.6 4.1 %concatenate.3 = bf16[96]{0:T(256)(128)(2,1)S(1)} concatenate(bf16[8]{0:T(256)(128)(2,1)} %param.18, bf16[8]{0:T(256)(128)(2,1)} %param.19, bf16[8]{0:T(256)(128)(2,1)} %param.23, bf16[8]{0:T(256)(128)(2,1)} %param.24, bf16[8]{0:T(256)(128)(2,1)} %param.25, bf16[8]{0:T(256)(128)(2,1)} %param.29, bf16[16]{0:T(256)(128)(2,1)S(1)} %reshape.60, bf16[32]{0:T(256)(128)(2,1)S(1)} %reshape.61), dimensions={0} | concatenate | bytes 384 | tf_op jit(solution)/shard_map/concatenate | solution.py:1231
  10.7 0.6 pad.4.refs_7_
  11.3 110.6 %forward.1 = (bf16[3,72,1024]{2,1,0:T(8,128)(2,1)}, f32[240,1024]{1,0:T(8,128)}, f32[8,1024]{1,0:T(8,128)}, f32[8,1024]{1,0:T(8,128)}, bf16[8,3,80,128]{3,2,1,0:...) custom-call(bf16[3,72,1024]{2,1,0:T(8,128)(2,1)} %bitcast.23, ...), custom_call_target="tpu_custom_call" | custom-call | tf_op jit(solution)/shard_map/forward/pallas_call | solution.py:802
  121.9 0.0 copy-start
  121.9 102.1 %backward.1 = (bf16[3,72,1024]{2,1,0:T(8,128)(2,1)}, f32[3,64,128]{2,1,0:T(8,128)}, f32[128,64]{1,0:T(8,128)}, f32[64,512]{1,0:T(8,128)}, f32[512,64]{1,0:T(8,128)}, /*index=5*/f32[16,1024]{1,0:T(8,128)}) custom-call(bf16[8,3,80,128]{3,2,1,0:T(8,128)(2,1)} %get-tuple-element.32.refs_0_, bf16[8,3,80,384]{3,2,1,0:T(8,128)(2,1)} %get-tuple-element.33.refs_1_, ...), custom_call_target="tpu_custom_call" | custom-call | tf_op jit(solution)/shard_map/backward/pallas_call | solution.py:1164
  224.0 1.5 dynamic-slice_bitcast_fusion
  225.5 0.8 slice.26
  226.2 0.1 reshape.66
  226.3 0.7 constant_dynamic-slice_fusion
  227.0 1.5 copy.45
  228.5 0.8 slice.30
  229.3 0.1 reshape.67
  229.4 0.1 dynamic_slice.11
  229.4 0.7 copy.47
  230.1 1.7 copy.46
  231.8 0.0 copy-done
  231.8 0.8 copy.52
  232.6 1.8 copy.53
  234.4 1.5 copy.54
  235.9 1.6 copy.55
Async XLA Ops:
  121.9 109.9 %copy-start = (bf16[3,72,1024]{2,1,0:T(8,128)(2,1)S(1)}, bf16[3,72,1024]{2,1,0:T(8,128)(2,1)}, u32[]{:S(2)}) copy-start(bf16[3,72,1024]{2,1,0:T(8,128)(2,1)} %get-tuple-element.31) | copy-start | bytes 1327108

commit v4 on v3

v4 whole, which is shorter than its diff:
```python
import functools
import math

import jax
import jax.numpy as jnp
from jax import lax
from jax.experimental import pallas as pl
from jax.experimental.pallas import tpu as pltpu
from jax.sharding import PartitionSpec as P

MESH = pl.DeviceIdType.MESH
HD = 64
SCALE = 1.0 / math.sqrt(HD)
EPSILON = 1e-05
BF16 = jnp.bfloat16
F32 = jnp.float32
VMEM_LIMIT = 62 * 2**20
MICRO, GROUP = 3, 8
ORDERS = (("x", "y", "z"), ("y", "z", "x"), ("z", "x", "y"))
SIZES = {"x": (4,), "z": (2, 2), "y": (4,)}
LEAD = (4, 2, 2, 4, 2)
STEPS = (1, -1, 2)
NN = (((1,), (0,)), ((), ()))
NT = (((1,), (1,)), ((), ()))
TN = (((0,), (0,)), ((), ()))


def mm(a, b, dims=NN):
    return lax.dot_general(a, b, dims, preferred_element_type=F32)


def place():
    f, t = lax.axis_index("fsdp"), lax.axis_index("tp")
    return {
        "x": t // 2,
        "y": lax.rem(f // 2, 4),
        "z": (f // 8) * 2 + lax.rem(t, 2),
        "c": lax.rem(f, 2),
    }


def device_at(spot):
    return (
        (spot["z"] // 2) * 8 + spot["y"] * 2 + spot["c"],
        spot["x"] * 2 + lax.rem(spot["z"], 2),
    )


def shifted(spot, axis, by):
    return {**spot, axis: lax.rem(spot[axis] + by + 4, 4)}


def sibling(spot):
    return {**spot, "c": 1 - spot["c"]}


def greet(me):
    f, t = lax.axis_index("fsdp"), lax.axis_index("tp")
    devices = [(f, lax.rem(t + step, GROUP)) for step in range(1, GROUP)]
    devices += [device_at(shifted(me, "y", by)) for by in STEPS]
    devices += [device_at(shifted(me, "z", 2))]
    devices += [device_at(shifted(me, "z", 2 * lax.rem(me["z"], 2) - 1))]
    devices += [device_at(sibling(me))]
    barrier = pltpu.get_barrier_semaphore()
    for device in devices:
        pl.semaphore_signal(barrier, inc=1, device_id=device, device_id_type=MESH)
    return lambda: pl.semaphore_wait(barrier, len(devices))


def view(ref, spot, full, core=None, rows=slice(None)):
    whole = slice(None)
    index = [
        whole if "x" in full else spot["x"],
        whole if "z" in full else lax.rem(spot["z"], 2),
        whole if "z" in full else spot["z"] // 2,
        whole if "y" in full else spot["y"],
    ]
    if core is not None:
        index.append(core)
    return ref.at[tuple(index) + (rows,)]


def decode(number, spot, full):
    at = {}
    for axis in "yzx":
        if axis in full:
            parts = []
            for size in reversed(SIZES[axis]):
                parts.append(lax.rem(number, size))
                number = number // size
            at[axis] = tuple(reversed(parts))
    fixed = {"x": (spot["x"],), "z": (lax.rem(spot["z"], 2), spot["z"] // 2), "y": (spot["y"],)}
    index, inner = (), ()
    for axis in "xzy":
        index += at.get(axis, fixed[axis])
        inner += at.get(axis, ())
    return index, inner


def bundle_shape(full):
    shape = ()
    for axis in "xzy":
        shape += SIZES[axis] if axis in full else ()
    return shape


def remote(src, dst, send, recv, device):
    copy = pltpu.make_async_remote_copy(
        src, dst, send, recv, device_id=device, device_id_type=MESH
    )
    copy.start()
    return copy


def take(ref, semaphore):
    pltpu.make_async_copy(ref, ref, semaphore).wait()


class Gather:
    sends, recvs = 5, 8

    def __init__(self, me, order, block, out, send, recv, local):
        self.me, self.order, self.block, self.out = me, order, block, out
        self.send, self.recv, self.local = send, recv, local
        self.core = me["c"]
        self.half = out.shape[-2] // 2
        self.plane = "".join(order[:2])

    def piece(self, spot, full, rows=slice(None)):
        return view(self.out, spot, full, self.core, rows)

    def spread(self, spot, full, axis, by, send, recv, rows=slice(None)):
        piece = self.piece(spot, full, rows)
        target = device_at(shifted(self.me, axis, by))
        remote(piece, piece, self.send.at[send], self.recv.at[recv], target)

    def share(self, spot):
        piece = self.piece(spot, self.plane)
        remote(piece, piece, self.send.at[4], self.recv.at[7], device_at(sibling(self.me)))

    def own(self):
        return pltpu.make_async_copy(
            self.block, view(self.out, self.me, "", self.core), self.local
        )

    def first(self):
        me, axis = self.me, self.order[0]
        self.own().start()
        for by in STEPS:
            target = device_at(shifted(me, axis, by))
            remote(self.block, self.piece(me, ""), self.send.at[0], self.recv.at[0], target)

    def second(self):
        self.own().wait()
        take(self.out.at[:3, 0, 0, 0, 0], self.recv.at[0])
        for by in STEPS:
            self.spread(self.me, self.order[0], self.order[1], by, 1, 1)

    def rows(self, way):
        return pl.ds(way * self.half, self.half)

    def third(self):
        take(self.out.at[:3, 0, 0, :, 0], self.recv.at[1])
        axis = self.order[2]
        for number, (by, way) in enumerate(((1, 0), (-1, 1), (1, 1), (-1, 0))):
            self.spread(self.me, self.plane, axis, by, 2, 2 + number, self.rows(way))
        self.share(self.me)

    def far(self):
        axis = self.order[2]
        for way, by in enumerate((1, -1)):
            take(self.out.at[:, 0, 0, :, 0, : self.half], self.recv.at[2 + way])
            spot = shifted(self.me, axis, -by)
            self.spread(spot, self.plane, axis, by, 3, 6, self.rows(way))

    def rest(self):
        for way, by in enumerate((1, -1)):
            take(self.out.at[:, 0, 0, :, 0, : self.half], self.recv.at[4 + way])
            self.share(shifted(self.me, self.order[2], -by))

    def last(self):
        take(self.out.at[:, 0, 0, :, 0], self.recv.at[6])
        self.share(shifted(self.me, self.order[2], 2))

    def done(self):
        take(self.out.at[:, :, :, :, 0], self.recv.at[7])

    def sent(self):
        out = self.out
        take(out.at[:3, 0, 0, 0, 0], self.send.at[0])
        take(out.at[:3, 0, 0, :, 0], self.send.at[1])
        take(out.at[:, :, 0, :, 0], self.send.at[2])
        take(out.at[:, 0, 0, :, 0], self.send.at[3])
        take(out.at[:, :, :, :, 0], self.send.at[4])


class Reduce:
    sends, recvs = 4, 5

    def __init__(self, me, order, acc, near, far, mid, tail, send, recv):
        self.me, self.order, self.acc = me, order, acc
        self.nears, self.fars, self.mid, self.tail = near, far, mid, tail
        self.send, self.recv = send, recv
        self.half = acc.shape[-2] // 2
        self.full = "".join(order[:2])

    def chunk(self, by):
        return shifted(self.me, self.order[2], by)

    def rows(self, way):
        return pl.ds(way * self.half, self.half)

    def add(self, spot, full, first, rows, terms):
        acc = self.acc

        def one(number, carry):
            index, inner = decode(number, spot, full)
            here = index + (pl.ds(first, rows),)
            total = acc[here]
            if len(terms) > 1:
                total = total.astype(F32)
            for ref, lead in terms:
                rows_there = pl.ds(first, rows) if ref.shape[-2] == acc.shape[-2] else slice(None)
                total += ref[(lead,) + inner + (rows_there,)].astype(total.dtype)
            acc[here] = total.astype(acc.dtype)
            return carry

        lax.fori_loop(0, math.prod(bundle_shape(full)), one, 0)

    def near(self, by, way):
        spot = self.chunk(by)
        box = self.nears.at[0 if by == 1 else 1]
        lead = (slice(None),) * (len(self.nears.shape) - 3)
        remote(
            view(self.acc, spot, self.full, None, self.rows(way)),
            box.at[lead + (self.rows(way),)],
            self.send.at[1],
            self.recv.at[2],
            device_at(spot),
        )

    def stage_far(self):
        spot = self.chunk(2)
        for way, by in enumerate((1, -1)):
            remote(
                view(self.acc, spot, self.full, None, self.rows(way)),
                self.fars.at[way],
                self.send.at[0],
                self.recv.at[way],
                device_at(self.chunk(by)),
            )
        for way, by in enumerate((1, -1)):
            self.near(by, 1 - way)

    def stage_near(self):
        for way, by in enumerate((1, -1)):
            take(self.fars.at[way], self.recv.at[way])
            self.add(self.chunk(by), self.full, way * self.half, self.half, [(self.fars, way)])
            self.near(by, way)

    def spread(self, axis, full, target, send, recv):
        for number, by in enumerate(STEPS):
            spot = shifted(self.me, axis, by)
            remote(
                view(self.acc, spot, full),
                target.at[number],
                self.send.at[send],
                self.recv.at[recv],
                device_at(spot),
            )

    def stage_mid(self):
        take(self.nears, self.recv.at[2])
        self.add(self.me, self.full, 0, 2 * self.half, [(self.nears, 0), (self.nears, 1)])
        self.spread(self.order[1], self.order[0], self.mid, 2, 3)

    def stage_tail(self):
        take(self.mid, self.recv.at[3])
        self.add(self.me, self.order[0], 0, 2 * self.half, [(self.mid, i) for i in range(3)])
        self.spread(self.order[0], "", self.tail, 3, 4)

    def stage_out(self):
        take(self.tail, self.recv.at[4])
        index, _ = decode(0, self.me, "")
        total = self.acc[index].astype(F32)
        for number in range(3):
            total += self.tail[number].astype(F32)
        return total

    def sent(self):
        take(self.fars, self.send.at[0])
        take(self.nears, self.send.at[1])
        take(self.mid, self.send.at[2])
        take(self.tail, self.send.at[3])


def reduce_scratch(order, lanes):
    full = bundle_shape(order[:2])
    return [
        pltpu.VMEM((4, 2, 2, 4, 64, lanes), BF16),
        pltpu.VMEM((2,) + full + (64, lanes), BF16),
        pltpu.VMEM((2,) + full + (32, lanes), BF16),
        pltpu.VMEM((3,) + bundle_shape(order[:1]) + (64, lanes), BF16),
        pltpu.VMEM((3, 64, lanes), BF16),
    ]


class Totals:
    def __init__(self, me, sums, inbox, send, recv):
        self.rounds = [[shifted(me, axis, by) for by in STEPS] for axis in "xyz"] + [[sibling(me)]]
        self.sums, self.inbox, self.send, self.recv = sums, inbox, send, recv

    def heard(self, number):
        return self.inbox.at[number, pl.ds(0, len(self.rounds[number]))]

    def speak(self, number):
        for i, spot in enumerate(self.rounds[number]):
            remote(
                self.sums.at[number],
                self.inbox.at[number, i],
                self.send.at[number],
                self.recv.at[number],
                device_at(spot),
            )

    def hear(self, number):
        take(self.heard(number), self.recv.at[number])
        total = self.sums[number]
        for i in range(len(self.rounds[number])):
            total += self.inbox[number, i]
        self.sums[number + 1] = total

    def pass_on(self, number):
        self.hear(number)
        self.speak(number + 1)

    def sent(self):
        for number in range(4):
            take(self.heard(number), self.send.at[number])


def norm_stats(values):
    average = jnp.mean(values, -1, keepdims=True)
    centered = values - average
    inverse = lax.rsqrt(jnp.mean(centered * centered, -1, keepdims=True) + EPSILON)
    return (centered * inverse, inverse)


def norm_back(upstream, normed, inverse, gain_vector):
    scaled = upstream * gain_vector
    return inverse * (
        scaled
        - jnp.mean(scaled, -1, keepdims=True)
        - normed * jnp.mean(scaled * normed, -1, keepdims=True)
    )


def softmax_columns(key_rows, queries, hidden):
    scores = mm(key_rows, queries, NT) + hidden
    powers = jnp.exp((scores - jnp.max(scores, 0, keepdims=True)) * SCALE)
    return powers * (1.0 / jnp.sum(powers, 0, keepdims=True))


def hidden_rows(seq, slot, tokens):
    row = lax.broadcasted_iota(jnp.int32, (seq, 1), 0)
    return jnp.where(lax.rem(row, slot) < tokens, 0.0, -1e30)


def head_lanes(head):
    lane = lax.broadcasted_iota(jnp.int32, (1, 128), 1)
    return jnp.where(lane // HD == head, 1.0, 0.0).astype(BF16)


def thirds(rows):
    return [rows[:, 128 * i : 128 * i + 128] for i in range(3)]


def attend(rows, hidden):
    queries, key_rows, value_rows = thirds(rows)

    def one_head(head, before):
        mine = head_lanes(head)
        probs = softmax_columns(key_rows, queries * mine, hidden).astype(BF16)
        return before + mm(probs, value_rows * mine, TN)

    return lax.fori_loop(0, 2, one_head, jnp.zeros(queries.shape, F32)).astype(BF16)


def attend_back(rows, grads, hidden):
    queries, key_rows, value_rows = thirds(rows)

    def one_head(head, before):
        mine = head_lanes(head)
        own_grads, own_queries = grads * mine, queries * mine
        probs = softmax_columns(key_rows, own_queries, hidden)
        d_probs = mm(value_rows, own_grads, NT)
        inner = jnp.sum(probs * d_probs, 0, keepdims=True)
        d_scores = (probs * (d_probs - inner)).astype(BF16)
        return (
            before[0] + mm(d_scores, key_rows * mine, TN),
            before[1] + mm(d_scores, own_queries),
            before[2] + mm(probs.astype(BF16), own_grads),
        )

    zero = jnp.zeros(queries.shape, F32)
    d_queries, d_keys, d_values = lax.fori_loop(0, 2, one_head, (zero, zero, zero))
    return [
        (d_queries * SCALE).astype(BF16),
        (d_keys * SCALE).astype(BF16),
        d_values.astype(BF16),
    ]


def padded_rows(ref, target):
    micro, tokens, width = ref.shape
    for m in range(micro):
        target[m, :tokens] = ref[m].astype(F32)
        target[m, tokens:] = jnp.zeros((target.shape[1] - tokens, width), F32)


def blocks_of(ref, index):
    value = ref[index // 2, lax.rem(index, 2)]
    return value.reshape(-1, value.shape[-1])


def half_planes(ref, value, kind, count):
    padded = jnp.concatenate(
        [value, jnp.zeros((ref.shape[-1] - count, value.shape[1]), value.dtype)], axis=0
    )
    ref[kind] = padded.T.reshape(ref.shape[1:])


def forward_kernel(*refs):
    (x_ref, cot_ref, valid_ref, qkv_in, out_in, fc1_in, fc2_in), refs = refs[:7], refs[7:]
    small_in, refs = refs[:8], refs[8:]
    (
        result_out,
        d_middle_out,
        vectors,
        sums_out,
        d_attended_out,
        images_out,
        attended_out,
        turned_out,
        act_out,
        qkv_out,
        rows,
        upstream,
        wq,
        wk,
        wv,
        up_a,
        up_b,
        down_xa,
        down_za,
        down_xb,
        down_zb,
        up_own,
        small_own,
        small,
        bias,
        hidden_bias,
        low,
        outbox,
        images,
        attended_box,
        attended,
        middle,
        normed_two,
        low_two,
        upstream_low,
        turned,
        forward_sum,
        back_sum,
        act_box,
        d_outbox,
        hidden_sums,
        local_sem,
        gather_send,
        gather_recv,
        send_sem,
        recv_sem,
        back_send,
        back_recv,
        store_sem,
        sib_send,
        sib_recv,
        ff_local,
        ff_send,
        ff_recv,
        call_send,
        call_recv,
    ) = refs
    me = place()
    f, t = lax.axis_index("fsdp"), lax.axis_index("tp")
    core = me["c"]
    other = device_at(sibling(me))
    micro, tokens, width = x_ref.shape
    slot = rows.shape[1]
    count = micro * slot
    met = greet(me)
    heads = [wq, wk, wv]
    made = []

    def gather(order, block, out):
        i = len(made)
        made.append(
            Gather(me, order, block, out, gather_send.at[i], gather_recv.at[i], local_sem.at[i])
        )
        return made[-1]

    narrow = [gather(ORDERS[i], qkv_in.at[i], heads[i]) for i in range(3)]
    vector = gather(ORDERS[0], small_own, small)
    early = [vector] + narrow
    first_half = [
        gather(ORDERS[2], up_own, up_a),
        gather(ORDERS[1], fc2_in.at[:, :128], down_xa),
        gather(ORDERS[0], fc2_in.at[:, 128:256], down_za),
    ]
    second_half = [
        gather(ORDERS[2], fc1_in.at[:, 256:], up_b),
        gather(ORDERS[1], fc2_in.at[:, 256:384], down_xb),
        gather(ORDERS[0], fc2_in.at[:, 384:], down_zb),
    ]
    stores = []

    def store(src, dst):
        copy = pltpu.make_async_copy(src, dst, store_sem.at[len(stores)])
        copy.start()
        stores.append(copy)

    shared = []

    def share(src, dst):
        slot_of = len(shared)
        copy = pltpu.make_async_remote_copy(
            src,
            dst,
            sib_send.at[slot_of],
            sib_recv.at[slot_of],
            device_id=other,
            device_id_type=MESH,
        )
        copy.start()
        shared.append(copy)

    def turn(kind, value):
        half_planes(turned, value, kind, count)
        store(turned.at[kind, :, core], turned_out.at[kind, 0])
        share(turned.at[kind, :, 1 - core], turned_out.at[kind, 1])

    padded_rows(x_ref, rows)
    up_own[:, :128] = out_in[...]
    up_own[:, 128:] = fc1_in[:, :256]
    small_own[...] = jnp.zeros_like(small_own)
    for v in range(6):
        small_own[0:1, 8 * v : 8 * v + 8] = small_in[v][...]
    for i in range(2):
        for j in range(2):
            at = 48 + 8 * i + 4 * j
            small_own[0:1, at : at + 4] = small_in[6][i, j : j + 1]
    for i in range(4):
        small_own[0:1, 64 + 8 * i : 72 + 8 * i] = small_in[7][i : i + 1]
    met()
    for part in early:
        part.first()
    normed, _ = norm_stats(rows[...].reshape(count, width))
    for part in first_half:
        part.first()
    for part in early:
        part.second()
    for part in second_half:
        part.first()
    for part in early:
        part.third()
    for part in first_half:
        part.second()
    for part in early:
        part.far()
    for part in first_half:
        part.third()
    vector.rest()
    vector.last()
    vector.done()
    table = jnp.sum(small[...].reshape(128, 32, 128).astype(F32), 1).astype(BF16)
    lane = lax.broadcasted_iota(jnp.int32, (128, 1024), 0)
    column = lax.broadcasted_iota(jnp.int32, (128, 1024), 1)
    owner = jnp.where(lax.rem(lane, 16) * 8 + lane // 16 == column // 8, 1.0, 0.0)
    for v in range(6):
        pick = jnp.where(lane == v * 8 + lax.rem(column, 8), 1.0, 0.0).astype(BF16)
        vectors[v : v + 1, :] = jnp.sum(mm(table, pick) * owner, 0, keepdims=True)
    vectors[6:8, :] = jnp.zeros((2, 1024), F32)

    def spread_bias(lanes, first, major, minor):
        lane = lax.broadcasted_iota(jnp.int32, (128, lanes), 0)
        column = lax.broadcasted_iota(jnp.int32, (128, lanes), 1)
        pick = lane == first + (column // 64) * major + lax.rem(column, 4) * minor
        owner = lax.rem(lane, 16) == lax.rem(column, 64) // 4
        values = mm(table, jnp.where(pick, 1.0, 0.0).astype(BF16))
        return jnp.sum(jnp.where(owner, values, 0.0).reshape(8, 16, lanes), 1)

    hidden_value = spread_bias(512, 64, 1, 8)
    query_bias, value_bias = spread_bias(128, 48, 4, 1), spread_bias(128, 56, 4, 1)
    for i in range(GROUP):
        hidden_bias[i] = hidden_value[i : i + 1]
        bias[i, :, 0:128] = query_bias[i : i + 1]
        bias[i, :, 128:256] = jnp.zeros((1, 128), F32)
        bias[i, :, 256:384] = value_bias[i : i + 1]
    low[...] = (normed * vectors[0:1, :] + vectors[1:2, :]).astype(BF16)
    for part in second_half:
        part.second()
    for part in narrow:
        part.rest()
    for part in narrow:
        part.last()
    for part in first_half:
        part.far()
    for part in narrow:
        part.done()

    def letter(k, m):
        target = lax.rem(t + k + 1, GROUP)
        return pltpu.make_async_remote_copy(
            outbox.at[target, m],
            images.at[t, m],
            send_sem,
            recv_sem.at[m],
            device_id=(f, target),
            device_id_type=MESH,
        )

    def project(k, carry):
        target = lax.rem(t + k + 1, GROUP)
        weights = jnp.concatenate([blocks_of(w, target) for w in heads], axis=1)
        result = (mm(low[...], weights) + bias[target]).astype(BF16)
        outbox[target] = result.reshape(outbox.shape[1:])

        @pl.when(k < GROUP - 1)
        def _():
            letter(k, 0).start()

        return carry

    lax.fori_loop(0, GROUP, project, 0)
    for m in range(1, MICRO):
        for k in range(GROUP - 1):
            letter(k, m).start()
    own = pltpu.make_async_copy(outbox.at[t], images.at[t], local_sem.at[len(made)])
    own.start()
    for i in range(3):
        store(heads[i], qkv_out.at[i])
    for part in second_half:
        part.third()
    turn(0, low[...])
    for m in range(micro):
        scale = valid_ref[0, m].astype(F32)
        upstream[m, :tokens] = cot_ref[m].astype(F32) * scale
        upstream[m, tokens:] = jnp.zeros((slot - tokens, width), F32)
    upstream_rows = upstream[...].reshape(count, width)
    sums_out[3:4, :] = jnp.sum(upstream_rows, 0, keepdims=True)
    upstream_low[...] = upstream_rows.astype(BF16)
    turn(1, upstream_low[...])
    own.wait()
    hidden = hidden_rows(GROUP * slot, slot, tokens)

    def reply(m, k):
        target = lax.rem(t + k + 1, GROUP)
        return pltpu.make_async_remote_copy(
            attended_box.at[m, target],
            attended.at[t, m],
            back_send,
            back_recv,
            device_id=(f, target),
            device_id_type=MESH,
        )

    for m in range(MICRO):
        take(images.at[: GROUP - 1, m], recv_sem.at[m])
        result = attend(images[:, m].reshape(GROUP * slot, 384), hidden)
        attended_box[m] = result.reshape(GROUP, slot, 128)
        for k in range(GROUP - 1):
            reply(m, k).start()
        attended[t, m] = attended_box[m, t]
        if m == 0:
            for part in first_half:
                part.rest()
            for part in second_half:
                part.far()
        if m == 1:
            for part in first_half:
                part.last()
    store(images, images_out)
    for part in second_half:
        part.rest()
    take(attended.at[: GROUP - 1], back_recv)
    store(attended, attended_out.at[0])
    share(attended, attended_out.at[1])
    for part in first_half:
        part.done()
    middle[...] = rows[...].reshape(count, width) + vectors[2:3, :]

    def out_weights(pair):
        both = [blocks_of(up_a, 2 * pair + i)[:, :128] for i in range(2)]
        return jnp.concatenate(both, axis=1)

    def out_project(pair, carry):
        both = [attended[2 * pair + i].reshape(count, 128) for i in range(2)]
        middle[...] += mm(jnp.concatenate(both, axis=1), out_weights(pair), NT)
        return carry

    lax.fori_loop(0, GROUP // 2, out_project, 0)
    normed, inverse = norm_stats(middle[...])
    normed_two[...] = normed
    low_two[...] = (normed * vectors[3:4, :] + vectors[4:5, :]).astype(BF16)
    turn(2, low_two[...])
    forward_sum[...] = jnp.zeros_like(forward_sum)
    back_sum[...] = jnp.zeros_like(back_sum)

    def ship(pair, h):
        piece = act_box.at[pl.ds(2 * pair, 2), :, pl.ds(2 * count * h, 2 * count)]
        at = (pl.ds(2 * pair, 2), slice(None), pl.ds(2 * count * h, 2 * count))
        pltpu.make_async_copy(piece, act_out.at[(0,) + at], ff_local).start()
        remote(piece, act_out.at[(1,) + at], ff_send, ff_recv, other)

    for h in range(2):
        if h == 1:
            for part in second_half:
                part.last()
            for part in second_half:
                part.done()

        def feed_forward(i, carry):
            up_weight = blocks_of(up_a, i)[:, 128:] if h == 0 else blocks_of(up_b, i)
            down_weight = jnp.concatenate(
                [blocks_of((down_xa, down_xb)[h], i), blocks_of((down_za, down_zb)[h], i)], axis=1
            )
            up_proj = mm(low_two[...], up_weight) + hidden_bias[i, :, 256 * h : 256 * h + 256]
            gate = jax.nn.sigmoid(1.702 * up_proj)
            activated = (up_proj * gate).astype(BF16)
            d_act = mm(upstream_low[...], down_weight)
            d_up = (d_act * (gate + 1.702 * up_proj * gate * (1.0 - gate))).astype(BF16)
            for j in range(2):
                at = pl.ds(count * (2 * h + j), count)
                act_box[i, 0, at] = activated[:, 128 * j : 128 * (j + 1)]
                act_box[i, 1, at] = d_up[:, 128 * j : 128 * (j + 1)]

            @pl.when(lax.rem(i, 2) == 1)
            def _():
                ship(i // 2, h)

            hidden_sums[i, :, 256 * h : 256 * h + 256] = jnp.sum(
                d_up.astype(F32), 0, keepdims=True
            )
            forward_sum[...] += mm(activated, down_weight, NT)
            back_sum[...] += mm(d_up, up_weight, NT)
            return carry

        lax.fori_loop(0, GROUP, feed_forward, 0)
    d_norm = back_sum[...]
    normed = normed_two[...]
    d_middle = upstream[...].reshape(count, width) + norm_back(
        d_norm, normed, inverse, vectors[3:4, :]
    )
    d_middle_out[...] = d_middle
    low[...] = d_middle.astype(BF16)

    def call(k):
        target = lax.rem(t + k + 1, GROUP)
        return pltpu.make_async_remote_copy(
            d_outbox.at[target],
            d_attended_out.at[t],
            call_send,
            call_recv,
            device_id=(f, target),
            device_id_type=MESH,
        )

    def project_back(pair, carry):
        both = mm(low[...], out_weights(pair)).astype(BF16)
        for i in range(2):
            d_outbox[2 * pair + i] = both[:, 128 * i : 128 * i + 128].reshape(d_outbox.shape[1:])
        return carry

    lax.fori_loop(0, GROUP // 2, project_back, 0)
    for k in range(GROUP - 1):
        call(k).start()
    store(d_outbox.at[t], d_attended_out.at[t])
    turn(3, low[...])
    sums_out[0:1, :] = jnp.sum(d_middle, 0, keepdims=True)
    sums_out[1:2, :] = jnp.sum(d_norm * normed, 0, keepdims=True)
    sums_out[2:3, :] = jnp.sum(d_norm, 0, keepdims=True)
    for i in range(GROUP):
        at = 4 + i // 2
        sums_out[at : at + 1, 512 * (i % 2) : 512 * (i % 2) + 512] = hidden_sums[i]
    output = (middle[...] + forward_sum[...] + vectors[5:6, :]).reshape(rows.shape)
    result_out[...] = output[:, :tokens].astype(BF16)
    for copy in shared:
        copy.wait()
    take(act_box, ff_local)
    take(act_box, ff_send)
    take(act_box, ff_recv)
    for part in made:
        part.sent()
    take(outbox.at[: GROUP - 1], send_sem)
    take(attended_box.at[:, : GROUP - 1], back_send)
    take(d_outbox.at[: GROUP - 1], call_send)
    take(d_outbox.at[: GROUP - 1], call_recv)
    for copy in stores:
        copy.wait()


ANY = pl.BlockSpec(memory_space=pl.ANY)
VMEM = pl.BlockSpec(memory_space=pltpu.VMEM)
SMEM = pl.BlockSpec(memory_space=pltpu.SMEM)


def forward(x, cotangent, valid, qkv_block, out_block, fc1_block, fc2_block, small, slot):
    width = x.shape[-1]
    count = MICRO * slot
    images = (GROUP, MICRO, slot, 384)
    attended = (GROUP, MICRO, slot, 128)
    acts = (2, GROUP, 2, 4 * count, 128)
    return pl.pallas_call(
        forward_kernel,
        out_shape=[
            jax.ShapeDtypeStruct(x.shape, BF16),
            jax.ShapeDtypeStruct((count, width), F32),
            jax.ShapeDtypeStruct((8, width), F32),
            jax.ShapeDtypeStruct((8, width), F32),
            jax.ShapeDtypeStruct(attended, BF16),
            jax.ShapeDtypeStruct(images, BF16),
            jax.ShapeDtypeStruct((2,) + attended, BF16),
            jax.ShapeDtypeStruct((4, 2, 8, 64, 256), BF16),
            jax.ShapeDtypeStruct(acts, BF16),
            jax.ShapeDtypeStruct((3,) + LEAD + (64, 128), BF16),
        ],
        in_specs=[VMEM, VMEM, SMEM, ANY, VMEM, VMEM, ANY] + [VMEM] * 8,
        out_specs=[VMEM] * 4 + [ANY] * 6,
        scratch_shapes=[
            pltpu.VMEM((MICRO, slot, width), F32),
            pltpu.VMEM((MICRO, slot, width), F32),
            pltpu.VMEM(LEAD + (64, 128), BF16),
            pltpu.VMEM(LEAD + (64, 128), BF16),
            pltpu.VMEM(LEAD + (64, 128), BF16),
            pltpu.VMEM(LEAD + (64, 384), BF16),
            pltpu.VMEM(LEAD + (64, 256), BF16),
            pltpu.VMEM(LEAD + (64, 128), BF16),
            pltpu.VMEM(LEAD + (64, 128), BF16),
            pltpu.VMEM(LEAD + (64, 128), BF16),
            pltpu.VMEM(LEAD + (64, 128), BF16),
            pltpu.VMEM((64, 384), BF16),
            pltpu.VMEM((32, 128), BF16),
            pltpu.VMEM(LEAD + (32, 128), BF16),
            pltpu.VMEM((GROUP, 1, 384), F32),
            pltpu.VMEM((GROUP, 1, 512), F32),
            pltpu.VMEM((count, width), BF16),
            pltpu.VMEM(images, BF16),
            pltpu.VMEM(images, BF16),
            pltpu.VMEM((MICRO, GROUP, slot, 128), BF16),
            pltpu.VMEM(attended, BF16),
            pltpu.VMEM((count, width), F32),
            pltpu.VMEM((count, width), F32),
            pltpu.VMEM((count, width), BF16),
            pltpu.VMEM((count, width), BF16),
            pltpu.VMEM((4, 8, 2, 64, 256), BF16),
            pltpu.VMEM((count, width), F32),
            pltpu.VMEM((count, width), F32),
            pltpu.VMEM(acts[1:], BF16),
            pltpu.VMEM(attended, BF16),
            pltpu.VMEM((GROUP, 1, 512), F32),
            pltpu.SemaphoreType.DMA((12,)),
            pltpu.SemaphoreType.DMA((10, Gather.sends)),
            pltpu.SemaphoreType.DMA((10, Gather.recvs)),
            pltpu.SemaphoreType.DMA,
            pltpu.SemaphoreType.DMA((MICRO,)),
            pltpu.SemaphoreType.DMA,
            pltpu.SemaphoreType.DMA,
            pltpu.SemaphoreType.DMA((10,)),
            pltpu.SemaphoreType.DMA((5,)),
            pltpu.SemaphoreType.DMA((5,)),
            pltpu.SemaphoreType.DMA,
            pltpu.SemaphoreType.DMA,
            pltpu.SemaphoreType.DMA,
            pltpu.SemaphoreType.DMA,
            pltpu.SemaphoreType.DMA,
        ],
        compiler_params=pltpu.CompilerParams(
            collective_id=0, has_side_effects=True, vmem_limit_bytes=VMEM_LIMIT
        ),
        name="forward",
    )(x, cotangent, valid, qkv_block, out_block, fc1_block, fc2_block, *small)


def backward_kernel(*refs):
    (
        d_attended_in,
        images_in,
        attended_in,
        turned_in,
        act_in,
        qkv_in,
        d_middle_ref,
        x_ref,
        vectors_ref,
        sums_ref,
        input_grad_out,
        qkv_grad,
        out_grad,
        fc1_grad,
        fc2_grad,
        totals_out,
        rows,
        pool,
        turned,
        attended,
        images,
        d_attended,
        outbox,
        d_images,
        d_norm,
        sums,
        sums_in,
        *rest,
    ) = refs
    scratch, sems = rest[: 5 * len(REDUCED)], rest[5 * len(REDUCED) :]
    (
        load_sem,
        reduce_send,
        reduce_recv,
        back_send,
        back_recv,
        sib_send,
        sib_recv,
        sum_send,
        sum_recv,
    ) = sems
    me = place()
    f, t = lax.axis_index("fsdp"), lax.axis_index("tp")
    other = device_at(sibling(me))
    met = greet(me)
    tokens, slot = x_ref.shape[1], rows.shape[1]
    count = MICRO * slot
    parts = [
        Reduce(
            me,
            REDUCED[i][0],
            *scratch[5 * i : 5 * i + 5],
            reduce_send.at[i],
            reduce_recv.at[i],
        )
        for i in range(len(REDUCED))
    ]
    late = parts[-3:]
    wide = parts[:-3]
    totals = [
        Totals(me, sums.at[i], sums_in.at[i], sum_send.at[i], sum_recv.at[i]) for i in range(2)
    ]
    loads = {}

    def load(name, src, dst):
        loads[name] = pltpu.make_async_copy(src, dst, load_sem.at[len(loads)])
        loads[name].start()

    kept = pl.ds(0, 4 * count)
    load("turned", turned_in, turned)
    for i in range(2):
        load(("dup", i), act_in.at[i, :, 1], pool.at[2 + i, :, kept])
    load("images", images_in, images)
    load("d_attended", d_attended_in, d_attended)
    for i in range(2):
        load(("act", i), act_in.at[i, :, 0], pool.at[i, :, kept])
    load("attended", attended_in, attended)
    sums[0, 0] = sums_ref[...]

    def both_cores(kind, values):
        total = 0.0
        for i in range(2):
            left = turned[kind, i].reshape(512, 256)[:, :count]
            total += mm(left, values[i])
        return total.astype(BF16)

    def pooled(first, index, lanes):
        return [
            jnp.concatenate(
                [pool[first + i, index, count * j : count * (j + 1)] for j in lanes], axis=1
            )
            for i in range(2)
        ]

    def spot_of(index):
        return (index // 2, lax.rem(index, 2))

    def fill(part, index, lanes, value):
        acc = part.acc
        acc[spot_of(index) + (slice(None),) * 3 + (lanes,)] = value.reshape(
            acc.shape[2:-1] + (value.shape[-1],)
        )

    def grads_up(half):
        def one(index, carry):
            value = both_cores(2, pooled(2, index, (2 * half, 2 * half + 1)))
            fill(wide[half], index, slice(0, 256), value)
            return carry

        return one

    def grads_down(index, carry):
        value = both_cores(1, pooled(0, index, range(4)))
        fill(wide[2], index, slice(0, 128), value[:, :128])
        fill(wide[3], index, slice(0, 256), value[:, 128:384])
        fill(wide[4], index, slice(0, 128), value[:, 384:])
        value = both_cores(3, [attended[i, index].reshape(count, 128) for i in range(2)])
        fill(wide[4], index, slice(128, 256), value)
        return carry

    loads["turned"].wait()
    for i in range(2):
        loads["dup", i].wait()
    lax.fori_loop(0, GROUP, grads_up(0), 0)
    met()
    wide[0].stage_far()
    totals[0].speak(0)
    lax.fori_loop(0, GROUP, grads_up(1), 0)
    wide[1].stage_far()
    loads["images"].wait()
    loads["d_attended"].wait()
    hidden = hidden_rows(GROUP * slot, slot, tokens)

    def reply(m, k):
        target = lax.rem(t + k + 1, GROUP)
        return pltpu.make_async_remote_copy(
            outbox.at[m, target],
            d_images.at[0, t, m],
            back_send,
            back_recv.at[k],
            device_id=(f, target),
            device_id_type=MESH,
        )

    for m in range(MICRO):
        results = attend_back(
            images[:, m].reshape(GROUP * slot, 384),
            d_attended[:, m].reshape(GROUP * slot, 128),
            hidden,
        )
        for i in range(3):
            outbox[m, :, :, 128 * i : 128 * i + 128] = results[i].reshape(GROUP, slot, 128)
        for k in range(GROUP - 1):
            reply(m, k).start()
        d_images[0, t, m] = outbox[m, t]
        if m == 0:
            for i in range(2):
                loads["act", i].wait()
            loads["attended"].wait()
            lax.fori_loop(0, GROUP, grads_down, 0)
            for part in wide[2:]:
                part.stage_far()
            for i in range(3):
                load(("weight", i), qkv_in.at[i], pool.at[i])
            wide[0].stage_near()
            totals[0].pass_on(0)
        if m == 1:
            wide[1].stage_near()
            totals[0].pass_on(1)
    for part in wide[2:]:
        part.stage_near()
    padded_rows(x_ref, rows)
    normed, inverse = norm_stats(rows[...].reshape(count, rows.shape[-1]))
    totals[0].pass_on(2)
    wide[0].stage_mid()

    def share(k):
        source = lax.rem(t + k + 1, GROUP)
        remote(d_images.at[0, source], d_images.at[1, source], sib_send, sib_recv, other)

    share(GROUP - 1)
    for k in reversed(range(GROUP - 1)):
        take(d_images.at[0, 0], back_recv.at[GROUP - 2 - k])
        share(k)
    wide[1].stage_mid()
    take(d_images.at[1], sib_recv)

    def grads_late(index, carry):
        value = both_cores(0, [d_images[i, index].reshape(count, 384) for i in range(2)])
        for i, part in enumerate(late):
            fill(part, index, slice(None), value[:, 128 * i : 128 * i + 128])
        return carry

    lax.fori_loop(0, GROUP, grads_late, 0)
    for part in late:
        part.stage_far()
    for part in wide[2:]:
        part.stage_mid()
    for i in range(3):
        loads["weight", i].wait()
    d_norm[...] = jnp.zeros_like(d_norm)

    def project_back(index, carry):
        weights = jnp.concatenate([pool[i, index] for i in range(3)], axis=1)
        d_norm[...] += mm(d_images[0, index].reshape(count, 384), weights, NT)
        return carry

    lax.fori_loop(0, GROUP, project_back, 0)
    for part in late:
        part.stage_near()
    for part in wide[:2]:
        part.stage_tail()
    gradient = d_norm[...]
    sums[1, 0, 0:1, :] = jnp.sum(gradient * normed, 0, keepdims=True)
    sums[1, 0, 1:2, :] = jnp.sum(gradient, 0, keepdims=True)
    for index in range(GROUP):
        grads = jnp.sum(d_images[0, index].reshape(count, 384).astype(F32), 0, keepdims=True)
        sums[1, 0, 2:3, 128 * index : 128 * index + 128] = grads[:, :128]
        sums[1, 0, 3:4, 128 * index : 128 * index + 128] = grads[:, 256:]
    sums[1, 0, 4:8, :] = jnp.zeros((4, sums.shape[-1]), F32)
    totals[1].speak(0)
    totals[0].hear(3)
    result = d_middle_ref[...] + norm_back(gradient, normed, inverse, vectors_ref[0:1, :])
    input_grad_out[...] = result.reshape(rows.shape)[:, :tokens].astype(BF16)
    totals[1].pass_on(0)
    for part in late:
        part.stage_mid()
    for part in wide[2:]:
        part.stage_tail()
    totals[1].pass_on(1)
    for part in late:
        part.stage_tail()
    fc1_grad[:, :256] = wide[0].stage_out()
    fc1_grad[:, 256:] = wide[1].stage_out()
    fc2_grad[:, :128] = wide[2].stage_out()
    fc2_grad[:, 128:384] = wide[3].stage_out()
    value = wide[4].stage_out()
    fc2_grad[:, 384:] = value[:, :128]
    out_grad[...] = value[:, 128:]
    totals[1].pass_on(2)
    for i in range(3):
        qkv_grad[i] = late[i].stage_out()
    totals[1].hear(3)
    totals_out[0:8, :] = sums[0, 4]
    totals_out[8:16, :] = sums[1, 4]
    for part in parts:
        part.sent()
    for total in totals:
        total.sent()
    take(d_images.at[1], sib_send)
    take(outbox.at[:, : GROUP - 1], back_send)


REDUCED = (
    (ORDERS[2], 256),
    (ORDERS[2], 256),
    (ORDERS[2], 128),
    (ORDERS[1], 256),
    (ORDERS[0], 256),
    (ORDERS[0], 128),
    (ORDERS[1], 128),
    (ORDERS[2], 128),
)


def backward(d_attended, images, attended, turned, act, qkv, d_middle, x, vectors, sums, slot):
    width = x.shape[-1]
    count = MICRO * slot
    scratch = []
    for order, lanes in REDUCED:
        scratch += reduce_scratch(order, lanes)
    return pl.pallas_call(
        backward_kernel,
        out_shape=[
            jax.ShapeDtypeStruct(x.shape, BF16),
            jax.ShapeDtypeStruct((3, 64, 128), F32),
            jax.ShapeDtypeStruct((64, 128), F32),
            jax.ShapeDtypeStruct((64, 512), F32),
            jax.ShapeDtypeStruct((64, 512), F32),
            jax.ShapeDtypeStruct((16, width), F32),
        ],
        in_specs=[ANY] * 6 + [VMEM] * 4,
        out_specs=[VMEM] * 6,
        scratch_shapes=[
            pltpu.VMEM((MICRO, slot, width), F32),
            pltpu.VMEM((4, GROUP, width, 128), BF16),
            pltpu.VMEM(turned.shape, BF16),
            pltpu.VMEM(attended.shape, BF16),
            pltpu.VMEM(images.shape, BF16),
            pltpu.VMEM(d_attended.shape, BF16),
            pltpu.VMEM((MICRO, GROUP, slot, 384), BF16),
            pltpu.VMEM((2,) + images.shape, BF16),
            pltpu.VMEM((count, width), F32),
            pltpu.VMEM((2, 5, 8, width), F32),
            pltpu.VMEM((2, 4, 3, 8, width), F32),
        ]
        + scratch
        + [
            pltpu.SemaphoreType.DMA((11,)),
            pltpu.SemaphoreType.DMA((len(REDUCED), Reduce.sends)),
            pltpu.SemaphoreType.DMA((len(REDUCED), Reduce.recvs)),
            pltpu.SemaphoreType.DMA,
            pltpu.SemaphoreType.DMA((GROUP,)),
            pltpu.SemaphoreType.DMA,
            pltpu.SemaphoreType.DMA,
            pltpu.SemaphoreType.DMA((2, 4)),
            pltpu.SemaphoreType.DMA((2, 4)),
        ],
        compiler_params=pltpu.CompilerParams(
            collective_id=1, has_side_effects=True, vmem_limit_bytes=VMEM_LIMIT
        ),
        name="backward",
    )(d_attended, images, attended, turned, act, qkv, d_middle, x, vectors, sums)


def finish_kernel(
    result,
    input_grad,
    qkv_grad,
    out_grad,
    fc1_grad,
    fc2_grad,
    totals,
    result_out,
    input_grad_out,
    qkv_out,
    out_out,
    fc1_out,
    fc2_out,
    vectors_out,
    pair_out,
    hidden_out,
):
    f, t = lax.axis_index("fsdp"), lax.axis_index("tp")
    result_out[...] = result[...]
    input_grad_out[...] = input_grad[...]
    qkv_out[...] = qkv_grad[...]
    out_out[...] = out_grad[...]
    fc1_out[...] = fc1_grad[...]
    fc2_out[...] = fc2_grad[...]
    width = totals.shape[-1]
    own = pltpu.roll(totals[...], lax.rem(width - (f * 8 + t) * 8, width), 1)
    for number, row in enumerate((8, 9, 0, 1, 2, 3)):
        vectors_out[number] = own[row : row + 1, :8]
    own = pltpu.roll(totals[...], lax.rem(width - t * 128 - f * 4, width), 1)
    for kind in range(2):
        for head in range(2):
            pair_out[kind, head : head + 1, :] = own[
                10 + kind : 11 + kind, HD * head : HD * head + 4
            ]
    row = totals[4:8, :]
    mine = lax.broadcasted_iota(jnp.int32, row.shape, 0) == t // 2
    row = jnp.sum(jnp.where(mine, row, 0.0), 0, keepdims=True)
    row = pltpu.roll(
        jnp.broadcast_to(row, (8, width)), lax.rem(width - 512 * lax.rem(t, 2) - f * 4, width), 1
    )
    for j in range(8):
        hidden_out[j : j + 1, :] = row[0:1, 64 * j : 64 * j + 4]


def finish(result, input_grad, qkv_grad, out_grad, fc1_grad, fc2_grad, totals):
    arrays = (result, input_grad, qkv_grad, out_grad, fc1_grad, fc2_grad)
    shapes = [jax.ShapeDtypeStruct(a.shape, a.dtype) for a in arrays]
    shapes += [
        jax.ShapeDtypeStruct((6, 1, 8), F32),
        jax.ShapeDtypeStruct((2, 2, 4), F32),
        jax.ShapeDtypeStruct((8, 4), F32),
    ]
    return pl.pallas_call(
        finish_kernel,
        out_shape=shapes,
        in_specs=[VMEM] * 7,
        out_specs=[VMEM] * 9,
        compiler_params=pltpu.CompilerParams(vmem_limit_bytes=VMEM_LIMIT),
        name="finish",
    )(*arrays, totals)


def per_device(
    inputs,
    cotangent,
    valid_slots,
    ln1_gain,
    ln1_bias,
    qkv_weight,
    qv_bias,
    out_weight,
    out_bias,
    ln2_gain,
    ln2_bias,
    fc1_weight,
    fc1_bias,
    fc2_weight,
    fc2_bias,
):
    micro, _, tokens, width = inputs.shape
    slot = -(-tokens // 16) * 16
    x = inputs.reshape(micro, tokens, width)
    small = [ln1_gain, ln1_bias, out_bias, ln2_gain, ln2_bias, fc2_bias]
    small = [v.reshape(1, 8) for v in small] + [qv_bias, fc1_bias.T]
    (
        result,
        d_middle,
        vectors,
        sums,
        d_attended,
        images,
        attended,
        turned,
        act,
        qkv,
    ) = forward(
        x,
        cotangent.reshape(x.shape),
        valid_slots.T,
        qkv_weight,
        out_weight.T,
        fc1_weight,
        fc2_weight.T,
        small,
        slot,
    )
    input_grad, qkv_grad, out_grad, fc1_grad, fc2_grad, total = backward(
        d_attended,
        images,
        attended,
        turned,
        act,
        qkv.reshape(3, GROUP, width, 128),
        d_middle,
        x,
        vectors,
        sums,
        slot,
    )
    result, input_grad, qkv_grad, out_grad, fc1_grad, fc2_grad, own, pair, hidden_grad = finish(
        result, input_grad, qkv_grad, out_grad, fc1_grad, fc2_grad, total
    )
    own = [own[i].reshape(8) for i in range(6)]
    return (
        result.reshape(inputs.shape),
        input_grad.reshape(inputs.shape),
        own[0],
        own[1],
        qkv_grad,
        pair,
        out_grad.T,
        own[2],
        own[3],
        own[4],
        fc1_grad,
        hidden_grad,
        fc2_grad.T,
        own[5],
    )


def solution(mesh):
    in_specs = (
        P(None, "fsdp", "tp", None),
        P(None, "fsdp", "tp", None),
        P(None, "fsdp"),
        P(("fsdp", "tp")),
        P(("fsdp", "tp")),
        P(None, "fsdp", "tp"),
        P(None, "tp", "fsdp"),
        P("tp", "fsdp"),
        P(("fsdp", "tp")),
        P(("fsdp", "tp")),
        P(("fsdp", "tp")),
        P("fsdp", "tp"),
        P("tp", "fsdp"),
        P("tp", "fsdp"),
        P(("fsdp", "tp")),
    )
    out_specs = (
        P(None, "fsdp", "tp", None),
        P(None, "fsdp", "tp", None),
        P(("fsdp", "tp")),
        P(("fsdp", "tp")),
        P(None, "fsdp", "tp"),
        P(None, "tp", "fsdp"),
        P("tp", "fsdp"),
        P(("fsdp", "tp")),
        P(("fsdp", "tp")),
        P(("fsdp", "tp")),
        P("fsdp", "tp"),
        P("tp", "fsdp"),
        P("tp", "fsdp"),
        P(("fsdp", "tp")),
    )
    return jax.shard_map(
        per_device, mesh=mesh, in_specs=in_specs, out_specs=out_specs, check_vma=False
    )
```

time: 238 us -> 217 us (0.912)
  local copies, waits for them, and re-layouts: 24.2 us -> 2.54 us
    unnamed x13 -> x1, local copies, waits for them, and re-layouts: 14.7 us -> 1.33 us
    concatenate x1 -> x0, local copies, waits for them, and re-layouts: 4.1 us -> none  [per_device(): jnp.concatenate([ln1_gain, ln1_bias, out_bias, ln2_gain, ln2_bias, fc2_bi...]
    pallas_call x1, Pallas kernels: 102 us -> 98.5 us  [backward(): pl.pallas_call(backward_kernel, out_shape=[jax.ShapeDtypeStruct(x.shape,...]
    pallas_call x0 -> x1, Pallas kernels: none -> 2.44 us  [finish(): pl.pallas_call(finish_kernel, out_shape=shapes, in_specs=[VMEM] * 7, out_...]
where the time goes in v4:
time: 217 us
  Pallas kernels  213 us (98%)
  local copies, waits for them, and re-layouts  2.54 us (1%)
    pallas_call x1, Pallas kernels, forward(): pl.pallas_call(forward_kernel, out_shape=[jax.ShapeDtypeStruct(x.shape, B...  113 us
    pallas_call x1, Pallas kernels, backward(): pl.pallas_call(backward_kernel, out_shape=[jax.ShapeDtypeStruct(x.shape,...  98.5 us

profile of v4, /device:TPU:0, one launch (start us, length us, event | category | flops | bytes accessed | tf_op | source)
XLA Modules:
  0.0 216.7 jit_solution(13130221276933489090)
XLA Ops:
  0.7 112.5 %forward.1 = (bf16[3,72,1024]{2,1,0:T(8,128)(2,1)}, f32[240,1024]{1,0:T(8,128)}, f32[8,1024]{1,0:T(8,128)}, f32[8,1024]{1,0:T(8,128)}, bf16[8,3,80,128]{3,2,1,0:...) custom-call(bf16[3,72,1024]{2,1,0:T(8,128)(2,1)} %bitcast.34, ...), custom_call_target="tpu_custom_call" | custom-call | tf_op jit(solution)/shard_map/forward/pallas_call | solution.py:823
  113.2 98.5 %backward.1 = (bf16[3,72,1024]{2,1,0:T(8,128)(2,1)}, f32[3,64,128]{2,1,0:T(8,128)}, f32[64,128]{1,0:T(8,128)}, f32[64,512]{1,0:T(8,128)}, f32[64,512]{1,0:T(8,128)}, /*index=5*/f32[16,1024]{1,0:T(8,128)}) custom-call(bf16[8,3,80,128]{3,2,1,0:T(8,128)(2,1)} %get-tuple-element.40.refs_0_, bf16[8,3,80,384]{3,2,1,0:T(8,128)(2,1)} %get-tuple-element.41.refs_1_, ...), custom_call_target="tpu_custom_call" | custom-call | tf_op jit(solution)/shard_map/backward/pallas_call | solution.py:1167
  211.7 2.4 %finish.1 = (bf16[3,72,1024]{2,1,0:T(8,128)(2,1)}, bf16[3,72,1024]{2,1,0:T(8,128)(2,1)}, f32[3,64,128]{2,1,0:T(8,128)}, f32[64,128]{1,0:T(8,128)}, f32[64,512]{1...) custom-call(bf16[3,72,1024]{2,1,0:T(8,128)(2,1)} %get-tuple-element.39.result, ...), custom_call_target="tpu_custom_call" | custom-call | tf_op jit(solution)/shard_map/finish/pallas_call | solution.py:1264
  214.1 1.3 copy.31
  215.5 1.2 slice_bitcast_fusion

commit v5 on v4

--- a/solution.py
+++ b/solution.py
@@ -15,7 +15,7 @@
 BF16 = jnp.bfloat16
 F32 = jnp.float32
 VMEM_LIMIT = 62 * 2**20
-MICRO, GROUP = 3, 8
+MICRO, GROUP, TOKENS = 3, 8, 72
 ORDERS = (("x", "y", "z"), ("y", "z", "x"), ("z", "x", "y"))
 SIZES = {"x": (4,), "z": (2, 2), "y": (4,)}
 LEAD = (4, 2, 2, 4, 2)
@@ -54,13 +54,19 @@
     return {**spot, "c": 1 - spot["c"]}
 
 
+def member(me, number):
+    return device_at({**me, "x": number // 2, "c": lax.rem(number, 2)})
+
+
+def crossed(me):
+    return device_at({**me, "z": me["z"] + 1 - 2 * lax.rem(me["z"], 2), "c": 1 - me["c"]})
+
+
 def greet(me):
-    f, t = lax.axis_index("fsdp"), lax.axis_index("tp")
-    devices = [(f, lax.rem(t + step, GROUP)) for step in range(1, GROUP)]
-    devices += [device_at(shifted(me, "y", by)) for by in STEPS]
-    devices += [device_at(shifted(me, "z", 2))]
-    devices += [device_at(shifted(me, "z", 2 * lax.rem(me["z"], 2) - 1))]
-    devices += [device_at(sibling(me))]
+    rank = 2 * me["x"] + me["c"]
+    devices = [member(me, lax.rem(rank + step, GROUP)) for step in range(1, GROUP)]
+    devices += [device_at(shifted(me, axis, by)) for axis in "yz" for by in STEPS]
+    devices += [crossed(me)]
     barrier = pltpu.get_barrier_semaphore()
     for device in devices:
         pl.semaphore_signal(barrier, inc=1, device_id=device, device_id_type=MESH)
@@ -411,11 +417,31 @@
     ]
 
 
-def padded_rows(ref, target):
-    micro, tokens, width = ref.shape
-    for m in range(micro):
-        target[m, :tokens] = ref[m].astype(F32)
-        target[m, tokens:] = jnp.zeros((target.shape[1] - tokens, width), F32)
+def fill_rows(box, m, values):
+    tokens = values.shape[0]
+    box[m, :tokens] = values
+    box[m, tokens:] = jnp.zeros((box.shape[1] - tokens, values.shape[1]), box.dtype)
+
+
+class Swap:
+    def __init__(self, me, send, recv):
+        self.stays = lax.rem(me["z"], 2) == me["c"]
+        self.partner = crossed(me)
+        self.send, self.recv = send, recv
+
+    def start(self, box, inbox):
+        @pl.when(self.stays)
+        def _():
+            pltpu.make_async_copy(box, inbox, self.recv).start()
+
+        @pl.when(jnp.logical_not(self.stays))
+        def _():
+            remote(box, inbox, self.send, self.recv, self.partner)
+
+    def sent(self, box):
+        @pl.when(jnp.logical_not(self.stays))
+        def _():
+            take(box, self.send)
 
 
 def blocks_of(ref, index):
@@ -430,32 +456,52 @@
     ref[kind] = padded.T.reshape(ref.shape[1:])
 
 
+SCHEDULE = {
+    "start": (("E", "first"),),
+    "first": (("A", "first"), ("E", "second"), ("B", "first")),
+    "swap": (("E", "third"), ("A", "second"), ("E", "far")),
+    "norm": (("A", "third"), ("V", "rest"), ("V", "last"), ("V", "done")),
+    "table": (("B", "second"), ("N", "rest"), ("N", "last"), ("A", "far"), ("N", "done")),
+    "project": (("A", "rest"), ("B", "third"), ("A", "last")),
+    "image 0": (("B", "far"),),
+    "image 1": (("B", "rest"),),
+    "image 2": (("B", "last"),),
+    "reply": (("A", "done"),),
+    "half 0": (),
+    "half 1": (("B", "done"),),
+}
+
+
 def forward_kernel(*refs):
     (x_ref, cot_ref, valid_ref, qkv_in, out_in, fc1_in, fc2_in), refs = refs[:7], refs[7:]
     small_in, refs = refs[:8], refs[8:]
     (
-        result_out,
         d_middle_out,
         vectors,
         sums_out,
+        result_out,
         d_attended_out,
         images_out,
         attended_out,
         turned_out,
         act_out,
         qkv_out,
-        rows,
-        upstream,
+        x_out,
+        x_box,
+        x_in,
+        cot_box,
+        cot_in,
+        result_box,
         wq,
         wk,
         wv,
         up_a,
         up_b,
+        side_a,
         down_xa,
-        down_za,
         down_xb,
         down_zb,
-        up_own,
+        side_own,
         small_own,
         small,
         bias,
@@ -468,7 +514,6 @@
         middle,
         normed_two,
         low_two,
-        upstream_low,
         turned,
         forward_sum,
         back_sum,
@@ -488,15 +533,15 @@
         ff_local,
         ff_send,
         ff_recv,
-        call_send,
-        call_recv,
+        swap_send,
+        swap_recv,
     ) = refs
     me = place()
-    f, t = lax.axis_index("fsdp"), lax.axis_index("tp")
     core = me["c"]
+    t = 2 * me["x"] + core
     other = device_at(sibling(me))
     micro, tokens, width = x_ref.shape
-    slot = rows.shape[1]
+    slot = x_in.shape[1]
     count = micro * slot
     met = greet(me)
     heads = [wq, wk, wv]
@@ -513,15 +558,29 @@
     vector = gather(ORDERS[0], small_own, small)
     early = [vector] + narrow
     first_half = [
-        gather(ORDERS[2], up_own, up_a),
+        gather(ORDERS[2], fc1_in.at[:, :256], up_a),
+        gather(ORDERS[0], side_own, side_a),
         gather(ORDERS[1], fc2_in.at[:, :128], down_xa),
-        gather(ORDERS[0], fc2_in.at[:, 128:256], down_za),
     ]
     second_half = [
-        gather(ORDERS[2], fc1_in.at[:, 256:], up_b),
-        gather(ORDERS[1], fc2_in.at[:, 256:384], down_xb),
-        gather(ORDERS[0], fc2_in.at[:, 384:], down_zb),
+        gather(ORDERS[0], fc1_in.at[:, 256:], up_b),
+        gather(ORDERS[2], fc2_in.at[:, 256:384], down_xb),
+        gather(ORDERS[2], fc2_in.at[:, 384:], down_zb),
     ]
+    groups = {
+        "V": [vector],
+        "N": narrow,
+        "E": early,
+        "A": first_half,
+        "B": second_half,
+    }
+
+    def run(point):
+        for names, stage in SCHEDULE[point]:
+            for name in names:
+                for part in groups[name]:
+                    getattr(part, stage)()
+
     stores = []
 
     def store(src, dst):
@@ -549,9 +608,10 @@
         store(turned.at[kind, :, core], turned_out.at[kind, 0])
         share(turned.at[kind, :, 1 - core], turned_out.at[kind, 1])
 
-    padded_rows(x_ref, rows)
-    up_own[:, :128] = out_in[...]
-    up_own[:, 128:] = fc1_in[:, :256]
+    for m in range(micro):
+        fill_rows(x_box, m, x_ref[m])
+    side_own[:, :128] = out_in[...]
+    side_own[:, 128:] = fc2_in[:, 128:256]
     small_own[...] = jnp.zeros_like(small_own)
     for v in range(6):
         small_own[0:1, 8 * v : 8 * v + 8] = small_in[v][...]
@@ -562,26 +622,21 @@
     for i in range(4):
         small_own[0:1, 64 + 8 * i : 72 + 8 * i] = small_in[7][i : i + 1]
     met()
-    for part in early:
-        part.first()
-    normed, _ = norm_stats(rows[...].reshape(count, width))
-    for part in first_half:
-        part.first()
-    for part in early:
-        part.second()
-    for part in second_half:
-        part.first()
-    for part in early:
-        part.third()
-    for part in first_half:
-        part.second()
-    for part in early:
-        part.far()
-    for part in first_half:
-        part.third()
-    vector.rest()
-    vector.last()
-    vector.done()
+    run("start")
+    swaps = [Swap(me, swap_send.at[i], swap_recv.at[i]) for i in range(3)]
+    swaps[0].start(x_box, x_in)
+    run("first")
+    for m in range(micro):
+        fill_rows(cot_box, m, (cot_ref[m].astype(F32) * valid_ref[0, m].astype(F32)).astype(BF16))
+    run("swap")
+    take(x_in, swap_recv.at[0])
+    store(x_in, x_out)
+
+    def rows_of(ref):
+        return ref[...].reshape(count, width).astype(F32)
+
+    normed, _ = norm_stats(rows_of(x_in))
+    run("norm")
     table = jnp.sum(small[...].reshape(128, 32, 128).astype(F32), 1).astype(BF16)
     lane = lax.broadcasted_iota(jnp.int32, (128, 1024), 0)
     column = lax.broadcasted_iota(jnp.int32, (128, 1024), 1)
@@ -607,16 +662,7 @@
         bias[i, :, 128:256] = jnp.zeros((1, 128), F32)
         bias[i, :, 256:384] = value_bias[i : i + 1]
     low[...] = (normed * vectors[0:1, :] + vectors[1:2, :]).astype(BF16)
-    for part in second_half:
-        part.second()
-    for part in narrow:
-        part.rest()
-    for part in narrow:
-        part.last()
-    for part in first_half:
-        part.far()
-    for part in narrow:
-        part.done()
+    run("table")
 
     def letter(k, m):
         target = lax.rem(t + k + 1, GROUP)
@@ -625,7 +671,7 @@
             images.at[t, m],
             send_sem,
             recv_sem.at[m],
-            device_id=(f, target),
+            device_id=member(me, target),
             device_id_type=MESH,
         )
 
@@ -649,17 +695,9 @@
     own.start()
     for i in range(3):
         store(heads[i], qkv_out.at[i])
-    for part in second_half:
-        part.third()
+    swaps[1].start(cot_box, cot_in)
+    run("project")
     turn(0, low[...])
-    for m in range(micro):
-        scale = valid_ref[0, m].astype(F32)
-        upstream[m, :tokens] = cot_ref[m].astype(F32) * scale
-        upstream[m, tokens:] = jnp.zeros((slot - tokens, width), F32)
-    upstream_rows = upstream[...].reshape(count, width)
-    sums_out[3:4, :] = jnp.sum(upstream_rows, 0, keepdims=True)
-    upstream_low[...] = upstream_rows.astype(BF16)
-    turn(1, upstream_low[...])
     own.wait()
     hidden = hidden_rows(GROUP * slot, slot, tokens)
 
@@ -670,7 +708,7 @@
             attended.at[t, m],
             back_send,
             back_recv,
-            device_id=(f, target),
+            device_id=member(me, target),
             device_id_type=MESH,
         )
 
@@ -681,26 +719,21 @@
         for k in range(GROUP - 1):
             reply(m, k).start()
         attended[t, m] = attended_box[m, t]
-        if m == 0:
-            for part in first_half:
-                part.rest()
-            for part in second_half:
-                part.far()
+        run(("image 0", "image 1", "image 2")[m])
         if m == 1:
-            for part in first_half:
-                part.last()
+            take(cot_in, swap_recv.at[1])
+            upstream_low = cot_in[...].reshape(count, width)
+            sums_out[3:4, :] = jnp.sum(upstream_low.astype(F32), 0, keepdims=True)
+            turn(1, upstream_low)
     store(images, images_out)
-    for part in second_half:
-        part.rest()
     take(attended.at[: GROUP - 1], back_recv)
     store(attended, attended_out.at[0])
     share(attended, attended_out.at[1])
-    for part in first_half:
-        part.done()
-    middle[...] = rows[...].reshape(count, width) + vectors[2:3, :]
+    run("reply")
+    middle[...] = rows_of(x_in) + vectors[2:3, :]
 
     def out_weights(pair):
-        both = [blocks_of(up_a, 2 * pair + i)[:, :128] for i in range(2)]
+        both = [blocks_of(side_a, 2 * pair + i)[:, :128] for i in range(2)]
         return jnp.concatenate(both, axis=1)
 
     def out_project(pair, carry):
@@ -723,57 +756,46 @@
         remote(piece, act_out.at[(1,) + at], ff_send, ff_recv, other)
 
     for h in range(2):
-        if h == 1:
-            for part in second_half:
-                part.last()
-            for part in second_half:
-                part.done()
-
-        def feed_forward(i, carry):
-            up_weight = blocks_of(up_a, i)[:, 128:] if h == 0 else blocks_of(up_b, i)
-            down_weight = jnp.concatenate(
-                [blocks_of((down_xa, down_xb)[h], i), blocks_of((down_za, down_zb)[h], i)], axis=1
-            )
-            up_proj = mm(low_two[...], up_weight) + hidden_bias[i, :, 256 * h : 256 * h + 256]
+        run(("half 0", "half 1")[h])
+
+        def feed_forward(pair, carry):
+            slabs = [2 * pair, 2 * pair + 1]
+            up_weight = jnp.concatenate([blocks_of((up_a, up_b)[h], i) for i in slabs], axis=1)
+            down = []
+            for i in slabs:
+                down.append(blocks_of((down_xa, down_xb)[h], i))
+                down.append(blocks_of(side_a, i)[:, 128:] if h == 0 else blocks_of(down_zb, i))
+            down_weight = jnp.concatenate(down, axis=1)
+            biases = [hidden_bias[i, :, 256 * h : 256 * h + 256] for i in slabs]
+            up_proj = mm(low_two[...], up_weight) + jnp.concatenate(biases, axis=1)
             gate = jax.nn.sigmoid(1.702 * up_proj)
             activated = (up_proj * gate).astype(BF16)
-            d_act = mm(upstream_low[...], down_weight)
+            d_act = mm(cot_in[...].reshape(count, width), down_weight)
             d_up = (d_act * (gate + 1.702 * up_proj * gate * (1.0 - gate))).astype(BF16)
-            for j in range(2):
-                at = pl.ds(count * (2 * h + j), count)
-                act_box[i, 0, at] = activated[:, 128 * j : 128 * (j + 1)]
-                act_box[i, 1, at] = d_up[:, 128 * j : 128 * (j + 1)]
-
-            @pl.when(lax.rem(i, 2) == 1)
-            def _():
-                ship(i // 2, h)
-
-            hidden_sums[i, :, 256 * h : 256 * h + 256] = jnp.sum(
-                d_up.astype(F32), 0, keepdims=True
-            )
+            column_sums = jnp.sum(d_up.astype(F32), 0, keepdims=True)
+            for n, i in enumerate(slabs):
+                for j in range(2):
+                    at = pl.ds(count * (2 * h + j), count)
+                    lanes = slice(256 * n + 128 * j, 256 * n + 128 * (j + 1))
+                    act_box[i, 0, at] = activated[:, lanes]
+                    act_box[i, 1, at] = d_up[:, lanes]
+                hidden_sums[i, :, 256 * h : 256 * h + 256] = column_sums[:, 256 * n : 256 * n + 256]
+            ship(pair, h)
             forward_sum[...] += mm(activated, down_weight, NT)
             back_sum[...] += mm(d_up, up_weight, NT)
             return carry
 
-        lax.fori_loop(0, GROUP, feed_forward, 0)
+        lax.fori_loop(0, GROUP // 2, feed_forward, 0)
+    output = (middle[...] + forward_sum[...] + vectors[5:6, :]).astype(BF16)
+    result_box[...] = output.reshape(result_box.shape)
+    swaps[2].start(result_box, result_out)
     d_norm = back_sum[...]
     normed = normed_two[...]
-    d_middle = upstream[...].reshape(count, width) + norm_back(
+    d_middle = rows_of(cot_in) + norm_back(
         d_norm, normed, inverse, vectors[3:4, :]
     )
     d_middle_out[...] = d_middle
     low[...] = d_middle.astype(BF16)
-
-    def call(k):
-        target = lax.rem(t + k + 1, GROUP)
-        return pltpu.make_async_remote_copy(
-            d_outbox.at[target],
-            d_attended_out.at[t],
-            call_send,
-            call_recv,
-            device_id=(f, target),
-            device_id_type=MESH,
-        )
 
     def project_back(pair, carry):
         both = mm(low[...], out_weights(pair)).astype(BF16)
@@ -782,9 +804,7 @@
         return carry
 
     lax.fori_loop(0, GROUP // 2, project_back, 0)
-    for k in range(GROUP - 1):
-        call(k).start()
-    store(d_outbox.at[t], d_attended_out.at[t])
+    store(d_outbox, d_attended_out)
     turn(3, low[...])
     sums_out[0:1, :] = jnp.sum(d_middle, 0, keepdims=True)
     sums_out[1:2, :] = jnp.sum(d_norm * normed, 0, keepdims=True)
@@ -792,8 +812,9 @@
     for i in range(GROUP):
         at = 4 + i // 2
         sums_out[at : at + 1, 512 * (i % 2) : 512 * (i % 2) + 512] = hidden_sums[i]
-    output = (middle[...] + forward_sum[...] + vectors[5:6, :]).reshape(rows.shape)
-    result_out[...] = output[:, :tokens].astype(BF16)
+    for swap, box in zip(swaps, (x_box, cot_box, result_box)):
+        swap.sent(box)
+    take(result_out, swap_recv.at[2])
     for copy in shared:
         copy.wait()
     take(act_box, ff_local)
@@ -803,8 +824,6 @@
         part.sent()
     take(outbox.at[: GROUP - 1], send_sem)
     take(attended_box.at[:, : GROUP - 1], back_send)
-    take(d_outbox.at[: GROUP - 1], call_send)
-    take(d_outbox.at[: GROUP - 1], call_recv)
     for copy in stores:
         copy.wait()
 
@@ -817,38 +836,43 @@
 def forward(x, cotangent, valid, qkv_block, out_block, fc1_block, fc2_block, small, slot):
     width = x.shape[-1]
     count = MICRO * slot
+    rows = (MICRO, slot, width)
     images = (GROUP, MICRO, slot, 384)
     attended = (GROUP, MICRO, slot, 128)
     acts = (2, GROUP, 2, 4 * count, 128)
     return pl.pallas_call(
         forward_kernel,
         out_shape=[
-            jax.ShapeDtypeStruct(x.shape, BF16),
             jax.ShapeDtypeStruct((count, width), F32),
             jax.ShapeDtypeStruct((8, width), F32),
             jax.ShapeDtypeStruct((8, width), F32),
+            jax.ShapeDtypeStruct(rows, BF16),
             jax.ShapeDtypeStruct(attended, BF16),
             jax.ShapeDtypeStruct(images, BF16),
             jax.ShapeDtypeStruct((2,) + attended, BF16),
             jax.ShapeDtypeStruct((4, 2, 8, 64, 256), BF16),
             jax.ShapeDtypeStruct(acts, BF16),
             jax.ShapeDtypeStruct((3,) + LEAD + (64, 128), BF16),
+            jax.ShapeDtypeStruct(rows, BF16),
         ],
-        in_specs=[VMEM, VMEM, SMEM, ANY, VMEM, VMEM, ANY] + [VMEM] * 8,
-        out_specs=[VMEM] * 4 + [ANY] * 6,
+        in_specs=[VMEM, VMEM, SMEM, ANY, VMEM, ANY, VMEM] + [VMEM] * 8,
+        out_specs=[VMEM] * 3 + [ANY] * 8,
         scratch_shapes=[
-            pltpu.VMEM((MICRO, slot, width), F32),
-            pltpu.VMEM((MICRO, slot, width), F32),
+            pltpu.VMEM(rows, BF16),
+            pltpu.VMEM(rows, BF16),
+            pltpu.VMEM(rows, BF16),
+            pltpu.VMEM(rows, BF16),
+            pltpu.VMEM(rows, BF16),
             pltpu.VMEM(LEAD + (64, 128), BF16),
             pltpu.VMEM(LEAD + (64, 128), BF16),
             pltpu.VMEM(LEAD + (64, 128), BF16),
-            pltpu.VMEM(LEAD + (64, 384), BF16),
+            pltpu.VMEM(LEAD + (64, 256), BF16),
+            pltpu.VMEM(LEAD + (64, 256), BF16),
             pltpu.VMEM(LEAD + (64, 256), BF16),
             pltpu.VMEM(LEAD + (64, 128), BF16),
             pltpu.VMEM(LEAD + (64, 128), BF16),
             pltpu.VMEM(LEAD + (64, 128), BF16),
-            pltpu.VMEM(LEAD + (64, 128), BF16),
-            pltpu.VMEM((64, 384), BF16),
+            pltpu.VMEM((64, 256), BF16),
             pltpu.VMEM((32, 128), BF16),
             pltpu.VMEM(LEAD + (32, 128), BF16),
             pltpu.VMEM((GROUP, 1, 384), F32),
@@ -860,7 +884,6 @@
             pltpu.VMEM(attended, BF16),
             pltpu.VMEM((count, width), F32),
             pltpu.VMEM((count, width), F32),
-            pltpu.VMEM((count, width), BF16),
             pltpu.VMEM((count, width), BF16),
             pltpu.VMEM((4, 8, 2, 64, 256), BF16),
             pltpu.VMEM((count, width), F32),
@@ -875,14 +898,14 @@
             pltpu.SemaphoreType.DMA((MICRO,)),
             pltpu.SemaphoreType.DMA,
             pltpu.SemaphoreType.DMA,
-            pltpu.SemaphoreType.DMA((10,)),
+            pltpu.SemaphoreType.DMA((11,)),
             pltpu.SemaphoreType.DMA((5,)),
             pltpu.SemaphoreType.DMA((5,)),
             pltpu.SemaphoreType.DMA,
             pltpu.SemaphoreType.DMA,
             pltpu.SemaphoreType.DMA,
-            pltpu.SemaphoreType.DMA,
-            pltpu.SemaphoreType.DMA,
+            pltpu.SemaphoreType.DMA((3,)),
+            pltpu.SemaphoreType.DMA((3,)),
         ],
         compiler_params=pltpu.CompilerParams(
             collective_id=0, has_side_effects=True, vmem_limit_bytes=VMEM_LIMIT
@@ -899,17 +922,18 @@
         turned_in,
         act_in,
         qkv_in,
+        x_in,
         d_middle_ref,
-        x_ref,
         vectors_ref,
         sums_ref,
-        input_grad_out,
         qkv_grad,
         out_grad,
         fc1_grad,
         fc2_grad,
         totals_out,
+        input_grad_out,
         rows,
+        box,
         pool,
         turned,
         attended,
@@ -927,18 +951,22 @@
         load_sem,
         reduce_send,
         reduce_recv,
+        send_sem,
+        recv_sem,
         back_send,
         back_recv,
         sib_send,
         sib_recv,
         sum_send,
         sum_recv,
+        swap_send,
+        swap_recv,
     ) = sems
     me = place()
-    f, t = lax.axis_index("fsdp"), lax.axis_index("tp")
+    t = 2 * me["x"] + me["c"]
     other = device_at(sibling(me))
     met = greet(me)
-    tokens, slot = x_ref.shape[1], rows.shape[1]
+    slot = rows.shape[1]
     count = MICRO * slot
     parts = [
         Reduce(
@@ -966,10 +994,11 @@
     for i in range(2):
         load(("dup", i), act_in.at[i, :, 1], pool.at[2 + i, :, kept])
     load("images", images_in, images)
-    load("d_attended", d_attended_in, d_attended)
+    load("own", d_attended_in.at[t], d_attended.at[t])
     for i in range(2):
         load(("act", i), act_in.at[i, :, 0], pool.at[i, :, kept])
     load("attended", attended_in, attended)
+    load("rows", x_in, rows)
     sums[0, 0] = sums_ref[...]
 
     def both_cores(kind, values):
@@ -1016,15 +1045,25 @@
     loads["turned"].wait()
     for i in range(2):
         loads["dup", i].wait()
+    met()
+    for m in range(MICRO):
+        for k in range(GROUP - 1):
+            target = lax.rem(t + k + 1, GROUP)
+            remote(
+                d_attended_in.at[target, m],
+                d_attended.at[t, m],
+                send_sem,
+                recv_sem.at[m],
+                member(me, target),
+            )
     lax.fori_loop(0, GROUP, grads_up(0), 0)
-    met()
     wide[0].stage_far()
     totals[0].speak(0)
     lax.fori_loop(0, GROUP, grads_up(1), 0)
     wide[1].stage_far()
     loads["images"].wait()
-    loads["d_attended"].wait()
-    hidden = hidden_rows(GROUP * slot, slot, tokens)
+    loads["own"].wait()
+    hidden = hidden_rows(GROUP * slot, slot, TOKENS)
 
     def reply(m, k):
         target = lax.rem(t + k + 1, GROUP)
@@ -1033,11 +1072,12 @@
             d_images.at[0, t, m],
             back_send,
             back_recv.at[k],
-            device_id=(f, target),
+            device_id=member(me, target),
             device_id_type=MESH,
         )
 
     for m in range(MICRO):
+        take(d_attended.at[: GROUP - 1, m], recv_sem.at[m])
         results = attend_back(
             images[:, m].reshape(GROUP * slot, 384),
             d_attended[:, m].reshape(GROUP * slot, 128),
@@ -1064,8 +1104,8 @@
             totals[0].pass_on(1)
     for part in wide[2:]:
         part.stage_near()
-    padded_rows(x_ref, rows)
-    normed, inverse = norm_stats(rows[...].reshape(count, rows.shape[-1]))
+    loads["rows"].wait()
+    normed, inverse = norm_stats(rows[...].reshape(count, rows.shape[-1]).astype(F32))
     totals[0].pass_on(2)
     wide[0].stage_mid()
 
@@ -1116,7 +1156,9 @@
     totals[1].speak(0)
     totals[0].hear(3)
     result = d_middle_ref[...] + norm_back(gradient, normed, inverse, vectors_ref[0:1, :])
-    input_grad_out[...] = result.reshape(rows.shape)[:, :tokens].astype(BF16)
+    box[...] = result.astype(BF16).reshape(box.shape)
+    swap = Swap(me, swap_send, swap_recv)
+    swap.start(box, input_grad_out)
     totals[1].pass_on(0)
     for part in late:
         part.stage_mid()
@@ -1144,13 +1186,16 @@
         total.sent()
     take(d_images.at[1], sib_send)
     take(outbox.at[:, : GROUP - 1], back_send)
+    take(d_attended.at[: GROUP - 1], send_sem)
+    swap.sent(box)
+    take(input_grad_out, swap_recv)
 
 
 REDUCED = (
     (ORDERS[2], 256),
+    (ORDERS[0], 256),
+    (ORDERS[1], 128),
     (ORDERS[2], 256),
-    (ORDERS[2], 128),
-    (ORDERS[1], 256),
     (ORDERS[0], 256),
     (ORDERS[0], 128),
     (ORDERS[1], 128),
@@ -1158,8 +1203,9 @@
 )
 
 
-def backward(d_attended, images, attended, turned, act, qkv, d_middle, x, vectors, sums, slot):
+def backward(d_attended, images, attended, turned, act, qkv, x, d_middle, vectors, sums):
     width = x.shape[-1]
+    slot = x.shape[1]
     count = MICRO * slot
     scratch = []
     for order, lanes in REDUCED:
@@ -1167,17 +1213,18 @@
     return pl.pallas_call(
         backward_kernel,
         out_shape=[
-            jax.ShapeDtypeStruct(x.shape, BF16),
             jax.ShapeDtypeStruct((3, 64, 128), F32),
             jax.ShapeDtypeStruct((64, 128), F32),
             jax.ShapeDtypeStruct((64, 512), F32),
             jax.ShapeDtypeStruct((64, 512), F32),
             jax.ShapeDtypeStruct((16, width), F32),
+            jax.ShapeDtypeStruct(x.shape, BF16),
         ],
-        in_specs=[ANY] * 6 + [VMEM] * 4,
-        out_specs=[VMEM] * 6,
+        in_specs=[ANY] * 7 + [VMEM] * 3,
+        out_specs=[VMEM] * 5 + [ANY],
         scratch_shapes=[
-            pltpu.VMEM((MICRO, slot, width), F32),
+            pltpu.VMEM(x.shape, BF16),
+            pltpu.VMEM(x.shape, BF16),
             pltpu.VMEM((4, GROUP, width, 128), BF16),
             pltpu.VMEM(turned.shape, BF16),
             pltpu.VMEM(attended.shape, BF16),
@@ -1191,21 +1238,25 @@
         ]
         + scratch
         + [
-            pltpu.SemaphoreType.DMA((11,)),
+            pltpu.SemaphoreType.DMA((12,)),
             pltpu.SemaphoreType.DMA((len(REDUCED), Reduce.sends)),
             pltpu.SemaphoreType.DMA((len(REDUCED), Reduce.recvs)),
+            pltpu.SemaphoreType.DMA,
+            pltpu.SemaphoreType.DMA((MICRO,)),
             pltpu.SemaphoreType.DMA,
             pltpu.SemaphoreType.DMA((GROUP,)),
             pltpu.SemaphoreType.DMA,
             pltpu.SemaphoreType.DMA,
             pltpu.SemaphoreType.DMA((2, 4)),
             pltpu.SemaphoreType.DMA((2, 4)),
+            pltpu.SemaphoreType.DMA,
+            pltpu.SemaphoreType.DMA,
         ],
         compiler_params=pltpu.CompilerParams(
             collective_id=1, has_side_effects=True, vmem_limit_bytes=VMEM_LIMIT
         ),
         name="backward",
-    )(d_attended, images, attended, turned, act, qkv, d_middle, x, vectors, sums)
+    )(d_attended, images, attended, turned, act, qkv, x, d_middle, vectors, sums)
 
 
 def finish_kernel(
@@ -1227,8 +1278,9 @@
     hidden_out,
 ):
     f, t = lax.axis_index("fsdp"), lax.axis_index("tp")
-    result_out[...] = result[...]
-    input_grad_out[...] = input_grad[...]
+    tokens = result_out.shape[1]
+    result_out[...] = result[:, :tokens]
+    input_grad_out[...] = input_grad[:, :tokens]
     qkv_out[...] = qkv_grad[...]
     out_out[...] = out_grad[...]
     fc1_out[...] = fc1_grad[...]
@@ -1255,7 +1307,8 @@
 
 def finish(result, input_grad, qkv_grad, out_grad, fc1_grad, fc2_grad, totals):
     arrays = (result, input_grad, qkv_grad, out_grad, fc1_grad, fc2_grad)
-    shapes = [jax.ShapeDtypeStruct(a.shape, a.dtype) for a in arrays]
+    rows = jax.ShapeDtypeStruct((MICRO, TOKENS, result.shape[-1]), BF16)
+    shapes = [rows, rows] + [jax.ShapeDtypeStruct(a.shape, a.dtype) for a in arrays[2:]]
     shapes += [
         jax.ShapeDtypeStruct((6, 1, 8), F32),
         jax.ShapeDtypeStruct((2, 2, 4), F32),
@@ -1294,16 +1347,17 @@
     small = [ln1_gain, ln1_bias, out_bias, ln2_gain, ln2_bias, fc2_bias]
     small = [v.reshape(1, 8) for v in small] + [qv_bias, fc1_bias.T]
     (
-        result,
         d_middle,
         vectors,
         sums,
+        result,
         d_attended,
         images,
         attended,
         turned,
         act,
         qkv,
+        x_rows,
     ) = forward(
         x,
         cotangent.reshape(x.shape),
@@ -1315,18 +1369,17 @@
         small,
         slot,
     )
-    input_grad, qkv_grad, out_grad, fc1_grad, fc2_grad, total = backward(
+    qkv_grad, out_grad, fc1_grad, fc2_grad, total, input_grad = backward(
         d_attended,
         images,
         attended,
         turned,
         act,
         qkv.reshape(3, GROUP, width, 128),
+        x_rows,
         d_middle,
-        x,
         vectors,
         sums,
-        slot,
     )
     result, input_grad, qkv_grad, out_grad, fc1_grad, fc2_grad, own, pair, hidden_grad = finish(
         result, input_grad, qkv_grad, out_grad, fc1_grad, fc2_grad, total

time: 217 us -> 201 us (0.926)
  Pallas kernels: 213 us -> 197 us
    pallas_call x2, Pallas kernels: 211 us -> 195 us  [the longest x1 100 us: forward(): pl.pallas_call(forward_kernel, out_shape=[jax.ShapeDtypeStruct((count, wi...]
where the time goes in v5:
time: 201 us; the launch traced here: 200 us
  Pallas kernels  197 us (98%)
  local copies, waits for them, and re-layouts  2.55 us (1%)
    pallas_call x1, Pallas kernels, forward(): pl.pallas_call(forward_kernel, out_shape=[jax.ShapeDtypeStruct((count, wi...  100 us
    pallas_call x1, Pallas kernels, backward(): pl.pallas_call(backward_kernel, out_shape=[jax.ShapeDtypeStruct((3, 64, 1...  94.3 us

profile of v5, /device:TPU:0, one launch (start us, length us, event | category | flops | bytes accessed | tf_op | source)
XLA Modules:
  0.0 200.3 jit_solution(13217867865132569277)
XLA Ops:
  0.7 100.3 %forward.1 = (f32[240,1024]{1,0:T(8,128)}, f32[8,1024]{1,0:T(8,128)}, f32[8,1024]{1,0:T(8,128)}, bf16[3,80,1024]{2,1,0:T(8,128)(2,1)}, bf16[8,3,80,128]{3,2,1,0:...) custom-call(bf16[3,72,1024]{2,1,0:T(8,128)(2,1)} %bitcast.34, ...), custom_call_target="tpu_custom_call" | custom-call | tf_op jit(solution)/shard_map/forward/pallas_call | solution.py:843
  101.0 94.3 %backward.1 = (f32[3,64,128]{2,1,0:T(8,128)}, f32[64,128]{1,0:T(8,128)}, f32[64,512]{1,0:T(8,128)}, f32[64,512]{1,0:T(8,128)}, f32[16,1024]{1,0:T(8,128)}, /*index=5*/bf16[3,80,1024]{2,1,0:T(8,128)(2,1)}) custom-call(bf16[8,3,80,128]{3,2,1,0:T(8,128)(2,1)} %get-tuple-element.41.refs_0_, bf16[8,3,80,384]{3,2,1,0:T(8,128)(2,1)} %get-tuple-element.42.refs_1_, ...), custom_call_target="tpu_custom_call" | custom-call | tf_op jit(solution)/shard_map/backward/pallas_call | solution.py:1213
  195.3 2.4 %finish.1 = (bf16[3,72,1024]{2,1,0:T(8,128)(2,1)}, bf16[3,72,1024]{2,1,0:T(8,128)(2,1)}, f32[3,64,128]{2,1,0:T(8,128)}, f32[64,128]{1,0:T(8,128)}, f32[64,512]{1...) custom-call(bf16[3,80,1024]{2,1,0:T(8,128)(2,1)} %get-tuple-element.40.result, ...), custom_call_target="tpu_custom_call" | custom-call | tf_op jit(solution)/shard_map/finish/pallas_call | solution.py:1317
  197.7 1.3 copy.31
  199.1 1.2 slice_bitcast_fusion

commit v6 on v5

--- a/solution.py
+++ b/solution.py
@@ -462,11 +462,11 @@
     "swap": (("E", "third"), ("A", "second"), ("E", "far")),
     "norm": (("A", "third"), ("V", "rest"), ("V", "last"), ("V", "done")),
     "table": (("B", "second"), ("N", "rest"), ("N", "last"), ("A", "far"), ("N", "done")),
-    "project": (("A", "rest"), ("B", "third"), ("A", "last")),
-    "image 0": (("B", "far"),),
-    "image 1": (("B", "rest"),),
-    "image 2": (("B", "last"),),
-    "reply": (("A", "done"),),
+    "project": (("A", "rest"), ("B", "third")),
+    "image 0": (("A", "last"),),
+    "image 1": (("B", "far"),),
+    "image 2": (("B", "rest"),),
+    "reply": (("A", "done"), ("B", "last")),
     "half 0": (),
     "half 1": (("B", "done"),),
 }
@@ -914,6 +914,27 @@
     )(x, cotangent, valid, qkv_block, out_block, fc1_block, fc2_block, *small)
 
 
+BACK_SCHEDULE = {
+    "image 0": (("down", 0), (0, -1), ("U", "stage_near")),
+    "image 1": (("V", "stage_near"), (0, 0)),
+    "image 2": (("D", "stage_near"), (0, 1)),
+    "norm": (("U", "stage_mid"), ("V", "stage_mid"), ("D", "stage_mid"), (0, 2)),
+    "late": ((0, 3), ("L", "stage_near")),
+    "rows": (
+        (1, 0),
+        ("L", "stage_mid"),
+        (1, 1),
+        ("U", "stage_tail"),
+        ("V", "stage_tail"),
+        ("D", "stage_tail"),
+        ("L", "stage_tail"),
+        (1, 2),
+    ),
+    "wide": (),
+    "end": ((1, 3),),
+}
+
+
 def backward_kernel(*refs):
     (
         d_attended_in,
@@ -1058,7 +1079,6 @@
             )
     lax.fori_loop(0, GROUP, grads_up(0), 0)
     wide[0].stage_far()
-    totals[0].speak(0)
     lax.fori_loop(0, GROUP, grads_up(1), 0)
     wide[1].stage_far()
     loads["images"].wait()
@@ -1075,6 +1095,32 @@
             device_id=member(me, target),
             device_id_type=MESH,
         )
+
+    def down():
+        for i in range(2):
+            loads["act", i].wait()
+        loads["attended"].wait()
+        lax.fori_loop(0, GROUP, grads_down, 0)
+        for part in wide[2:]:
+            part.stage_far()
+        for i in range(3):
+            load(("weight", i), qkv_in.at[i], pool.at[i])
+
+    groups = {"U": wide[:1], "V": wide[1:2], "D": wide[2:], "L": late}
+
+    def run(point):
+        for name, stage in BACK_SCHEDULE[point]:
+            if name == "down":
+                down()
+            elif name in groups:
+                for part in groups[name]:
+                    getattr(part, stage)()
+            elif stage < 0:
+                totals[name].speak(0)
+            elif stage < 3:
+                totals[name].pass_on(stage)
+            else:
+                totals[name].hear(3)
 
     for m in range(MICRO):
         take(d_attended.at[: GROUP - 1, m], recv_sem.at[m])
@@ -1088,26 +1134,10 @@
         for k in range(GROUP - 1):
             reply(m, k).start()
         d_images[0, t, m] = outbox[m, t]
-        if m == 0:
-            for i in range(2):
-                loads["act", i].wait()
-            loads["attended"].wait()
-            lax.fori_loop(0, GROUP, grads_down, 0)
-            for part in wide[2:]:
-                part.stage_far()
-            for i in range(3):
-                load(("weight", i), qkv_in.at[i], pool.at[i])
-            wide[0].stage_near()
-            totals[0].pass_on(0)
-        if m == 1:
-            wide[1].stage_near()
-            totals[0].pass_on(1)
-    for part in wide[2:]:
-        part.stage_near()
+        run(("image 0", "image 1", "image 2")[m])
     loads["rows"].wait()
     normed, inverse = norm_stats(rows[...].reshape(count, rows.shape[-1]).astype(F32))
-    totals[0].pass_on(2)
-    wide[0].stage_mid()
+    run("norm")
 
     def share(k):
         source = lax.rem(t + k + 1, GROUP)
@@ -1117,7 +1147,16 @@
     for k in reversed(range(GROUP - 1)):
         take(d_images.at[0, 0], back_recv.at[GROUP - 2 - k])
         share(k)
-    wide[1].stage_mid()
+    for i in range(3):
+        loads["weight", i].wait()
+    d_norm[...] = jnp.zeros_like(d_norm)
+
+    def project_back(index, carry):
+        weights = jnp.concatenate([pool[i, index] for i in range(3)], axis=1)
+        d_norm[...] += mm(d_images[0, index].reshape(count, 384), weights, NT)
+        return carry
+
+    lax.fori_loop(0, GROUP, project_back, 0)
     take(d_images.at[1], sib_recv)
 
     def grads_late(index, carry):
@@ -1129,22 +1168,6 @@
     lax.fori_loop(0, GROUP, grads_late, 0)
     for part in late:
         part.stage_far()
-    for part in wide[2:]:
-        part.stage_mid()
-    for i in range(3):
-        loads["weight", i].wait()
-    d_norm[...] = jnp.zeros_like(d_norm)
-
-    def project_back(index, carry):
-        weights = jnp.concatenate([pool[i, index] for i in range(3)], axis=1)
-        d_norm[...] += mm(d_images[0, index].reshape(count, 384), weights, NT)
-        return carry
-
-    lax.fori_loop(0, GROUP, project_back, 0)
-    for part in late:
-        part.stage_near()
-    for part in wide[:2]:
-        part.stage_tail()
     gradient = d_norm[...]
     sums[1, 0, 0:1, :] = jnp.sum(gradient * normed, 0, keepdims=True)
     sums[1, 0, 1:2, :] = jnp.sum(gradient, 0, keepdims=True)
@@ -1154,19 +1177,12 @@
         sums[1, 0, 3:4, 128 * index : 128 * index + 128] = grads[:, 256:]
     sums[1, 0, 4:8, :] = jnp.zeros((4, sums.shape[-1]), F32)
     totals[1].speak(0)
-    totals[0].hear(3)
+    run("late")
     result = d_middle_ref[...] + norm_back(gradient, normed, inverse, vectors_ref[0:1, :])
     box[...] = result.astype(BF16).reshape(box.shape)
     swap = Swap(me, swap_send, swap_recv)
     swap.start(box, input_grad_out)
-    totals[1].pass_on(0)
-    for part in late:
-        part.stage_mid()
-    for part in wide[2:]:
-        part.stage_tail()
-    totals[1].pass_on(1)
-    for part in late:
-        part.stage_tail()
+    run("rows")
     fc1_grad[:, :256] = wide[0].stage_out()
     fc1_grad[:, 256:] = wide[1].stage_out()
     fc2_grad[:, :128] = wide[2].stage_out()
@@ -1174,10 +1190,10 @@
     value = wide[4].stage_out()
     fc2_grad[:, 384:] = value[:, :128]
     out_grad[...] = value[:, 128:]
-    totals[1].pass_on(2)
+    run("wide")
     for i in range(3):
         qkv_grad[i] = late[i].stage_out()
-    totals[1].hear(3)
+    run("end")
     totals_out[0:8, :] = sums[0, 4]
     totals_out[8:16, :] = sums[1, 4]
     for part in parts:

time: 201 us -> 190 us (0.945)
  Pallas kernels: 197 us -> 186 us
    pallas_call x1, Pallas kernels: 94.3 us -> 86 us  [backward(): pl.pallas_call(backward_kernel, out_shape=[jax.ShapeDtypeStruct((3, 64, 1...]
    pallas_call x1, Pallas kernels: 100 us -> 98.1 us  [forward(): pl.pallas_call(forward_kernel, out_shape=[jax.ShapeDtypeStruct((count, wi...]
where the time goes in v6:
time: 190 us
  Pallas kernels  186 us (98%)
  local copies, waits for them, and re-layouts  2.55 us (1%)
    pallas_call x1, Pallas kernels, forward(): pl.pallas_call(forward_kernel, out_shape=[jax.ShapeDtypeStruct((count, wi...  98.1 us
    pallas_call x1, Pallas kernels, backward(): pl.pallas_call(backward_kernel, out_shape=[jax.ShapeDtypeStruct((3, 64, 1...  86 us

profile of v6, /device:TPU:0, one launch (start us, length us, event | category | flops | bytes accessed | tf_op | source)
XLA Modules:
  0.0 189.7 jit_solution(13788332435516847475)
XLA Ops:
  0.7 98.1 %forward.1 = (f32[240,1024]{1,0:T(8,128)}, f32[8,1024]{1,0:T(8,128)}, f32[8,1024]{1,0:T(8,128)}, bf16[3,80,1024]{2,1,0:T(8,128)(2,1)}, bf16[8,3,80,128]{3,2,1,0:...) custom-call(bf16[3,72,1024]{2,1,0:T(8,128)(2,1)} %bitcast.34, ...), custom_call_target="tpu_custom_call" | custom-call | tf_op jit(solution)/shard_map/forward/pallas_call | solution.py:843
  98.7 86.0 %backward.1 = (f32[3,64,128]{2,1,0:T(8,128)}, f32[64,128]{1,0:T(8,128)}, f32[64,512]{1,0:T(8,128)}, f32[64,512]{1,0:T(8,128)}, f32[16,1024]{1,0:T(8,128)}, /*index=5*/bf16[3,80,1024]{2,1,0:T(8,128)(2,1)}) custom-call(bf16[8,3,80,128]{3,2,1,0:T(8,128)(2,1)} %get-tuple-element.41.refs_0_, bf16[8,3,80,384]{3,2,1,0:T(8,128)(2,1)} %get-tuple-element.42.refs_1_, ...), custom_call_target="tpu_custom_call" | custom-call | tf_op jit(solution)/shard_map/backward/pallas_call | solution.py:1229
  184.7 2.4 %finish.1 = (bf16[3,72,1024]{2,1,0:T(8,128)(2,1)}, bf16[3,72,1024]{2,1,0:T(8,128)(2,1)}, f32[3,64,128]{2,1,0:T(8,128)}, f32[64,128]{1,0:T(8,128)}, f32[64,512]{1...) custom-call(bf16[3,80,1024]{2,1,0:T(8,128)(2,1)} %get-tuple-element.40.result, ...), custom_call_target="tpu_custom_call" | custom-call | tf_op jit(solution)/shard_map/finish/pallas_call | solution.py:1333
  187.2 1.3 copy.31
  188.5 1.2 slice_bitcast_fusion

commit v7 on v6

--- a/solution.py
+++ b/solution.py
@@ -456,6 +456,7 @@
     ref[kind] = padded.T.reshape(ref.shape[1:])
 
 
+SLABS = 4
 SCHEDULE = {
     "start": (("E", "first"),),
     "first": (("A", "first"), ("E", "second"), ("B", "first")),
@@ -463,10 +464,10 @@
     "norm": (("A", "third"), ("V", "rest"), ("V", "last"), ("V", "done")),
     "table": (("B", "second"), ("N", "rest"), ("N", "last"), ("A", "far"), ("N", "done")),
     "project": (("A", "rest"), ("B", "third")),
-    "image 0": (("A", "last"),),
+    "image 0": (("A", "last"), ("E", "sent")),
     "image 1": (("B", "far"),),
     "image 2": (("B", "rest"),),
-    "reply": (("A", "done"), ("B", "last")),
+    "reply": (("A", "done"), ("B", "last"), ("A", "sent")),
     "half 0": (),
     "half 1": (("B", "done"),),
 }
@@ -499,8 +500,7 @@
         up_b,
         side_a,
         down_xa,
-        down_xb,
-        down_zb,
+        down_b,
         side_own,
         small_own,
         small,
@@ -564,8 +564,7 @@
     ]
     second_half = [
         gather(ORDERS[0], fc1_in.at[:, 256:], up_b),
-        gather(ORDERS[2], fc2_in.at[:, 256:384], down_xb),
-        gather(ORDERS[2], fc2_in.at[:, 384:], down_zb),
+        gather(ORDERS[2], fc2_in.at[:, 256:], down_b),
     ]
     groups = {
         "V": [vector],
@@ -749,22 +748,24 @@
     forward_sum[...] = jnp.zeros_like(forward_sum)
     back_sum[...] = jnp.zeros_like(back_sum)
 
-    def ship(pair, h):
-        piece = act_box.at[pl.ds(2 * pair, 2), :, pl.ds(2 * count * h, 2 * count)]
-        at = (pl.ds(2 * pair, 2), slice(None), pl.ds(2 * count * h, 2 * count))
+    def ship(step, h):
+        at = (pl.ds(SLABS * step, SLABS), slice(None), pl.ds(2 * count * h, 2 * count))
+        piece = act_box.at[at]
         pltpu.make_async_copy(piece, act_out.at[(0,) + at], ff_local).start()
         remote(piece, act_out.at[(1,) + at], ff_send, ff_recv, other)
 
     for h in range(2):
         run(("half 0", "half 1")[h])
 
-        def feed_forward(pair, carry):
-            slabs = [2 * pair, 2 * pair + 1]
+        def feed_forward(step, carry):
+            slabs = [SLABS * step + n for n in range(SLABS)]
             up_weight = jnp.concatenate([blocks_of((up_a, up_b)[h], i) for i in slabs], axis=1)
             down = []
             for i in slabs:
-                down.append(blocks_of((down_xa, down_xb)[h], i))
-                down.append(blocks_of(side_a, i)[:, 128:] if h == 0 else blocks_of(down_zb, i))
+                if h == 0:
+                    down += [blocks_of(down_xa, i), blocks_of(side_a, i)[:, 128:]]
+                else:
+                    down.append(blocks_of(down_b, i))
             down_weight = jnp.concatenate(down, axis=1)
             biases = [hidden_bias[i, :, 256 * h : 256 * h + 256] for i in slabs]
             up_proj = mm(low_two[...], up_weight) + jnp.concatenate(biases, axis=1)
@@ -780,12 +781,12 @@
                     act_box[i, 0, at] = activated[:, lanes]
                     act_box[i, 1, at] = d_up[:, lanes]
                 hidden_sums[i, :, 256 * h : 256 * h + 256] = column_sums[:, 256 * n : 256 * n + 256]
-            ship(pair, h)
+            ship(step, h)
             forward_sum[...] += mm(activated, down_weight, NT)
             back_sum[...] += mm(d_up, up_weight, NT)
             return carry
 
-        lax.fori_loop(0, GROUP // 2, feed_forward, 0)
+        lax.fori_loop(0, GROUP // SLABS, feed_forward, 0)
     output = (middle[...] + forward_sum[...] + vectors[5:6, :]).astype(BF16)
     result_box[...] = output.reshape(result_box.shape)
     swaps[2].start(result_box, result_out)
@@ -820,7 +821,7 @@
     take(act_box, ff_local)
     take(act_box, ff_send)
     take(act_box, ff_recv)
-    for part in made:
+    for part in second_half:
         part.sent()
     take(outbox.at[: GROUP - 1], send_sem)
     take(attended_box.at[:, : GROUP - 1], back_send)
@@ -870,8 +871,7 @@
             pltpu.VMEM(LEAD + (64, 256), BF16),
             pltpu.VMEM(LEAD + (64, 256), BF16),
             pltpu.VMEM(LEAD + (64, 128), BF16),
-            pltpu.VMEM(LEAD + (64, 128), BF16),
-            pltpu.VMEM(LEAD + (64, 128), BF16),
+            pltpu.VMEM(LEAD + (64, 256), BF16),
             pltpu.VMEM((64, 256), BF16),
             pltpu.VMEM((32, 128), BF16),
             pltpu.VMEM(LEAD + (32, 128), BF16),
@@ -915,6 +915,7 @@
 
 
 BACK_SCHEDULE = {
+    "early": True,
     "image 0": (("down", 0), (0, -1), ("U", "stage_near")),
     "image 1": (("V", "stage_near"), (0, 0)),
     "image 2": (("D", "stage_near"), (0, 1)),
@@ -930,7 +931,7 @@
         ("L", "stage_tail"),
         (1, 2),
     ),
-    "wide": (),
+    "wide": (("U", "sent"), ("V", "sent"), ("D", "sent")),
     "end": ((1, 3),),
 }
 
@@ -1079,8 +1080,9 @@
             )
     lax.fori_loop(0, GROUP, grads_up(0), 0)
     wide[0].stage_far()
-    lax.fori_loop(0, GROUP, grads_up(1), 0)
-    wide[1].stage_far()
+    if BACK_SCHEDULE["early"]:
+        lax.fori_loop(0, GROUP, grads_up(1), 0)
+        wide[1].stage_far()
     loads["images"].wait()
     loads["own"].wait()
     hidden = hidden_rows(GROUP * slot, slot, TOKENS)
@@ -1112,6 +1114,9 @@
         for name, stage in BACK_SCHEDULE[point]:
             if name == "down":
                 down()
+            elif name == "up":
+                lax.fori_loop(0, GROUP, grads_up(1), 0)
+                wide[1].stage_far()
             elif name in groups:
                 for part in groups[name]:
                     getattr(part, stage)()
@@ -1196,7 +1201,7 @@
     run("end")
     totals_out[0:8, :] = sums[0, 4]
     totals_out[8:16, :] = sums[1, 4]
-    for part in parts:
+    for part in late:
         part.sent()
     for total in totals:
         total.sent()
@@ -1289,10 +1294,9 @@
     out_out,
     fc1_out,
     fc2_out,
-    vectors_out,
-    pair_out,
-    hidden_out,
+    *rest,
 ):
+    vectors_out, (pair_out, hidden_out) = rest[:6], rest[6:]
     f, t = lax.axis_index("fsdp"), lax.axis_index("tp")
     tokens = result_out.shape[1]
     result_out[...] = result[:, :tokens]
@@ -1304,7 +1308,7 @@
     width = totals.shape[-1]
     own = pltpu.roll(totals[...], lax.rem(width - (f * 8 + t) * 8, width), 1)
     for number, row in enumerate((8, 9, 0, 1, 2, 3)):
-        vectors_out[number] = own[row : row + 1, :8]
+        vectors_out[number][...] = own[row : row + 1, :8]
     own = pltpu.roll(totals[...], lax.rem(width - t * 128 - f * 4, width), 1)
     for kind in range(2):
         for head in range(2):
@@ -1317,24 +1321,24 @@
     row = pltpu.roll(
         jnp.broadcast_to(row, (8, width)), lax.rem(width - 512 * lax.rem(t, 2) - f * 4, width), 1
     )
-    for j in range(8):
-        hidden_out[j : j + 1, :] = row[0:1, 64 * j : 64 * j + 4]
+    turned = jnp.concatenate([row[0:1, 64 * j : 64 * j + 128] for j in range(8)], axis=0)
+    hidden_out[...] = turned.T[:4]
 
 
 def finish(result, input_grad, qkv_grad, out_grad, fc1_grad, fc2_grad, totals):
     arrays = (result, input_grad, qkv_grad, out_grad, fc1_grad, fc2_grad)
     rows = jax.ShapeDtypeStruct((MICRO, TOKENS, result.shape[-1]), BF16)
     shapes = [rows, rows] + [jax.ShapeDtypeStruct(a.shape, a.dtype) for a in arrays[2:]]
+    shapes += [jax.ShapeDtypeStruct((1, 8), F32)] * 6
     shapes += [
-        jax.ShapeDtypeStruct((6, 1, 8), F32),
         jax.ShapeDtypeStruct((2, 2, 4), F32),
-        jax.ShapeDtypeStruct((8, 4), F32),
+        jax.ShapeDtypeStruct((4, 8), F32),
     ]
     return pl.pallas_call(
         finish_kernel,
         out_shape=shapes,
         in_specs=[VMEM] * 7,
-        out_specs=[VMEM] * 9,
+        out_specs=[VMEM] * 14,
         compiler_params=pltpu.CompilerParams(vmem_limit_bytes=VMEM_LIMIT),
         name="finish",
     )(*arrays, totals)
@@ -1397,7 +1401,7 @@
         vectors,
         sums,
     )
-    result, input_grad, qkv_grad, out_grad, fc1_grad, fc2_grad, own, pair, hidden_grad = finish(
+    result, input_grad, qkv_grad, out_grad, fc1_grad, fc2_grad, *own, pair, hidden_grad = finish(
         result, input_grad, qkv_grad, out_grad, fc1_grad, fc2_grad, total
     )
     own = [own[i].reshape(8) for i in range(6)]
@@ -1413,7 +1417,7 @@
         own[3],
         own[4],
         fc1_grad,
-        hidden_grad,
+        hidden_grad.T,
         fc2_grad.T,
         own[5],
     )

time: 190 us -> 186 us (0.979)
  local copies, waits for them, and re-layouts: 2.55 us -> 0 us
where the time goes in v7:
time: 186 us
  Pallas kernels  185 us (99%)
    pallas_call x1, Pallas kernels, forward(): pl.pallas_call(forward_kernel, out_shape=[jax.ShapeDtypeStruct((count, wi...  97 us
    pallas_call x1, Pallas kernels, backward(): pl.pallas_call(backward_kernel, out_shape=[jax.ShapeDtypeStruct((3, 64, 1...  85.1 us

profile of v7, /device:TPU:0, one launch (start us, length us, event | category | flops | bytes accessed | tf_op | source)
XLA Modules:
  0.0 185.5 jit_solution(1733451573834903309)
XLA Ops:
  0.7 97.0 %forward.1 = (f32[240,1024]{1,0:T(8,128)}, f32[8,1024]{1,0:T(8,128)}, f32[8,1024]{1,0:T(8,128)}, bf16[3,80,1024]{2,1,0:T(8,128)(2,1)}, bf16[8,3,80,128]{3,2,1,0:...) custom-call(bf16[3,72,1024]{2,1,0:T(8,128)(2,1)} %bitcast.29, ...), custom_call_target="tpu_custom_call" | custom-call | tf_op jit(solution)/shard_map/forward/pallas_call | solution.py:844
  97.7 85.1 %backward.1 = (f32[3,64,128]{2,1,0:T(8,128)}, f32[64,128]{1,0:T(8,128)}, f32[64,512]{1,0:T(8,128)}, f32[64,512]{1,0:T(8,128)}, f32[16,1024]{1,0:T(8,128)}, /*index=5*/bf16[3,80,1024]{2,1,0:T(8,128)(2,1)}) custom-call(bf16[8,3,80,128]{3,2,1,0:T(8,128)(2,1)} %get-tuple-element.46.refs_0_, bf16[8,3,80,384]{3,2,1,0:T(8,128)(2,1)} %get-tuple-element.47.refs_1_, ...), custom_call_target="tpu_custom_call" | custom-call | tf_op jit(solution)/shard_map/backward/pallas_call | solution.py:1234
  182.8 2.6 %finish.1 = (bf16[3,72,1024]{2,1,0:T(8,128)(2,1)}, bf16[3,72,1024]{2,1,0:T(8,128)(2,1)}, f32[3,64,128]{2,1,0:T(8,128)}, f32[64,128]{1,0:T(8,128)}, f32[64,512]{1...) custom-call(bf16[3,80,1024]{2,1,0:T(8,128)(2,1)} %get-tuple-element., ...), custom_call_target="tpu_custom_call" | custom-call | tf_op jit(solution)/shard_map/finish/pallas_call | solution.py:1337

commit v8 on v7

--- a/solution.py
+++ b/solution.py
@@ -460,10 +460,10 @@
 SCHEDULE = {
     "start": (("E", "first"),),
     "first": (("A", "first"), ("E", "second"), ("B", "first")),
-    "swap": (("E", "third"), ("A", "second"), ("E", "far")),
-    "norm": (("A", "third"), ("V", "rest"), ("V", "last"), ("V", "done")),
-    "table": (("B", "second"), ("N", "rest"), ("N", "last"), ("A", "far"), ("N", "done")),
-    "project": (("A", "rest"), ("B", "third")),
+    "swap": (("E", "third"), ("A", "second"), ("E", "far"), ("A", "third")),
+    "norm": (("V", "rest"), ("V", "last"), ("V", "done")),
+    "table": (("N", "rest"), ("N", "last"), ("B", "second"), ("A", "far"), ("N", "done")),
+    "project": (("B", "third"), ("A", "rest")),
     "image 0": (("A", "last"), ("E", "sent")),
     "image 1": (("B", "far"),),
     "image 2": (("B", "rest"),),

time: 186 us -> 186 us (level)
  no operation moved by 1% of the time
where the time goes in v8:
time: 186 us
  Pallas kernels  185 us (99%)
    pallas_call x1, Pallas kernels, forward(): pl.pallas_call(forward_kernel, out_shape=[jax.ShapeDtypeStruct((count, wi...  97 us
    pallas_call x1, Pallas kernels, backward(): pl.pallas_call(backward_kernel, out_shape=[jax.ShapeDtypeStruct((3, 64, 1...  85.1 us

profile of v8, /device:TPU:0, one launch (start us, length us, event | category | flops | bytes accessed | tf_op | source)
XLA Modules:
  0.0 185.5 jit_solution(14375060542028759652)
XLA Ops:
  0.7 97.0 %forward.1 = (f32[240,1024]{1,0:T(8,128)}, f32[8,1024]{1,0:T(8,128)}, f32[8,1024]{1,0:T(8,128)}, bf16[3,80,1024]{2,1,0:T(8,128)(2,1)}, bf16[8,3,80,128]{3,2,1,0:...) custom-call(bf16[3,72,1024]{2,1,0:T(8,128)(2,1)} %bitcast.29, ...), custom_call_target="tpu_custom_call" | custom-call | tf_op jit(solution)/shard_map/forward/pallas_call | solution.py:844
  97.7 85.1 %backward.1 = (f32[3,64,128]{2,1,0:T(8,128)}, f32[64,128]{1,0:T(8,128)}, f32[64,512]{1,0:T(8,128)}, f32[64,512]{1,0:T(8,128)}, f32[16,1024]{1,0:T(8,128)}, /*index=5*/bf16[3,80,1024]{2,1,0:T(8,128)(2,1)}) custom-call(bf16[8,3,80,128]{3,2,1,0:T(8,128)(2,1)} %get-tuple-element.46.refs_0_, bf16[8,3,80,384]{3,2,1,0:T(8,128)(2,1)} %get-tuple-element.47.refs_1_, ...), custom_call_target="tpu_custom_call" | custom-call | tf_op jit(solution)/shard_map/backward/pallas_call | solution.py:1234
  182.8 2.6 %finish.1 = (bf16[3,72,1024]{2,1,0:T(8,128)(2,1)}, bf16[3,72,1024]{2,1,0:T(8,128)(2,1)}, f32[3,64,128]{2,1,0:T(8,128)}, f32[64,128]{1,0:T(8,128)}, f32[64,512]{1...) custom-call(bf16[3,80,1024]{2,1,0:T(8,128)(2,1)} %get-tuple-element., ...), custom_call_target="tpu_custom_call" | custom-call | tf_op jit(solution)/shard_map/finish/pallas_call | solution.py:1337
